TPU v7x, 32 devices: a whole 2x2x4 slice. The times are simulated.
32 devices in a mesh: groups: 2 (over y), latent: 4 (over z), dp: 2 (over x), mp: 2 (over core).
Axes of the slice: x: 2, y: 2, z: 4, core: 2. Of those that a mesh axis runs over, the one named last changes fastest.
Arguments:
- tokens: bfloat16 [768, 8192], P(('groups', 'latent'), ('dp', 'mp')), parts along dimension 0, may hold values from -6 to 6
- active_latent_index: int32 [768, 64], P(('groups', 'latent')), parts along dimension 0, may hold values from 0 to 8191, as said below
- latent_values: bfloat16 [768, 64], P(('groups', 'latent')), parts along dimension 0, may hold values from 0.19921875 to 2
- dec_bias: float32 [16384], P(('groups', 'dp', 'mp')), parts along dimension 0, may hold values from -3 to 3
- dec_weight: bfloat16 [16384, 8192], P(('groups', 'latent'), ('dp', 'mp')), parts along dimension 0, may hold values from -0.75 to 0.75
Outputs:
- token_error: bfloat16 [768, 8192], P(('groups', 'latent'), ('dp', 'mp')), parts along dimension 0
- dec_grad: bfloat16 [16384, 8192], P(('groups', 'latent'), ('dp', 'mp')), parts along dimension 0
There are 2 independent parts, one for each index of `groups`. A program takes and returns all parts, laid end to end along the dimension named above; each array names one. Nothing has to cross between parts.
Inputs may be any that keep to these rules, and one draw needn't show every extreme that they name: `active_latent_index`: each row names 64 different latents; where 384 * 64 >= 8192, every latent is named by some row.
All inputs are finite; a program needn't handle non-finite values.
Results may differ from a plain program's by a relative error of at most 0.0041.
Values may be sent and summed in bfloat16 or wider, within the bound.
No kernel may reach another device: no remote copies, remote signals or barrier semaphores. Data moves between devices by JAX's collectives and lax.ppermute only.
A program may use at most 64 MiB of HBM per device.

v0:
```python
import math

import jax
import jax.numpy as jnp
from jax import lax
from jax.sharding import PartitionSpec as P


def select_table(all_ids, all_values, first_latent, shard_width):
    row_count = all_ids.shape[0]
    active = all_ids.shape[1]
    block_rows = math.gcd(row_count, 64)
    numbers = first_latent + jnp.arange(shard_width, dtype=jnp.int32)
    id_blocks = all_ids.reshape(row_count // block_rows, block_rows, active)
    value_blocks = all_values.reshape(row_count // block_rows, block_rows, active)

    def one_block(inputs):
        block_latent_index, block_latent_value = inputs
        hits = block_latent_index[:, :, None] == numbers[None, None, :]
        placed = jnp.where(hits, block_latent_value[:, :, None], jnp.zeros((), jnp.bfloat16))
        return jnp.sum(placed, axis=1, dtype=jnp.float32).astype(jnp.bfloat16)

    table_blocks = lax.map(one_block, (id_blocks, value_blocks))
    return table_blocks.reshape(row_count, shard_width)


def local(tokens, active_latent_index, latent_values, dec_bias, dec_weight):
    shard_width = dec_weight.shape[0]
    own_rows = tokens.shape[0]
    all_ids = lax.all_gather(active_latent_index, "latent", axis=0, tiled=True)
    all_values = lax.all_gather(latent_values, "latent", axis=0, tiled=True)
    first_latent = lax.axis_index("latent") * shard_width
    onehot_table = select_table(all_ids, all_values, first_latent, shard_width)
    contracted_rows = (((0,), (0,)), ((), ()))
    all_tokens = lax.all_gather(tokens, "latent", axis=0, tiled=True)
    partial_value = jnp.dot(onehot_table, dec_weight, preferred_element_type=jnp.float32)
    summed = lax.psum(partial_value, "latent")
    all_errors = (summed + dec_bias - all_tokens.astype(jnp.float32)).astype(jnp.bfloat16)
    token_error = lax.dynamic_slice_in_dim(
        all_errors, lax.axis_index("latent") * own_rows, own_rows, 0
    )
    grad_sum = lax.dot_general(
        onehot_table, all_errors, contracted_rows, preferred_element_type=jnp.float32
    )
    return (token_error, grad_sum.astype(jnp.bfloat16))


def solution(mesh):
    in_specs = (
        P(("groups", "latent"), ("dp", "mp")),
        P(("groups", "latent"), None),
        P(("groups", "latent"), None),
        P(("groups", "dp", "mp")),
        P(("groups", "latent"), ("dp", "mp")),
    )
    out_specs = (P(("groups", "latent"), ("dp", "mp")), P(("groups", "latent"), ("dp", "mp")))
    return jax.shard_map(local, mesh=mesh, in_specs=in_specs, out_specs=out_specs, check_vma=False)
```

profile of v0, /device:TPU:0, one launch (start us, length us, event | category | flops | bytes accessed | tf_op | source)
XLA Modules:
  0.0 216.0 jit_solution(7255486620436528294)
XLA Ops:
  7.2 0.0 all-gather.4.cloned.1.call-start
  7.2 0.7 all-gather.4.cloned.1.call-update
  7.9 0.0 all-reduce.2.cloned.1.call-start
  8.0 15.1 %all-gather.1 = bf16[4,96,64]{1,2,0:T(8,128)(2,1)S(1)} all-gather(bf16[1,96,64]{1,2,0:T(8,128)(2,1)} %bitcast.24), channel_id=1, replica_groups=mesh['groups'=2,'latent'=4,'dp'=2,'mp'=2] {'latent'}, dimensions={0}, use_global_device_ids=true | all-gather | bytes 61440 | tf_op jit(solution)/shard_map/all_gather | solution.py:31
  23.1 0.1 copy.12
  23.2 14.7 %all-gather = s32[4,96,64]{1,2,0:T(8,128)S(1)} all-gather(s32[1,96,64]{1,2,0:T(8,128)} %bitcast.23), channel_id=1, replica_groups=mesh['groups'=2,'latent'=4,'dp'=2,'mp'=2] {'latent'}, dimensions={0}, use_global_device_ids=true | all-gather | bytes 122880 | tf_op jit(solution)/shard_map/all_gather | solution.py:30
  37.9 0.1 copy.11
  38.0 29.9 %while.13 = (s32[]{:T(128)}, bf16[6,64,2048]{2,1,0:T(8,128)(2,1)S(1)}, s32[6,64,64]{2,1,0:T(8,128)S(1)}, bf16[6,64,64]{2,1,0:T(8,128)(2,1)S(1)}, s32[]{:T(128)}, /*index=5*/s32[]{:T(128)}) while((s32[]{:T(128)}, bf16[6,64,2048]{2,1,0:T(8,128)(2,1)S(1)}, s32[6,64,64]{2,1,0:T(8,128)S(1)}, bf16[6,64,64]{2,1,0:T(8,128)(2,1)S(1)}, ...), condition=%wide.region_2.3_spmd.clone, body=%wide.region_0.2_spmd.clone.sunk | while | flops 25036800 | bytes 876637 | solution.py:23
  38.1 4.9 %fusion.9 = bf16[64,2048]{1,0:T(8,128)(2,1)S(1)} fusion(s32[2048]{0:T(1024)S(1)} %iota_add_fusion.2, s32[64,64]{1,0:T(8,128)S(1)} %dynamic-slice_bitcast_fusion.4, bf16[64,64]{1,0:T(8,128)(2,1)S(1)} %dynamic-slice_bitcast_fusion.5), kind=kLoop, calls=%fused_computation.2.clone.1 | loop fusion | flops 25034752 | bytes 294912 | tf_op jit(solution)/shard_map/while/body/eval_jaxpr/reduce_sum | solution.py:21
  43.1 4.9 %fusion.9 = bf16[64,2048]{1,0:T(8,128)(2,1)S(1)} fusion(s32[2048]{0:T(1024)S(1)} %iota_add_fusion.2, s32[64,64]{1,0:T(8,128)S(1)} %dynamic-slice_bitcast_fusion.4, bf16[64,64]{1,0:T(8,128)(2,1)S(1)} %dynamic-slice_bitcast_fusion.5), kind=kLoop, calls=%fused_computation.2.clone.1 | loop fusion | flops 25034752 | bytes 294912 | tf_op jit(solution)/shard_map/while/body/eval_jaxpr/reduce_sum | solution.py:21
  48.1 4.9 %fusion.9 = bf16[64,2048]{1,0:T(8,128)(2,1)S(1)} fusion(s32[2048]{0:T(1024)S(1)} %iota_add_fusion.2, s32[64,64]{1,0:T(8,128)S(1)} %dynamic-slice_bitcast_fusion.4, bf16[64,64]{1,0:T(8,128)(2,1)S(1)} %dynamic-slice_bitcast_fusion.5), kind=kLoop, calls=%fused_computation.2.clone.1 | loop fusion | flops 25034752 | bytes 294912 | tf_op jit(solution)/shard_map/while/body/eval_jaxpr/reduce_sum | solution.py:21
  53.0 4.9 %fusion.9 = bf16[64,2048]{1,0:T(8,128)(2,1)S(1)} fusion(s32[2048]{0:T(1024)S(1)} %iota_add_fusion.2, s32[64,64]{1,0:T(8,128)S(1)} %dynamic-slice_bitcast_fusion.4, bf16[64,64]{1,0:T(8,128)(2,1)S(1)} %dynamic-slice_bitcast_fusion.5), kind=kLoop, calls=%fused_computation.2.clone.1 | loop fusion | flops 25034752 | bytes 294912 | tf_op jit(solution)/shard_map/while/body/eval_jaxpr/reduce_sum | solution.py:21
  58.0 4.9 %fusion.9 = bf16[64,2048]{1,0:T(8,128)(2,1)S(1)} fusion(s32[2048]{0:T(1024)S(1)} %iota_add_fusion.2, s32[64,64]{1,0:T(8,128)S(1)} %dynamic-slice_bitcast_fusion.4, bf16[64,64]{1,0:T(8,128)(2,1)S(1)} %dynamic-slice_bitcast_fusion.5), kind=kLoop, calls=%fused_computation.2.clone.1 | loop fusion | flops 25034752 | bytes 294912 | tf_op jit(solution)/shard_map/while/body/eval_jaxpr/reduce_sum | solution.py:21
  63.0 4.9 %fusion.9 = bf16[64,2048]{1,0:T(8,128)(2,1)S(1)} fusion(s32[2048]{0:T(1024)S(1)} %iota_add_fusion.2, s32[64,64]{1,0:T(8,128)S(1)} %dynamic-slice_bitcast_fusion.4, bf16[64,64]{1,0:T(8,128)(2,1)S(1)} %dynamic-slice_bitcast_fusion.5), kind=kLoop, calls=%fused_computation.2.clone.1 | loop fusion | flops 25034752 | bytes 294912 | tf_op jit(solution)/shard_map/while/body/eval_jaxpr/reduce_sum | solution.py:21
  67.9 8.5 %fusion.3 = f32[384,2048]{1,0:T(8,128)} fusion(bf16[384,2048]{1,0:T(8,128)(2,1)S(1)} %bitcast.25, bf16[2048,2048]{1,0:T(8,128)(2,1)} %param.11), kind=kOutput, calls=%fused_computation.10 | convolution fusion | flops 3221225472 | bytes 13107200 | tf_op jit(solution)/shard_map/dot_general | solution.py:36
  76.4 0.0 copy-start
  76.4 0.0 all-reduce.2.cloned.1.call-update
  76.4 0.0 all-gather.4.cloned.1.call-done
  76.5 122.2 %all-reduce.2.cloned.1.call-done = f32[384,2048]{1,0:T(8,128)} async-done(((f32[384,2048]{1,0:T(8,128)}), f32[384,2048]{1,0:T(8,128)}) %all-reduce.2.cloned.1.call-update) | async-done | bytes 3145744 | tf_op jit(solution)/shard_map/psum | solution.py:37
  198.7 0.0 copy-done
  198.7 2.9 %subtract_convert_fusion = bf16[384,2048]{1,0:T(8,128)(2,1)S(1)} fusion(bf16[384,2048]{1,0:T(8,128)(2,1)} %all-gather.4.cloned.1.call-done, f32[384,2048]{1,0:T(8,128)} %all-reduce.2.cloned.1.call-done, f32[2048]{0:T(1024)S(1)} %copy-done), kind=kLoop, calls=%fused_computation.8 | loop fusion | flops 3145728 | bytes 6299648 | tf_op jit(solution)/shard_map/convert_element_type | solution.py:38
  201.6 6.8 %convolution_convert_fusion = bf16[2048,2048]{1,0:T(8,128)(2,1)} fusion(bf16[384,2048]{1,0:T(8,128)(2,1)S(1)} %bitcast.26, bf16[384,2048]{1,0:T(8,128)(2,1)S(1)} %subtract_convert_fusion), kind=kOutput, calls=%fused_computation.7 | convolution fusion | flops 3225419776 | bytes 11534336 | tf_op jit(solution)/shard_map/dot_general | solution.py:42
  208.4 0.8 constant_dynamic-slice_fusion
  (25 shorter events, 0.3 us)
Async XLA Ops:
  7.2 69.3 %all-gather.4.cloned.1.call-start = ((), (), s32[]{:S(2)}) async-start(), calls=%async_computation.1 | async-start | bytes 1966080 | tf_op jit(solution)/shard_map/all_gather | solution.py:35
  7.9 190.8 %all-reduce.2.cloned.1.call-start = ((), (), s32[]{:S(2)}) async-start(), calls=%async_computation | async-start | bytes 6291456 | tf_op jit(solution)/shard_map/psum | solution.py:37
  76.4 122.3 %copy-start = (f32[2048]{0:T(1024)S(1)}, f32[2048]{0:T(1024)}, u32[]{:S(2)}) copy-start(f32[2048]{0:T(1024)} %param.10) | copy-start | bytes 24580
Sparse Core Ops, SparseCore 0:
  9.6 41.8 all-gather.3
  76.5 122.0 all-reduce.1
where the time goes:
time: 216 us
  waiting for transfers between devices  123 us (57%)
  other arithmetic  32.2 us (15%)
  blocking collectives  29.8 us (14%)
  matrix products  15.3 us (7%)
  between operations  14.1 us (7%)
    psum x1, waiting for transfers between devices, local(): summed = lax.psum(partial_value, 'latent')  122 us
    reduce_sum x6, other arithmetic, one_block(): return jnp.sum(placed, axis=1, dtype=jnp.float32).astype(jnp.bfloat16)  29.3 us
    all_gather x1, blocking collectives, local(): all_values = lax.all_gather(latent_values, 'latent', axis=0, tiled=True)  15.1 us
    all_gather x1, blocking collectives, local(): all_ids = lax.all_gather(active_latent_index, 'latent', axis=0, tiled=True)  14.7 us
    dot_general x1, matrix products, local(): jnp.dot(onehot_table, dec_weight, preferred_element_type=jnp.float32)  8.46 us
    dot_general x1, matrix products, local(): lax.dot_general(onehot_table, all_errors, contracted_rows, preferred_elem...  6.79 us
  transfers between devices with their start and end apart: 2, of which 1 were waited for; matrix products, arithmetic and copies ran while one was open for 18% of the time, Pallas kernels for 0%

commit v1 on v0

v1 whole, which is shorter than its diff:
```python
import functools

import jax
import jax.numpy as jnp
from jax import lax
from jax.experimental import pallas as pl
from jax.experimental.pallas import tpu as pltpu
from jax.sharding import PartitionSpec as P

LANES = 128
GROUP = 8
CHAINS = 2
VMEM_LIMIT = 48 * 1024 * 1024


def params(grid_dims=1):
    return pltpu.CompilerParams(
        vmem_limit_bytes=VMEM_LIMIT, dimension_semantics=("arbitrary",) * grid_dims
    )


def ring_order(count):
    return [0] + list(range(1, count, 2)) + list(range(count - 2 + count % 2, 0, -2))


def ring_shift(count, step):
    order = ring_order(count)
    return [(order[i], order[(i + step) % count]) for i in range(count)]


def pack_kernel(ids_ref, values_ref, out_ref, wide_ref):
    rows, active = ids_ref.shape
    half = rows // 2
    wide_ref[0:rows, :] = ids_ref[...].astype(jnp.float32)
    wide_ref[rows:, :] = values_ref[...].astype(jnp.float32)
    even = wide_ref[pl.ds(0, 2 * half, stride=2), :]
    odd = wide_ref[pl.ds(1, 2 * half, stride=2), :]
    out_ref[...] = jnp.concatenate([even, odd], axis=1)


def pack(ids, values):
    rows, active = ids.shape
    return pl.pallas_call(
        pack_kernel,
        out_shape=jax.ShapeDtypeStruct((rows, 2 * active), jnp.float32),
        scratch_shapes=[pltpu.VMEM((2 * rows, active), jnp.float32)],
        compiler_params=params(0),
        name="pack",
    )(ids, values)


def build_table(first, packed_ref, table_ref, row0, keys_ref, width):
    rows = packed_ref.shape[0]
    half = rows // 2
    per_row = 2
    rows_per_group = GROUP // per_row
    high_count = width // LANES
    ids = packed_ref[0:half, :].astype(jnp.int32) - first
    high = lax.shift_right_arithmetic(ids, 7)
    low = jnp.bitwise_and(ids, LANES - 1)
    row = lax.broadcasted_iota(jnp.int32, ids.shape, 0)
    lane = lax.broadcasted_iota(jnp.int32, ids.shape, 1)
    place = per_row * jnp.bitwise_and(row, rows_per_group - 1) + jnp.where(lane >= LANES // 2, 1, 0)
    inside = jnp.logical_and(ids >= 0, ids < width)
    key = jnp.where(inside, high * GROUP + place, -1)
    keys_ref[0:half, :] = key.astype(jnp.float32)
    keys_ref[half : 2 * half, :] = low.astype(jnp.float32)
    tall = lax.broadcasted_iota(jnp.int32, (high_count * GROUP, LANES), 0).astype(jnp.float32).astype(jnp.bfloat16)
    wide = lax.broadcasted_iota(jnp.int32, (LANES, LANES), 0).astype(jnp.float32).astype(jnp.bfloat16)
    zero, one = jnp.zeros((), jnp.bfloat16), jnp.ones((), jnp.bfloat16)

    def group_rows(r0):
        left, right = [], []
        for j in range(rows_per_group):
            key = keys_ref[pl.ds(r0 + j, 1), :].astype(jnp.bfloat16)
            low = keys_ref[pl.ds(half + r0 + j, 1), :].astype(jnp.bfloat16)
            value = packed_ref[pl.ds(half + r0 + j, 1), :].astype(jnp.bfloat16)
            left.append(jnp.where(tall == key, value, zero))
            right.append(jnp.where(wide == low, one, zero))
        left = jnp.concatenate(left, axis=1)
        right = jnp.concatenate(right, axis=1)
        product = lax.dot_general(left, right, (((1,), (1,)), ((), ())), preferred_element_type=jnp.float32)
        pieces = [product[h * GROUP : (h + 1) * GROUP, :] for h in range(high_count)]
        return jnp.concatenate(pieces, axis=1)

    @pl.loop(0, rows // (2 * GROUP))
    def _(i):
        r0 = i * (2 * rows_per_group)
        both = jnp.concatenate([group_rows(r0), group_rows(r0 + rows_per_group)], axis=0)
        table_ref[pl.ds(pl.multiple_of(row0 + i * 2 * GROUP, 2 * GROUP), 2 * GROUP), :] = both.astype(jnp.bfloat16)


def partial_kernel(blocks, build, wire, first_ref, *refs):
    if build:
        packed, (weight_ref, table_ref), refs = refs[:blocks], refs[blocks : blocks + 2], refs[blocks + 2 :]
        outs, keys_ref = refs[:blocks], refs[blocks]
        rows = packed[0].shape[0]

        @pl.when(pl.program_id(0) == 0)
        def _():
            for b in range(blocks):
                build_table(first_ref[0], packed[b], table_ref, b * rows, keys_ref, weight_ref.shape[0])
    else:
        (table_ref, weight_ref), outs = refs[:2], refs[2:]
        rows = table_ref.shape[0] // blocks
    product = jnp.dot(table_ref[...], weight_ref[...], preferred_element_type=jnp.float32)
    for b in range(blocks):
        outs[b][...] = product[b * rows : (b + 1) * rows, :].astype(outs[b].dtype)


def partial_sums(first, packed, table, weight, chain, chains, wire, tile=256):
    build = table is None
    width, features = weight.shape
    columns = features // chains
    blocks = len(packed)
    rows = packed[0].shape[0]
    tile = min(tile, columns)
    base = chain * (columns // tile)
    whole = lambda shape: pl.BlockSpec(shape, lambda i, f: (0, 0))
    weight_spec = pl.BlockSpec((width, tile), lambda i, f: (0, base + i))
    table_shape = jax.ShapeDtypeStruct((blocks * rows, width), jnp.bfloat16)
    out_shapes = [
        jax.ShapeDtypeStruct((rows, columns), jnp.bfloat16 if b < wire else jnp.float32) for b in range(blocks)
    ]
    out_specs = [pl.BlockSpec((rows, tile), lambda i, f: (0, i)) for b in range(blocks)]
    if build:
        in_specs = [whole(p.shape) for p in packed] + [weight_spec]
        operands = (*packed, weight)
        out_shapes = [table_shape] + out_shapes
        out_specs = [whole(table_shape.shape)] + out_specs
        scratch = [pltpu.VMEM(packed[0].shape, jnp.float32)]
    else:
        in_specs = [whole(table_shape.shape), weight_spec]
        operands = (table, weight)
        scratch = []
    flops = 2 * blocks * rows * width * columns
    result = pl.pallas_call(
        functools.partial(partial_kernel, blocks, build, wire),
        grid_spec=pltpu.PrefetchScalarGridSpec(
            num_scalar_prefetch=1,
            grid=(columns // tile,),
            in_specs=in_specs,
            out_specs=out_specs,
            scratch_shapes=scratch,
        ),
        out_shape=out_shapes,
        compiler_params=params(),
        cost_estimate=pl.CostEstimate(flops=flops, bytes_accessed=2 * width * columns, transcendentals=0),
        name="partial_build" if build else "partial",
    )(first, *operands)
    if build:
        return result[0], list(result[1:])
    return table, list(result)


def grad_kernel(blocks, table_ref, *refs):
    errors, out_ref, all_ref = refs[:blocks], refs[-2], refs[-1]
    rows = errors[0].shape[0]

    @pl.when(pl.program_id(0) == 0)
    def _():
        for b in range(blocks):
            all_ref[b * rows : (b + 1) * rows, :] = errors[b][...]

    out_ref[...] = jnp.dot(table_ref[...], all_ref[...], preferred_element_type=jnp.float32).astype(out_ref.dtype)


def grad_part(table_t, errors, features, chain, previous, tile=512):
    width, tokens = table_t.shape
    rows, columns = errors[0].shape
    blocks = len(errors)
    in_specs = [pl.BlockSpec((tile, tokens), lambda i: (i, 0))] + [
        pl.BlockSpec((rows, columns), lambda i: (0, 0)) for _ in errors
    ]
    operands = [table_t, *errors]
    aliases = {}
    if previous is not None:
        in_specs.append(pl.BlockSpec(memory_space=pl.ANY))
        operands.append(previous)
        aliases = {len(operands) - 1: 0}
    return pl.pallas_call(
        functools.partial(grad_kernel, blocks),
        grid=(width // tile,),
        in_specs=in_specs,
        out_specs=pl.BlockSpec((tile, columns), lambda i: (i, chain)),
        out_shape=jax.ShapeDtypeStruct((width, features), jnp.bfloat16),
        scratch_shapes=[pltpu.VMEM((tokens, columns), jnp.bfloat16)],
        input_output_aliases=aliases,
        compiler_params=params(),
        cost_estimate=pl.CostEstimate(
            flops=2 * width * tokens * columns, bytes_accessed=2 * width * columns, transcendentals=0
        ),
        name="grad",
    )(*operands)


def local(count, tokens, active_latent_index, latent_values, dec_bias, dec_weight):
    width, features = dec_weight.shape
    columns = features // CHAINS
    first = (lax.axis_index("latent") * width).astype(jnp.int32).reshape(1)

    def send(x, step=1):
        return lax.ppermute(x, "latent", ring_shift(count, step))

    own = pack(active_latent_index, latent_values)
    others = [send(own, k) for k in range(1, count)]
    own_table, own_first = partial_sums(first, [own], None, dec_weight, 0, 1, 0)
    own_sum = own_first[0]
    other_table, sums = None, []
    for c in range(CHAINS):
        other_table, parts = partial_sums(first, others, other_table, dec_weight, c, CHAINS, 1)
        sums.append(parts)
    running = [sums[c][0] for c in range(CHAINS)]
    for step in range(1, count):
        for c in range(CHAINS):
            running[c] = send(running[c])
            if step < count - 1:
                running[c] = (running[c].astype(jnp.float32) + sums[c][step]).astype(jnp.bfloat16)
    errors = []
    for c in range(CHAINS):
        at = slice(c * columns, (c + 1) * columns)
        total = running[c].astype(jnp.float32) + own_sum[:, at] + dec_bias[at] - tokens[:, at].astype(jnp.float32)
        errors.append([total.astype(jnp.bfloat16)])
    for step in range(1, count):
        for c in range(CHAINS):
            errors[c].append(send(errors[c][-1]))
    table_t = jnp.concatenate([own_table, other_table], axis=0).T
    grad = None
    for c in range(CHAINS):
        grad = grad_part(table_t, errors[c], features, c, grad)
    token_error = jnp.concatenate([errors[c][0] for c in range(CHAINS)], axis=1)
    return token_error, grad


def solution(mesh):
    in_specs = (
        P(("groups", "latent"), ("dp", "mp")),
        P(("groups", "latent"), None),
        P(("groups", "latent"), None),
        P(("groups", "dp", "mp")),
        P(("groups", "latent"), ("dp", "mp")),
    )
    out_specs = (P(("groups", "latent"), ("dp", "mp")), P(("groups", "latent"), ("dp", "mp")))
    body = functools.partial(local, mesh.shape["latent"])
    return jax.shard_map(body, mesh=mesh, in_specs=in_specs, out_specs=out_specs, check_vma=False)
```

time: 216 us -> 91.9 us (0.43)
  waiting for transfers between devices: 123 us -> 37.6 us
  blocking collectives: 29.8 us -> 0 us
  Pallas kernels: 0 us -> 28.9 us
  other arithmetic: 32.2 us -> 3.44 us
  starting transfers between devices: 0.08 us -> 17.2 us
  matrix products: 15.3 us -> 0 us
  between operations: 14.1 us -> 0.74 us
  local copies, waits for them, and re-layouts: 1.28 us -> 3.49 us
    psum x1 -> x0, waiting for transfers between devices: 122 us -> none  [local(): summed = lax.psum(partial_value, 'latent')]
    ppermute x0 -> x15, waiting for transfers between devices: none -> 37.6 us  [send(): return lax.ppermute(x, 'latent', ring_shift(count, step))]
    all_gather x2 -> x0, blocking collectives: 29.8 us -> none  [the longest x1 15.1 us: local(): all_values = lax.all_gather(latent_values, 'latent', axis=0, tiled=True)]
    reduce_sum x6 -> x0, other arithmetic: 29.3 us -> none  [one_block(): return jnp.sum(placed, axis=1, dtype=jnp.float32).astype(jnp.bfloat16)]
    pallas_call x0 -> x6, Pallas kernels: none -> 28.9 us  [the longest x3 20.6 us: partial_sums(): pl.pallas_call(functools.partial(partial_kernel, blocks, build, wire), gr...]
    ppermute x0 -> x15, starting transfers between devices: none -> 17.2 us  [send(): return lax.ppermute(x, 'latent', ring_shift(count, step))]
    dot_general x2 -> x0, matrix products: 15.3 us -> none  [the longest x1 8.46 us: local(): jnp.dot(onehot_table, dec_weight, preferred_element_type=jnp.float32)]
    convert_element_type x1 -> x5, other arithmetic: 2.89 us -> 0.33 us  [the longest x1 0.17 us: local(): errors.append([total.astype(jnp.bfloat16)])]
  transfers between devices with their start and end apart: 2 -> 15, of which waited for: 1 -> 12; matrix products, arithmetic and copies ran while one was open for 18% -> 6% of each run, Pallas kernels for 0% -> 13%
where the time goes in v1:
time: 91.9 us; the launch traced here: 91.4 us
  waiting for transfers between devices  37.6 us (41%)
  Pallas kernels  28.9 us (31%)
  starting transfers between devices  17.2 us (19%)
  local copies, waits for them, and re-layouts  3.49 us (4%)
  other arithmetic  3.44 us (4%)
    ppermute x15, waiting for transfers between devices, send(): return lax.ppermute(x, 'latent', ring_shift(count, step))  37.6 us
    pallas_call x3, Pallas kernels, partial_sums(): pl.pallas_call(functools.partial(partial_kernel, blocks, build, wire), gr...  20.6 us
    ppermute x15, starting transfers between devices, send(): return lax.ppermute(x, 'latent', ring_shift(count, step))  17.2 us
    pallas_call x2, Pallas kernels, grad_part(): pl.pallas_call(functools.partial(grad_kernel, blocks), grid=(width // til...  8.27 us
    transpose x1, other arithmetic, local(): table_t = jnp.concatenate([own_table, other_table], axis=0).T  2.34 us
  transfers between devices with their start and end apart: 15, of which 12 were waited for; matrix products, arithmetic and copies ran while one was open for 6% of the time, Pallas kernels for 13%

profile of v1, /device:TPU:0, one launch (start us, length us, event | category | flops | bytes accessed | tf_op | source)
XLA Modules:
  0.0 91.4 jit_solution(8497205427313949020)
XLA Ops:
  0.6 0.8 copy.8.ids_ref
  1.5 0.8 copy.9.values_ref
  2.3 0.1 pack.1.refs_0_
  2.4 3.1 %collective-permute-start = (f32[96,128]{1,0:T(8,128)S(1)}, f32[96,128]{1,0:T(8,128)S(1)}, u32[]{:S(2)}, u32[]{:S(2)}) collective-permute-start(f32[96,128]{1,0:T(8,128)S(1)} %pack.1.refs_0_), channel_id=1, source_target_pairs={{0,4},{4,12},{12,8},{8,0},{1,5},{5,13},{13,9},{9,1},{2,6},{6,14},{... | collective-permute-start | bytes 147464 | tf_op jit(solution)/shard_map/ppermute | solution.py:203
  5.5 2.5 %collective-permute-start.1 = (f32[96,128]{1,0:T(8,128)S(1)}, f32[96,128]{1,0:T(8,128)S(1)}, u32[]{:S(2)}, u32[]{:S(2)}) collective-permute-start(f32[96,128]{1,0:T(8,128)S(1)} %pack.1.refs_0_), channel_id=1, source_target_pairs={{0,12},{4,8},{12,0},{8,4},{1,13},{5,9},{13,1},{9,5},{2,14},{6,10},... | collective-permute-start | bytes 147464 | tf_op jit(solution)/shard_map/ppermute | solution.py:203
  7.9 1.6 %collective-permute-start.2 = (f32[96,128]{1,0:T(8,128)S(1)}, f32[96,128]{1,0:T(8,128)S(1)}, u32[]{:S(2)}, u32[]{:S(2)}) collective-permute-start(f32[96,128]{1,0:T(8,128)S(1)} %pack.1.refs_0_), channel_id=1, source_target_pairs={{0,8},{4,0},{12,4},{8,12},{1,9},{5,1},{13,5},{9,13},{2,10},{6,2},{... | collective-permute-start | bytes 147464 | tf_op jit(solution)/shard_map/ppermute | solution.py:203
  9.5 0.0 collective-permute-done.refs_0_
  9.5 2.1 %collective-permute-done.1.refs_1_ = f32[96,128]{1,0:T(8,128)S(1)} collective-permute-done((f32[96,128]{1,0:T(8,128)S(1)}, f32[96,128]{1,0:T(8,128)S(1)}, u32[]{:S(2)}, u32[]{:S(2)}) %collective-permute-start.1) | collective-permute-done | bytes 49184 | tf_op jit(solution)/shard_map/ppermute | solution.py:203
  11.7 0.5 collective-permute-done.2.refs_2_
  12.2 8.3 %partial_build.2 = (bf16[288,2048]{1,0:T(8,128)(2,1)S(1)}, bf16[96,1024]{1,0:T(8,128)(2,1)S(1)}, f32[96,1024]{1,0:T(8,128)S(1)}, f32[96,1024]{1,0:T(8,128)S(1)}) custom-call(s32[1]{0:T(128)} %bitcast.first_ref, f32[96,128]{1,0:T(8,128)S(1)} %collective-permute-done.refs_0_, f32[96,128]{1,0:T(8,128)S(1)} %collective-permute-done.1.refs_1_, ...), custom_call_target="tpu_custom_call" | custom-call | flops 1207959552 | bytes 4194304 | tf_op jit(solution)/shard_map/partial_build/pallas_call | solution.py:137
  20.5 4.1 %partial.1 = (bf16[96,1024]{1,0:T(8,128)(2,1)S(1)}, f32[96,1024]{1,0:T(8,128)S(1)}, f32[96,1024]{1,0:T(8,128)S(1)}) custom-call(s32[1]{0:T(128)} %bitcast.first_ref, bf16[288,2048]{1,0:T(8,128)(2,1)S(1)} %get-tuple-element.15.refs_0_, bf16[2048,2048]{1,0:T(8,128)(2,1)} %refs_1_.3), custom_call_target="tpu_custom_call" | custom-call | flops 1207959552 | bytes 4194304 | tf_op jit(solution)/shard_map/partial/pallas_call | solution.py:137
  24.6 1.1 %collective-permute-start.6 = (bf16[96,1024]{1,0:T(8,128)(2,1)S(1)}, bf16[96,1024]{1,0:T(8,128)(2,1)S(1)}, u32[]{:S(2)}, u32[]{:S(2)}) collective-permute-start(bf16[96,1024]{1,0:T(8,128)(2,1)S(1)} %get-tuple-element.16), channel_id=1, source_target_pairs={{0,4},{4,12},{12,8},{8,0},{1,5},{5,13},{13,9},{9,1},{2,6},{6,14},{... | collective-permute-start | bytes 589832 | tf_op jit(solution)/shard_map/ppermute | solution.py:203
  25.7 8.2 %partial_build.3 = (bf16[96,2048]{1,0:T(8,128)(2,1)S(1)}, f32[96,2048]{1,0:T(8,128)S(1)}) custom-call(s32[1]{0:T(128)} %bitcast.first_ref, f32[96,128]{1,0:T(8,128)S(1)} %pack.1.refs_0_, bf16[2048,2048]{1,0:T(8,128)(2,1)} %refs_1_.3), custom_call_target="tpu_custom_call" | custom-call | flops 805306368 | bytes 8388608 | tf_op jit(solution)/shard_map/partial_build/pallas_call | solution.py:137
  33.9 1.7 %collective-permute-start.3 = (bf16[96,1024]{1,0:T(8,128)(2,1)S(1)}, bf16[96,1024]{1,0:T(8,128)(2,1)S(1)}, u32[]{:S(2)}, u32[]{:S(2)}) collective-permute-start(bf16[96,1024]{1,0:T(8,128)(2,1)S(1)} %get-tuple-element.11), channel_id=1, source_target_pairs={{0,4},{4,12},{12,8},{8,0},{1,5},{5,13},{13,9},{9,1},{2,6},{6,14},{... | collective-permute-start | bytes 589832 | tf_op jit(solution)/shard_map/ppermute | solution.py:203
  35.6 0.0 collective-permute-done.6
  35.6 0.0 copy-start.1
  35.6 0.0 copy-start
  35.7 1.7 %collective-permute-start.7 = (bf16[96,1024]{1,0:T(8,128)(2,1)S(1)}, bf16[96,1024]{1,0:T(8,128)(2,1)S(1)}, u32[]{:S(2)}, u32[]{:S(2)}) collective-permute-start(bf16[96,1024]{1,0:T(8,128)(2,1)S(1)} %add_convert_fusion.1), channel_id=1, source_target_pairs={{0,4},{4,12},{12,8},{8,0},{1,5},{5,13},{13,9},{9,1},{2,6},{6,14},{... | collective-permute-start | bytes 589832 | tf_op jit(solution)/shard_map/ppermute | solution.py:203
  37.3 5.3 %collective-permute-done.3 = bf16[96,1024]{1,0:T(8,128)(2,1)S(1)} collective-permute-done((bf16[96,1024]{1,0:T(8,128)(2,1)S(1)}, bf16[96,1024]{1,0:T(8,128)(2,1)S(1)}, u32[]{:S(2)}, u32[]{:S(2)}) %collective-permute-start.3) | collective-permute-done | bytes 196640 | tf_op jit(solution)/shard_map/ppermute | solution.py:203
  42.7 0.8 collective-permute-start.4
  43.5 3.4 %collective-permute-done.7 = bf16[96,1024]{1,0:T(8,128)(2,1)S(1)} collective-permute-done((bf16[96,1024]{1,0:T(8,128)(2,1)S(1)}, bf16[96,1024]{1,0:T(8,128)(2,1)S(1)}, u32[]{:S(2)}, u32[]{:S(2)}) %collective-permute-start.7) | collective-permute-done | bytes 196640 | tf_op jit(solution)/shard_map/ppermute | solution.py:203
  46.9 0.8 collective-permute-start.8
  47.7 3.8 %collective-permute-done.4 = bf16[96,1024]{1,0:T(8,128)(2,1)S(1)} collective-permute-done((bf16[96,1024]{1,0:T(8,128)(2,1)S(1)}, bf16[96,1024]{1,0:T(8,128)(2,1)S(1)}, u32[]{:S(2)}, u32[]{:S(2)}) %collective-permute-start.4) | collective-permute-done | bytes 196640 | tf_op jit(solution)/shard_map/ppermute | solution.py:203
  51.5 0.4 collective-permute-start.5
  51.9 0.0 copy-done.1
  51.9 2.7 %collective-permute-done.8 = bf16[96,1024]{1,0:T(8,128)(2,1)S(1)} collective-permute-done((bf16[96,1024]{1,0:T(8,128)(2,1)S(1)}, bf16[96,1024]{1,0:T(8,128)(2,1)S(1)}, u32[]{:S(2)}, u32[]{:S(2)}) %collective-permute-start.8) | collective-permute-done | bytes 196640 | tf_op jit(solution)/shard_map/ppermute | solution.py:203
  54.6 4.3 %collective-permute-done.5 = bf16[96,1024]{1,0:T(8,128)(2,1)S(1)} collective-permute-done((bf16[96,1024]{1,0:T(8,128)(2,1)S(1)}, bf16[96,1024]{1,0:T(8,128)(2,1)S(1)}, u32[]{:S(2)}, u32[]{:S(2)}) %collective-permute-start.5) | collective-permute-done | bytes 196640 | tf_op jit(solution)/shard_map/ppermute | solution.py:203
  58.9 0.0 copy-done
  58.9 0.2 subtract_convert_fusion.1
  59.1 0.1 collective-permute-start.12
  59.2 3.0 %collective-permute-start.9 = (bf16[96,1024]{1,0:T(8,128)(2,1)S(1)}, bf16[96,1024]{1,0:T(8,128)(2,1)S(1)}, u32[]{:S(2)}, u32[]{:S(2)}) collective-permute-start(bf16[96,1024]{1,0:T(8,128)(2,1)S(1)} %get-tuple-element.21.refs_0_), channel_id=1, source_target_pairs={{0,4},{4,12},{12,8},{8,0},{1,5},{5,13},{13,9},{9,1},{2,6},{6,14},{... | collective-permute-start | bytes 589832 | tf_op jit(solution)/shard_map/ppermute | solution.py:203
  62.2 0.3 copy.10
  62.4 1.5 %copy.11 = bf16[288,2048]{0,1:T(8,128)(2,1)} copy(bf16[288,2048]{1,0:T(8,128)(2,1)S(1)} %get-tuple-element.15.refs_0_) | data formatting | bytes 2359296 | tf_op jit(solution)/shard_map/partial_build/pallas_call | solution.py:137
  64.0 3.9 %collective-permute-done.12.refs_1_ = bf16[96,1024]{1,0:T(8,128)(2,1)S(1)} collective-permute-done((bf16[96,1024]{1,0:T(8,128)(2,1)S(1)}, bf16[96,1024]{1,0:T(8,128)(2,1)S(1)}, u32[]{:S(2)}, u32[]{:S(2)}) %collective-permute-start.12) | collective-permute-done | bytes 196640 | tf_op jit(solution)/shard_map/ppermute | solution.py:203
  67.9 0.0 collective-permute-start.13
  67.9 4.2 %collective-permute-done.9.refs_1_ = bf16[96,1024]{1,0:T(8,128)(2,1)S(1)} collective-permute-done((bf16[96,1024]{1,0:T(8,128)(2,1)S(1)}, bf16[96,1024]{1,0:T(8,128)(2,1)S(1)}, u32[]{:S(2)}, u32[]{:S(2)}) %collective-permute-start.9) | collective-permute-done | bytes 196640 | tf_op jit(solution)/shard_map/ppermute | solution.py:203
  72.1 0.0 collective-permute-start.10
  72.1 2.3 %maximum_bitcast_fusion.table_ref = bf16[2048,384]{1,0:T(8,128)(2,1)S(1)} fusion(bf16[288,2048]{0,1:T(8,128)(2,1)} %copy.11, bf16[96,2048]{0,1:T(8,128)(2,1)S(1)} %copy.10), kind=kLoop, calls=%fused_computation | loop fusion | flops 3145728 | bytes 3145728 | tf_op jit(solution)/shard_map/transpose | solution.py:227
  74.4 2.2 %collective-permute-done.13.refs_2_ = bf16[96,1024]{1,0:T(8,128)(2,1)S(1)} collective-permute-done((bf16[96,1024]{1,0:T(8,128)(2,1)S(1)}, bf16[96,1024]{1,0:T(8,128)(2,1)S(1)}, u32[]{:S(2)}, u32[]{:S(2)}) %collective-permute-start.13) | collective-permute-done | bytes 196640 | tf_op jit(solution)/shard_map/ppermute | solution.py:203
  76.6 0.6 collective-permute-start.14
  77.2 3.2 %collective-permute-done.10.refs_2_ = bf16[96,1024]{1,0:T(8,128)(2,1)S(1)} collective-permute-done((bf16[96,1024]{1,0:T(8,128)(2,1)S(1)}, bf16[96,1024]{1,0:T(8,128)(2,1)S(1)}, u32[]{:S(2)}, u32[]{:S(2)}) %collective-permute-start.10) | collective-permute-done | bytes 196640 | tf_op jit(solution)/shard_map/ppermute | solution.py:203
  80.4 0.0 collective-permute-start.11
  80.4 0.8 pad_maximum_fusion
  81.2 1.9 %collective-permute-done.14.refs_3_ = bf16[96,1024]{1,0:T(8,128)(2,1)S(1)} collective-permute-done((bf16[96,1024]{1,0:T(8,128)(2,1)S(1)}, bf16[96,1024]{1,0:T(8,128)(2,1)S(1)}, u32[]{:S(2)}, u32[]{:S(2)}) %collective-permute-start.14) | collective-permute-done | bytes 196640 | tf_op jit(solution)/shard_map/ppermute | solution.py:203
  83.2 4.1 %grad.2.refs_4_ = bf16[2048,2048]{1,0:T(8,128)(2,1)} custom-call(bf16[2048,384]{1,0:T(8,128)(2,1)S(1)} %maximum_bitcast_fusion.table_ref, bf16[96,1024]{1,0:T(8,128)(2,1)S(1)} %get-tuple-element.20.refs_0_, bf16[96,1024]{1,0:T(8,128)(2,1)S(1)} %collective-permute-done.12.refs_1_, bf16[96,1024]{1,0:T(8,128)(2,1)S(1)} %collective-permute-done.13.refs_2_, ...), custom_call_target="tpu_custom_call" | custom-call | flops 1610612736 | bytes 4194304 | tf_op jit(solution)/shard_map/grad/pallas_call | solution.py:181
  87.3 0.0 collective-permute-done.11.refs_3_
  87.3 4.1 %grad.3 = bf16[2048,2048]{1,0:T(8,128)(2,1)} custom-call(bf16[2048,384]{1,0:T(8,128)(2,1)S(1)} %maximum_bitcast_fusion.table_ref, bf16[96,1024]{1,0:T(8,128)(2,1)S(1)} %get-tuple-element.21.refs_0_, bf16[96,1024]{1,0:T(8,128)(2,1)S(1)} %collective-permute-done.9.refs_1_, ...), custom_call_target="tpu_custom_call", output_to_operand_aliasing={{}: (5, {})} | custom-call | flops 1610612736 | bytes 4194304 | tf_op jit(solution)/shard_map/grad/pallas_call | solution.py:181
  (5 shorter events, 0.2 us)
Async XLA Ops:
  2.4 7.1 %collective-permute-start = (f32[96,128]{1,0:T(8,128)S(1)}, f32[96,128]{1,0:T(8,128)S(1)}, u32[]{:S(2)}, u32[]{:S(2)}) collective-permute-start(f32[96,128]{1,0:T(8,128)S(1)} %pack.1.refs_0_), channel_id=1, source_target_pairs={{0,4},{4,12},{12,8},{8,0},{1,5},{5,13},{13,9},{9,1},{2,6},{6,14},{... | collective-permute-start | bytes 147464 | tf_op jit(solution)/shard_map/ppermute | solution.py:203
  5.5 6.2 %collective-permute-start.1 = (f32[96,128]{1,0:T(8,128)S(1)}, f32[96,128]{1,0:T(8,128)S(1)}, u32[]{:S(2)}, u32[]{:S(2)}) collective-permute-start(f32[96,128]{1,0:T(8,128)S(1)} %pack.1.refs_0_), channel_id=1, source_target_pairs={{0,12},{4,8},{12,0},{8,4},{1,13},{5,9},{13,1},{9,5},{2,14},{6,10},... | collective-permute-start | bytes 147464 | tf_op jit(solution)/shard_map/ppermute | solution.py:203
  7.9 4.2 %collective-permute-start.2 = (f32[96,128]{1,0:T(8,128)S(1)}, f32[96,128]{1,0:T(8,128)S(1)}, u32[]{:S(2)}, u32[]{:S(2)}) collective-permute-start(f32[96,128]{1,0:T(8,128)S(1)} %pack.1.refs_0_), channel_id=1, source_target_pairs={{0,8},{4,0},{12,4},{8,12},{1,9},{5,1},{13,5},{9,13},{2,10},{6,2},{... | collective-permute-start | bytes 147464 | tf_op jit(solution)/shard_map/ppermute | solution.py:203
  24.6 11.0 %collective-permute-start.6 = (bf16[96,1024]{1,0:T(8,128)(2,1)S(1)}, bf16[96,1024]{1,0:T(8,128)(2,1)S(1)}, u32[]{:S(2)}, u32[]{:S(2)}) collective-permute-start(bf16[96,1024]{1,0:T(8,128)(2,1)S(1)} %get-tuple-element.16), channel_id=1, source_target_pairs={{0,4},{4,12},{12,8},{8,0},{1,5},{5,13},{13,9},{9,1},{2,6},{6,14},{... | collective-permute-start | bytes 589832 | tf_op jit(solution)/shard_map/ppermute | solution.py:203
  33.9 8.8 %collective-permute-start.3 = (bf16[96,1024]{1,0:T(8,128)(2,1)S(1)}, bf16[96,1024]{1,0:T(8,128)(2,1)S(1)}, u32[]{:S(2)}, u32[]{:S(2)}) collective-permute-start(bf16[96,1024]{1,0:T(8,128)(2,1)S(1)} %get-tuple-element.11), channel_id=1, source_target_pairs={{0,4},{4,12},{12,8},{8,0},{1,5},{5,13},{13,9},{9,1},{2,6},{6,14},{... | collective-permute-start | bytes 589832 | tf_op jit(solution)/shard_map/ppermute | solution.py:203
  35.6 16.3 %copy-start.1 = (f32[2048]{0:T(1024)S(1)}, f32[2048]{0:T(1024)}, u32[]{:S(2)}) copy-start(f32[2048]{0:T(1024)} %param.8) | copy-start | bytes 24580
  35.6 23.3 %copy-start = (bf16[96,2048]{1,0:T(8,128)(2,1)S(1)}, bf16[96,2048]{1,0:T(8,128)(2,1)}, u32[]{:S(2)}) copy-start(bf16[96,2048]{1,0:T(8,128)(2,1)} %param.5) | copy-start | bytes 1179652
  35.7 11.2 %collective-permute-start.7 = (bf16[96,1024]{1,0:T(8,128)(2,1)S(1)}, bf16[96,1024]{1,0:T(8,128)(2,1)S(1)}, u32[]{:S(2)}, u32[]{:S(2)}) collective-permute-start(bf16[96,1024]{1,0:T(8,128)(2,1)S(1)} %add_convert_fusion.1), channel_id=1, source_target_pairs={{0,4},{4,12},{12,8},{8,0},{1,5},{5,13},{13,9},{9,1},{2,6},{6,14},{... | collective-permute-start | bytes 589832 | tf_op jit(solution)/shard_map/ppermute | solution.py:203
  42.7 8.8 %collective-permute-start.4 = (bf16[96,1024]{1,0:T(8,128)(2,1)S(1)}, bf16[96,1024]{1,0:T(8,128)(2,1)S(1)}, u32[]{:S(2)}, u32[]{:S(2)}) collective-permute-start(bf16[96,1024]{1,0:T(8,128)(2,1)S(1)} %add_convert_fusion.3), channel_id=1, source_target_pairs={{0,4},{4,12},{12,8},{8,0},{1,5},{5,13},{13,9},{9,1},{2,6},{6,14},{... | collective-permute-start | bytes 589832 | tf_op jit(solution)/shard_map/ppermute | solution.py:203
  46.9 7.7 %collective-permute-start.8 = (bf16[96,1024]{1,0:T(8,128)(2,1)S(1)}, bf16[96,1024]{1,0:T(8,128)(2,1)S(1)}, u32[]{:S(2)}, u32[]{:S(2)}) collective-permute-start(bf16[96,1024]{1,0:T(8,128)(2,1)S(1)} %add_convert_fusion), channel_id=1, source_target_pairs={{0,4},{4,12},{12,8},{8,0},{1,5},{5,13},{13,9},{9,1},{2,6},{6,14},{... | collective-permute-start | bytes 589832 | tf_op jit(solution)/shard_map/ppermute | solution.py:203
  51.5 7.4 %collective-permute-start.5 = (bf16[96,1024]{1,0:T(8,128)(2,1)S(1)}, bf16[96,1024]{1,0:T(8,128)(2,1)S(1)}, u32[]{:S(2)}, u32[]{:S(2)}) collective-permute-start(bf16[96,1024]{1,0:T(8,128)(2,1)S(1)} %add_convert_fusion.2), channel_id=1, source_target_pairs={{0,4},{4,12},{12,8},{8,0},{1,5},{5,13},{13,9},{9,1},{2,6},{6,14},{... | collective-permute-start | bytes 589832 | tf_op jit(solution)/shard_map/ppermute | solution.py:203
  59.1 8.7 %collective-permute-start.12 = (bf16[96,1024]{1,0:T(8,128)(2,1)S(1)}, bf16[96,1024]{1,0:T(8,128)(2,1)S(1)}, u32[]{:S(2)}, u32[]{:S(2)}) collective-permute-start(bf16[96,1024]{1,0:T(8,128)(2,1)S(1)} %get-tuple-element.20.refs_0_), channel_id=1, source_target_pairs={{0,4},{4,12},{12,8},{8,0},{1,5},{5,13},{13,9},{9,1},{2,6},{6,14},{... | collective-permute-start | bytes 589832 | tf_op jit(solution)/shard_map/ppermute | solution.py:203
  59.2 12.9 %collective-permute-start.9 = (bf16[96,1024]{1,0:T(8,128)(2,1)S(1)}, bf16[96,1024]{1,0:T(8,128)(2,1)S(1)}, u32[]{:S(2)}, u32[]{:S(2)}) collective-permute-start(bf16[96,1024]{1,0:T(8,128)(2,1)S(1)} %get-tuple-element.21.refs_0_), channel_id=1, source_target_pairs={{0,4},{4,12},{12,8},{8,0},{1,5},{5,13},{13,9},{9,1},{2,6},{6,14},{... | collective-permute-start | bytes 589832 | tf_op jit(solution)/shard_map/ppermute | solution.py:203
  67.9 8.7 %collective-permute-start.13 = (bf16[96,1024]{1,0:T(8,128)(2,1)S(1)}, bf16[96,1024]{1,0:T(8,128)(2,1)S(1)}, u32[]{:S(2)}, u32[]{:S(2)}) collective-permute-start(bf16[96,1024]{1,0:T(8,128)(2,1)S(1)} %collective-permute-done.12.refs_1_), channel_id=1, source_target_pairs={{0,4},{4,12},{12,8},{8,0},{1,5},{5,13},{13,9},{9,1},{2,6},{6,14},{... | collective-permute-start | bytes 589832 | tf_op jit(solution)/shard_map/ppermute | solution.py:203
  72.1 8.4 %collective-permute-start.10 = (bf16[96,1024]{1,0:T(8,128)(2,1)S(1)}, bf16[96,1024]{1,0:T(8,128)(2,1)S(1)}, u32[]{:S(2)}, u32[]{:S(2)}) collective-permute-start(bf16[96,1024]{1,0:T(8,128)(2,1)S(1)} %collective-permute-done.9.refs_1_), channel_id=1, source_target_pairs={{0,4},{4,12},{12,8},{8,0},{1,5},{5,13},{13,9},{9,1},{2,6},{6,14},{... | collective-permute-start | bytes 589832 | tf_op jit(solution)/shard_map/ppermute | solution.py:203
  76.6 6.6 %collective-permute-start.14 = (bf16[96,1024]{1,0:T(8,128)(2,1)S(1)}, bf16[96,1024]{1,0:T(8,128)(2,1)S(1)}, u32[]{:S(2)}, u32[]{:S(2)}) collective-permute-start(bf16[96,1024]{1,0:T(8,128)(2,1)S(1)} %collective-permute-done.13.refs_2_), channel_id=1, source_target_pairs={{0,4},{4,12},{12,8},{8,0},{1,5},{5,13},{13,9},{9,1},{2,6},{6,14},{... | collective-permute-start | bytes 589832 | tf_op jit(solution)/shard_map/ppermute | solution.py:203
  80.4 6.9 %collective-permute-start.11 = (bf16[96,1024]{1,0:T(8,128)(2,1)S(1)}, bf16[96,1024]{1,0:T(8,128)(2,1)S(1)}, u32[]{:S(2)}, u32[]{:S(2)}) collective-permute-start(bf16[96,1024]{1,0:T(8,128)(2,1)S(1)} %collective-permute-done.10.refs_2_), channel_id=1, source_target_pairs={{0,4},{4,12},{12,8},{8,0},{1,5},{5,13},{13,9},{9,1},{2,6},{6,14},{... | collective-permute-start | bytes 589832 | tf_op jit(solution)/shard_map/ppermute | solution.py:203

commit v2 on v0

v2 whole, which is shorter than its diff:
```python
import functools

import jax
import jax.numpy as jnp
from jax import lax
from jax.experimental import pallas as pl
from jax.experimental.pallas import tpu as pltpu
from jax.sharding import PartitionSpec as P

LANES = 128
GROUP = 8
CHAINS = 2
TILE = 512
VMEM_LIMIT = 24 * 1024 * 1024
IN_VMEM = pl.BlockSpec(memory_space=pltpu.VMEM)
IN_SMEM = pl.BlockSpec(memory_space=pltpu.SMEM)
IN_PLACE = pl.BlockSpec(memory_space=pl.ANY)


def params():
    return pltpu.CompilerParams(vmem_limit_bytes=VMEM_LIMIT)


def cost(byte_count):
    return pl.CostEstimate(flops=0, bytes_accessed=byte_count, transcendentals=0)


def ring_order(count):
    return [0] + list(range(1, count, 2)) + list(range(count - 2 + count % 2, 0, -2))


def ring_shift(count, step):
    order = ring_order(count)
    return [(order[i], order[(i + step) % count]) for i in range(count)]


def pack_kernel(ids_ref, values_ref, out_ref, wide_ref):
    active, rows = ids_ref.shape
    wide_ref[0:rows, :] = ids_ref[...].astype(jnp.float32).T
    wide_ref[rows:, :] = values_ref[...].astype(jnp.float32).T
    even = wide_ref[pl.ds(0, rows, stride=2), :]
    odd = wide_ref[pl.ds(1, rows, stride=2), :]
    out_ref[...] = jnp.concatenate([even, odd], axis=1)


def pack(ids, values):
    rows, active = ids.shape
    return pl.pallas_call(
        pack_kernel,
        in_specs=[IN_VMEM, IN_VMEM],
        out_specs=IN_VMEM,
        out_shape=jax.ShapeDtypeStruct((rows, 2 * active), jnp.float32),
        scratch_shapes=[pltpu.VMEM((2 * rows, active), jnp.float32)],
        compiler_params=params(),
        cost_estimate=cost(32 * 1024 * 1024),
        name="pack",
    )(ids.T, values.T)


def build_table(first, packed_ref, table_ref, keys_ref):
    rows, width = table_ref.shape
    half = rows // 2
    per_row = 2
    rows_per_group = GROUP // per_row
    high_count = width // LANES
    ids = packed_ref[0:half, :].astype(jnp.int32) - first
    high = lax.shift_right_arithmetic(ids, 7)
    low = jnp.bitwise_and(ids, LANES - 1)
    row = lax.broadcasted_iota(jnp.int32, ids.shape, 0)
    lane = lax.broadcasted_iota(jnp.int32, ids.shape, 1)
    place = per_row * jnp.bitwise_and(row, rows_per_group - 1) + jnp.where(lane >= LANES // 2, 1, 0)
    inside = jnp.logical_and(ids >= 0, ids < width)
    key = jnp.where(inside, high * GROUP + place, -1)
    keys_ref[0:half, :] = key.astype(jnp.float32)
    keys_ref[half : 2 * half, :] = low.astype(jnp.float32)
    tall = lax.broadcasted_iota(jnp.int32, (high_count * GROUP, LANES), 0).astype(jnp.float32).astype(jnp.bfloat16)
    wide = lax.broadcasted_iota(jnp.int32, (LANES, LANES), 0).astype(jnp.float32).astype(jnp.bfloat16)
    zero, one = jnp.zeros((), jnp.bfloat16), jnp.ones((), jnp.bfloat16)

    def group_rows(r0):
        left, right = [], []
        for r in range(r0, r0 + rows_per_group):
            key = keys_ref[r : r + 1, :].astype(jnp.bfloat16)
            low = keys_ref[half + r : half + r + 1, :].astype(jnp.bfloat16)
            value = packed_ref[half + r : half + r + 1, :].astype(jnp.bfloat16)
            left.append(jnp.where(tall == key, value, zero))
            right.append(jnp.where(wide == low, one, zero))
        left = jnp.concatenate(left, axis=1)
        right = jnp.concatenate(right, axis=1)
        product = lax.dot_general(left, right, (((1,), (1,)), ((), ())), preferred_element_type=jnp.float32)
        pieces = [product[h * GROUP : (h + 1) * GROUP, :] for h in range(high_count)]
        return jnp.concatenate(pieces, axis=1)

    for i in range(rows // (2 * GROUP)):
        r0 = i * (2 * rows_per_group)
        both = jnp.concatenate([group_rows(r0), group_rows(r0 + rows_per_group)], axis=0)
        table_ref[i * 2 * GROUP : (i + 1) * 2 * GROUP, :] = both.astype(jnp.bfloat16)


def multiply(table_ref, weight_ref, column0, columns, write):
    tile = min(TILE, columns)
    for c in range(0, columns, tile):
        product = jnp.dot(
            table_ref[...], weight_ref[:, column0 + c : column0 + c + tile], preferred_element_type=jnp.float32
        )
        write(slice(c, c + tile), product)


def build_kernel(blocks, column0, first_ref, *refs):
    packed, refs = refs[:blocks], refs[blocks:]
    if column0 is not None:
        weight_ref, refs = refs[0], refs[1:]
    tables, refs = refs[:blocks], refs[blocks:]
    for packed_ref, table_ref in zip(packed, tables):
        build_table(first_ref[0], packed_ref, table_ref, refs[-1])
    if column0 is not None:
        out_ref = refs[0]

        def write(at, product):
            out_ref[:, at] = product.astype(out_ref.dtype)

        multiply(tables[0], weight_ref, column0, out_ref.shape[1], write)


def build(first, packed, width, weight=None, column0=None, columns=None):
    blocks = len(packed)
    rows = packed[0].shape[0]
    tables = [jax.ShapeDtypeStruct((rows, width), jnp.bfloat16)] * blocks
    extra = [] if weight is None else [weight]
    sums = [] if weight is None else [jax.ShapeDtypeStruct((rows, columns), jnp.bfloat16)]
    return pl.pallas_call(
        functools.partial(build_kernel, blocks, column0),
        in_specs=[IN_SMEM] + [IN_VMEM] * (blocks + len(extra)),
        out_specs=[IN_VMEM] * (blocks + len(sums)),
        out_shape=tables + sums,
        scratch_shapes=[pltpu.VMEM(packed[0].shape, jnp.float32)],
        compiler_params=params(),
        cost_estimate=cost(1 << 20),
        name="build",
    )(first, *packed, *extra)


def partial_kernel(column0, added, table_ref, weight_ref, *refs):
    out_ref = refs[-1]

    def write(at, product):
        if added:
            product = product + refs[0][:, at].astype(jnp.float32)
        out_ref[:, at] = product.astype(out_ref.dtype)

    multiply(table_ref, weight_ref, column0, out_ref.shape[1], write)


def partial_sum(table, weight, column0, columns, arrived=None):
    extra = [] if arrived is None else [arrived]
    return pl.pallas_call(
        functools.partial(partial_kernel, column0, len(extra)),
        in_specs=[IN_VMEM] * (2 + len(extra)),
        out_specs=IN_VMEM,
        out_shape=jax.ShapeDtypeStruct((table.shape[0], columns), jnp.bfloat16),
        compiler_params=params(),
        cost_estimate=cost(1 << 20),
        name="partial_sum",
    )(table, weight, *extra)


def error_kernel(column0, table_ref, weight_ref, arrived_ref, bias_ref, tokens_ref, out_ref):
    def write(at, product):
        where = slice(column0 + at.start, column0 + at.stop)
        total = product + arrived_ref[:, at].astype(jnp.float32) + bias_ref[:, where]
        out_ref[:, at] = (total - tokens_ref[:, where].astype(jnp.float32)).astype(out_ref.dtype)

    multiply(table_ref, weight_ref, column0, out_ref.shape[1], write)


def token_errors(table, weight, column0, arrived, bias, tokens):
    return pl.pallas_call(
        functools.partial(error_kernel, column0),
        in_specs=[IN_VMEM] * 5,
        out_specs=IN_VMEM,
        out_shape=jax.ShapeDtypeStruct(arrived.shape, jnp.bfloat16),
        compiler_params=params(),
        cost_estimate=cost(1 << 20),
        name="token_errors",
    )(table, weight, arrived, bias, tokens)


def grad_kernel(blocks, column0, tile, table_ref, *refs):
    errors = refs[:blocks]
    out_ref, all_ref, made_ref, sems = refs[-4:]
    rows, columns = errors[0].shape
    for b in range(blocks):
        all_ref[b * rows : (b + 1) * rows, :] = errors[b][...]
    copies = []
    for i, c in enumerate(range(0, columns, tile)):
        product = jnp.dot(table_ref[...], all_ref[:, c : c + tile], preferred_element_type=jnp.float32)
        made_ref[:, c : c + tile] = product.astype(made_ref.dtype)
        copy = pltpu.make_async_copy(
            made_ref.at[:, pl.ds(c, tile)], out_ref.at[:, pl.ds(column0 + c, tile)], sems.at[i]
        )
        copy.start()
        copies.append(copy)
    for copy in copies:
        copy.wait()


def grad_part(table_t, errors, features, column0, previous, tile=256):
    width, tokens = table_t.shape
    rows, columns = errors[0].shape
    blocks = len(errors)
    tile = min(tile, columns)
    in_specs = [IN_VMEM] * (1 + blocks)
    operands = [table_t, *errors]
    aliases = {}
    if previous is not None:
        in_specs.append(IN_PLACE)
        operands.append(previous)
        aliases = {len(operands) - 1: 0}
    return pl.pallas_call(
        functools.partial(grad_kernel, blocks, column0, tile),
        in_specs=in_specs,
        out_specs=IN_PLACE,
        out_shape=jax.ShapeDtypeStruct((width, features), jnp.bfloat16),
        scratch_shapes=[
            pltpu.VMEM((tokens, columns), jnp.bfloat16),
            pltpu.VMEM((width, columns), jnp.bfloat16),
            pltpu.SemaphoreType.DMA((columns // tile,)),
        ],
        input_output_aliases=aliases,
        compiler_params=params(),
        cost_estimate=cost(1 << 20),
        name="grad",
    )(*operands)


def local(count, tokens, active_latent_index, latent_values, dec_bias, dec_weight):
    width, features = dec_weight.shape
    columns = features // CHAINS
    starts = [c * columns for c in range(CHAINS)]
    first = (lax.axis_index("latent") * width).astype(jnp.int32).reshape(1)
    bias = dec_bias.reshape(1, features)

    def send(x, step=1):
        return lax.ppermute(x, "latent", ring_shift(count, step))

    own = pack(active_latent_index, latent_values)
    packed = lax.optimization_barrier([own] + [send(own, k) for k in range(1, count)])
    tables = [None] * count
    tables[1], sent = build(first, [packed[1]], width, dec_weight, 0, columns)
    running = [sent] + [partial_sum(tables[1], dec_weight, at, columns) for at in starts[1:]]
    later = list(range(2, count)) + [0]
    last_sent, *waiting = lax.optimization_barrier([running[-1]] + [packed[k] for k in later])
    running[-1] = last_sent
    for k, table in zip(later, build(first, waiting, width)):
        tables[k] = table
    errors = [None] * CHAINS
    for k in later:
        for c, at in enumerate(starts):
            arrived = send(running[c])
            if k:
                running[c] = partial_sum(tables[k], dec_weight, at, columns, arrived)
            else:
                errors[c] = [token_errors(tables[k], dec_weight, at, arrived, bias, tokens)]
    for step in range(1, count):
        for c in range(CHAINS):
            errors[c].append(send(errors[c][-1]))
    table_t = jnp.concatenate(tables, axis=0).T
    grad = None
    for c, at in enumerate(starts):
        grad = grad_part(table_t, errors[c], features, at, grad)
    token_error = jnp.concatenate([errors[c][0] for c in range(CHAINS)], axis=1)
    return token_error, grad


def solution(mesh):
    in_specs = (
        P(("groups", "latent"), ("dp", "mp")),
        P(("groups", "latent"), None),
        P(("groups", "latent"), None),
        P(("groups", "dp", "mp")),
        P(("groups", "latent"), ("dp", "mp")),
    )
    out_specs = (P(("groups", "latent"), ("dp", "mp")), P(("groups", "latent"), ("dp", "mp")))
    body = functools.partial(local, mesh.shape["latent"])
    return jax.shard_map(body, mesh=mesh, in_specs=in_specs, out_specs=out_specs, check_vma=False)
```

time: 216 us -> 77.1 us (0.36)
  waiting for transfers between devices: 123 us -> 39 us
  blocking collectives: 29.8 us -> 0 us
  other arithmetic: 32.2 us -> 2.77 us
  Pallas kernels: 0 us -> 16.3 us
  matrix products: 15.3 us -> 0 us
  between operations: 14.1 us -> 0.93 us
  starting transfers between devices: 0.08 us -> 10.1 us
  local copies, waits for them, and re-layouts: 1.28 us -> 7.65 us
    psum x1 -> x0, waiting for transfers between devices: 122 us -> none  [local(): summed = lax.psum(partial_value, 'latent')]
    ppermute x0 -> x15, waiting for transfers between devices: none -> 39 us  [send(): return lax.ppermute(x, 'latent', ring_shift(count, step))]
    all_gather x2 -> x0, blocking collectives: 29.8 us -> none  [the longest x1 15.1 us: local(): all_values = lax.all_gather(latent_values, 'latent', axis=0, tiled=True)]
    reduce_sum x6 -> x0, other arithmetic: 29.3 us -> none  [one_block(): return jnp.sum(placed, axis=1, dtype=jnp.float32).astype(jnp.bfloat16)]
    pallas_call x0 -> x12, Pallas kernels: none -> 16.3 us  [the longest x2 7.73 us: grad_part(): pl.pallas_call(functools.partial(grad_kernel, blocks, column0, tile), in_...]
    dot_general x2 -> x0, matrix products: 15.3 us -> none  [the longest x1 8.46 us: local(): jnp.dot(onehot_table, dec_weight, preferred_element_type=jnp.float32)]
    ppermute x0 -> x15, starting transfers between devices: none -> 10.1 us  [send(): return lax.ppermute(x, 'latent', ring_shift(count, step))]
    unnamed x2 -> x12, local copies, waits for them, and re-layouts: 0.01 us -> 5.82 us
  transfers between devices with their start and end apart: 2 -> 15, of which waited for: 1 -> 14; matrix products, arithmetic and copies ran while one was open for 18% -> 6% of each run, Pallas kernels for 0% -> 14%
where the time goes in v2:
time: 77.1 us; the launch traced here: 76.7 us
  waiting for transfers between devices  39 us (51%)
  Pallas kernels  16.3 us (21%)
  starting transfers between devices  10.1 us (13%)
  local copies, waits for them, and re-layouts  7.65 us (10%)
  other arithmetic  2.77 us (4%)
  between operations  0.93 us (1%)
    ppermute x15, waiting for transfers between devices, send(): return lax.ppermute(x, 'latent', ring_shift(count, step))  39 us
    ppermute x15, starting transfers between devices, send(): return lax.ppermute(x, 'latent', ring_shift(count, step))  10.1 us
    pallas_call x2, Pallas kernels, grad_part(): pl.pallas_call(functools.partial(grad_kernel, blocks, column0, tile), in_...  7.73 us
    unnamed x12, local copies, waits for them, and re-layouts  5.82 us
    pallas_call x5, Pallas kernels, partial_sum(): pl.pallas_call(functools.partial(partial_kernel, column0, len(extra)), in...  4.01 us
    pallas_call x2, Pallas kernels, build(): pl.pallas_call(functools.partial(build_kernel, blocks, column0), in_specs...  2.72 us
    transpose x1, other arithmetic, local(): table_t = jnp.concatenate(tables, axis=0).T  2 us
    pallas_call x4, local copies, waits for them, and re-layouts, build(): pl.pallas_call(functools.partial(build_kernel, blocks, column0), in_specs...  1.84 us
  transfers between devices with their start and end apart: 15, of which 14 were waited for; matrix products, arithmetic and copies ran while one was open for 6% of the time, Pallas kernels for 14%

profile of v2, /device:TPU:0, one launch (start us, length us, event | category | flops | bytes accessed | tf_op | source)
XLA Modules:
  0.0 76.7 jit_solution(9232325229713134421)
XLA Ops:
  0.6 0.7 copy-done.3
  1.4 0.7 copy-done.5
  2.1 0.2 pack.1.refs_2_
  2.3 3.1 %collective-permute-start = (f32[96,128]{1,0:T(8,128)S(1)}, f32[96,128]{1,0:T(8,128)S(1)}, u32[]{:S(2)}, u32[]{:S(2)}) collective-permute-start(f32[96,128]{1,0:T(8,128)S(1)} %pack.1.refs_2_), channel_id=1, source_target_pairs={{0,4},{4,12},{12,8},{8,0},{1,5},{5,13},{13,9},{9,1},{2,6},{6,14},{... | collective-permute-start | bytes 147464 | tf_op jit(solution)/shard_map/ppermute | solution.py:244
  5.4 2.5 %collective-permute-start.1 = (f32[96,128]{1,0:T(8,128)S(1)}, f32[96,128]{1,0:T(8,128)S(1)}, u32[]{:S(2)}, u32[]{:S(2)}) collective-permute-start(f32[96,128]{1,0:T(8,128)S(1)} %pack.1.refs_2_), channel_id=1, source_target_pairs={{0,12},{4,8},{12,0},{8,4},{1,13},{5,9},{13,1},{9,5},{2,14},{6,10},... | collective-permute-start | bytes 147464 | tf_op jit(solution)/shard_map/ppermute | solution.py:244
  7.8 1.6 %collective-permute-start.2 = (f32[96,128]{1,0:T(8,128)S(1)}, f32[96,128]{1,0:T(8,128)S(1)}, u32[]{:S(2)}, u32[]{:S(2)}) collective-permute-start(f32[96,128]{1,0:T(8,128)S(1)} %pack.1.refs_2_), channel_id=1, source_target_pairs={{0,8},{4,0},{12,4},{8,12},{1,9},{5,1},{13,5},{9,13},{2,10},{6,2},{... | collective-permute-start | bytes 147464 | tf_op jit(solution)/shard_map/ppermute | solution.py:244
  9.4 2.1 %collective-permute-done.1.refs_0_ = f32[96,128]{1,0:T(8,128)S(1)} collective-permute-done((f32[96,128]{1,0:T(8,128)S(1)}, f32[96,128]{1,0:T(8,128)S(1)}, u32[]{:S(2)}, u32[]{:S(2)}) %collective-permute-start.1) | collective-permute-done | bytes 49184 | tf_op jit(solution)/shard_map/ppermute | solution.py:244
  11.6 0.5 collective-permute-done.2.refs_1_
  12.1 3.4 %copy-done = bf16[2048,2048]{1,0:T(8,128)(2,1)S(1)} copy-done((bf16[2048,2048]{1,0:T(8,128)(2,1)S(1)}, bf16[2048,2048]{1,0:T(8,128)(2,1)}, u32[]{:S(2)}) %copy-start) | copy-done | bytes 8388632
  15.4 1.3 %build.2 = (bf16[96,2048]{1,0:T(8,128)(2,1)S(1)}, bf16[96,1024]{1,0:T(8,128)(2,1)S(1)}) custom-call(s32[1]{0:T(128)} %bitcast.first_ref, f32[96,128]{1,0:T(8,128)S(1)} %collective-permute-done.refs_0_, bf16[2048,2048]{1,0:T(8,128)(2,1)S(1)} %copy-done), custom_call_target="tpu_custom_call" | custom-call | bytes 1048576 | tf_op jit(solution)/shard_map/build/pallas_call | solution.py:131
  16.8 1.1 %collective-permute-start.3 = (bf16[96,1024]{1,0:T(8,128)(2,1)S(1)}, bf16[96,1024]{1,0:T(8,128)(2,1)S(1)}, u32[]{:S(2)}, u32[]{:S(2)}) collective-permute-start(bf16[96,1024]{1,0:T(8,128)(2,1)S(1)} %get-tuple-element.26), channel_id=1, source_target_pairs={{0,4},{4,12},{12,8},{8,0},{1,5},{5,13},{13,9},{9,1},{2,6},{6,14},{... | collective-permute-start | bytes 589832 | tf_op jit(solution)/shard_map/ppermute | solution.py:244
  17.9 1.0 %copy-done.1 = bf16[2048,2048]{1,0:T(8,128)(2,1)S(1)} copy-done((bf16[2048,2048]{1,0:T(8,128)(2,1)S(1)}, bf16[2048,2048]{1,0:T(8,128)(2,1)}, u32[]{:S(2)}) %copy-start.1) | copy-done | bytes 8388632
  18.8 0.8 %partial_sum.5 = bf16[96,1024]{1,0:T(8,128)(2,1)S(1)} custom-call(bf16[96,2048]{1,0:T(8,128)(2,1)S(1)} %get-tuple-element.16.table_ref, bf16[2048,2048]{1,0:T(8,128)(2,1)S(1)} %copy-done.1), custom_call_target="tpu_custom_call" | custom-call | bytes 1048576 | tf_op jit(solution)/shard_map/partial_sum/pallas_call | solution.py:156
  19.6 1.1 %collective-permute-start.6 = (bf16[96,1024]{1,0:T(8,128)(2,1)S(1)}, bf16[96,1024]{1,0:T(8,128)(2,1)S(1)}, u32[]{:S(2)}, u32[]{:S(2)}) collective-permute-start(bf16[96,1024]{1,0:T(8,128)(2,1)S(1)} %partial_sum.5), channel_id=1, source_target_pairs={{0,4},{4,12},{12,8},{8,0},{1,5},{5,13},{13,9},{9,1},{2,6},{6,14},{... | collective-permute-start | bytes 589832 | tf_op jit(solution)/shard_map/ppermute | solution.py:244
  20.7 1.4 %build.3 = (bf16[96,2048]{1,0:T(8,128)(2,1)S(1)}, bf16[96,2048]{1,0:T(8,128)(2,1)S(1)}, bf16[96,2048]{1,0:T(8,128)(2,1)S(1)}) custom-call(s32[1]{0:T(128)} %bitcast.first_ref, f32[96,128]{1,0:T(8,128)S(1)} %collective-permute-done.1.refs_0_, f32[96,128]{1,0:T(8,128)S(1)} %collective-permute-done.2.refs_1_, f32[96,128]{1,0:T(8,128)S(1)} %pack.1.refs_2_), custom_call_target="tpu_custom_call" | custom-call | bytes 1048576 | tf_op jit(solution)/shard_map/build/pallas_call | solution.py:131
  22.1 3.2 %collective-permute-done.3.refs_0_ = bf16[96,1024]{1,0:T(8,128)(2,1)S(1)} collective-permute-done((bf16[96,1024]{1,0:T(8,128)(2,1)S(1)}, bf16[96,1024]{1,0:T(8,128)(2,1)S(1)}, u32[]{:S(2)}, u32[]{:S(2)}) %collective-permute-start.3) | collective-permute-done | bytes 196640 | tf_op jit(solution)/shard_map/ppermute | solution.py:244
  25.3 0.8 %partial_sum.6 = bf16[96,1024]{1,0:T(8,128)(2,1)S(1)} custom-call(bf16[96,2048]{1,0:T(8,128)(2,1)S(1)} %get-tuple-element.25.table_ref, bf16[2048,2048]{1,0:T(8,128)(2,1)S(1)} %copy-done.1, bf16[96,1024]{1,0:T(8,128)(2,1)S(1)} %collective-permute-done.3.refs_0_), custom_call_target="tpu_custom_call" | custom-call | bytes 1048576 | tf_op jit(solution)/shard_map/partial_sum/pallas_call | solution.py:156
  26.1 0.1 collective-permute-start.4
  26.2 3.3 %collective-permute-done.6.refs_0_ = bf16[96,1024]{1,0:T(8,128)(2,1)S(1)} collective-permute-done((bf16[96,1024]{1,0:T(8,128)(2,1)S(1)}, bf16[96,1024]{1,0:T(8,128)(2,1)S(1)}, u32[]{:S(2)}, u32[]{:S(2)}) %collective-permute-start.6) | collective-permute-done | bytes 196640 | tf_op jit(solution)/shard_map/ppermute | solution.py:244
  29.5 0.8 %partial_sum.8 = bf16[96,1024]{1,0:T(8,128)(2,1)S(1)} custom-call(bf16[96,2048]{1,0:T(8,128)(2,1)S(1)} %get-tuple-element.25.table_ref, bf16[2048,2048]{1,0:T(8,128)(2,1)S(1)} %copy-done.1, bf16[96,1024]{1,0:T(8,128)(2,1)S(1)} %collective-permute-done.6.refs_0_), custom_call_target="tpu_custom_call" | custom-call | bytes 1048576 | tf_op jit(solution)/shard_map/partial_sum/pallas_call | solution.py:156
  30.3 0.1 collective-permute-start.7
  30.4 4.3 %collective-permute-done.4.refs_0_ = bf16[96,1024]{1,0:T(8,128)(2,1)S(1)} collective-permute-done((bf16[96,1024]{1,0:T(8,128)(2,1)S(1)}, bf16[96,1024]{1,0:T(8,128)(2,1)S(1)}, u32[]{:S(2)}, u32[]{:S(2)}) %collective-permute-start.4) | collective-permute-done | bytes 196640 | tf_op jit(solution)/shard_map/ppermute | solution.py:244
  34.7 0.8 %partial_sum.7 = bf16[96,1024]{1,0:T(8,128)(2,1)S(1)} custom-call(bf16[96,2048]{1,0:T(8,128)(2,1)S(1)} %get-tuple-element.24.table_ref, bf16[2048,2048]{1,0:T(8,128)(2,1)S(1)} %copy-done.1, bf16[96,1024]{1,0:T(8,128)(2,1)S(1)} %collective-permute-done.4.refs_0_), custom_call_target="tpu_custom_call" | custom-call | bytes 1048576 | tf_op jit(solution)/shard_map/partial_sum/pallas_call | solution.py:156
  35.6 0.1 collective-permute-start.5
  35.6 3.0 %collective-permute-done.7.refs_0_ = bf16[96,1024]{1,0:T(8,128)(2,1)S(1)} collective-permute-done((bf16[96,1024]{1,0:T(8,128)(2,1)S(1)}, bf16[96,1024]{1,0:T(8,128)(2,1)S(1)}, u32[]{:S(2)}, u32[]{:S(2)}) %collective-permute-start.7) | collective-permute-done | bytes 196640 | tf_op jit(solution)/shard_map/ppermute | solution.py:244
  38.6 0.8 %partial_sum.9 = bf16[96,1024]{1,0:T(8,128)(2,1)S(1)} custom-call(bf16[96,2048]{1,0:T(8,128)(2,1)S(1)} %get-tuple-element.24.table_ref, bf16[2048,2048]{1,0:T(8,128)(2,1)S(1)} %copy-done.1, bf16[96,1024]{1,0:T(8,128)(2,1)S(1)} %collective-permute-done.7.refs_0_), custom_call_target="tpu_custom_call" | custom-call | bytes 1048576 | tf_op jit(solution)/shard_map/partial_sum/pallas_call | solution.py:156
  39.4 0.1 collective-permute-start.8
  39.5 3.4 %collective-permute-done.5.arrived_ref = bf16[96,1024]{1,0:T(8,128)(2,1)S(1)} collective-permute-done((bf16[96,1024]{1,0:T(8,128)(2,1)S(1)}, bf16[96,1024]{1,0:T(8,128)(2,1)S(1)}, u32[]{:S(2)}, u32[]{:S(2)}) %collective-permute-start.5) | collective-permute-done | bytes 196640 | tf_op jit(solution)/shard_map/ppermute | solution.py:244
  43.0 0.8 %token_errors.2.refs_0_ = bf16[96,1024]{1,0:T(8,128)(2,1)S(1)} custom-call(bf16[96,2048]{1,0:T(8,128)(2,1)S(1)} %get-tuple-element.23.table_ref, bf16[2048,2048]{1,0:T(8,128)(2,1)S(1)} %copy-done.1, bf16[96,1024]{1,0:T(8,128)(2,1)S(1)} %collective-permute-done.5.arrived_ref, f32[1,2048]{1,0:T(1,128)S(1)} %bitcast.7, bf16[96,2048]{1,0:T(8,128)(2,1)S(1)} %copy-done.2), custom_call_target="tpu_custom_call" | custom-call | bytes 1048576 | tf_op jit(solution)/shard_map/token_errors/pallas_call | solution.py:177
  43.8 0.1 collective-permute-start.12
  43.9 4.3 %collective-permute-done.8.arrived_ref = bf16[96,1024]{1,0:T(8,128)(2,1)S(1)} collective-permute-done((bf16[96,1024]{1,0:T(8,128)(2,1)S(1)}, bf16[96,1024]{1,0:T(8,128)(2,1)S(1)}, u32[]{:S(2)}, u32[]{:S(2)}) %collective-permute-start.8) | collective-permute-done | bytes 196640 | tf_op jit(solution)/shard_map/ppermute | solution.py:244
  48.2 0.8 %token_errors.3.refs_0_ = bf16[96,1024]{1,0:T(8,128)(2,1)S(1)} custom-call(bf16[96,2048]{1,0:T(8,128)(2,1)S(1)} %get-tuple-element.23.table_ref, bf16[2048,2048]{1,0:T(8,128)(2,1)S(1)} %copy-done.1, bf16[96,1024]{1,0:T(8,128)(2,1)S(1)} %collective-permute-done.8.arrived_ref, f32[1,2048]{1,0:T(1,128)S(1)} %bitcast.8, bf16[96,2048]{1,0:T(8,128)(2,1)S(1)} %copy-done.2), custom_call_target="tpu_custom_call" | custom-call | bytes 1048576 | tf_op jit(solution)/shard_map/token_errors/pallas_call | solution.py:177
  49.1 0.1 collective-permute-start.9
  49.1 0.3 copy.10
  49.4 0.3 copy.11
  49.7 0.3 copy.8
  50.0 1.0 %copy.9 = bf16[96,2048]{0,1:T(8,128)(2,1)} copy(bf16[96,2048]{1,0:T(8,128)(2,1)S(1)} %get-tuple-element.16.table_ref) | data formatting | bytes 786432 | tf_op jit(solution)/shard_map/build/pallas_call | solution.py:131
  51.0 1.6 %collective-permute-done.12.refs_1_ = bf16[96,1024]{1,0:T(8,128)(2,1)S(1)} collective-permute-done((bf16[96,1024]{1,0:T(8,128)(2,1)S(1)}, bf16[96,1024]{1,0:T(8,128)(2,1)S(1)}, u32[]{:S(2)}, u32[]{:S(2)}) %collective-permute-start.12) | collective-permute-done | bytes 196640 | tf_op jit(solution)/shard_map/ppermute | solution.py:244
  52.6 0.3 collective-permute-start.13
  52.9 4.9 %collective-permute-done.9.refs_1_ = bf16[96,1024]{1,0:T(8,128)(2,1)S(1)} collective-permute-done((bf16[96,1024]{1,0:T(8,128)(2,1)S(1)}, bf16[96,1024]{1,0:T(8,128)(2,1)S(1)}, u32[]{:S(2)}, u32[]{:S(2)}) %collective-permute-start.9) | collective-permute-done | bytes 196640 | tf_op jit(solution)/shard_map/ppermute | solution.py:244
  57.8 2.0 %maximum_bitcast_fusion.table_ref = bf16[2048,384]{1,0:T(8,128)(2,1)S(1)} fusion(bf16[96,2048]{0,1:T(8,128)(2,1)S(1)} %copy.11, bf16[96,2048]{0,1:T(8,128)(2,1)S(1)} %copy.10, bf16[96,2048]{0,1:T(8,128)(2,1)} %copy.9, bf16[96,2048]{0,1:T(8,128)(2,1)S(1)} %copy.8), kind=kLoop, calls=%fused_computation | loop fusion | flops 6291456 | bytes 3145728 | tf_op jit(solution)/shard_map/transpose | solution.py:267
  59.8 2.2 %collective-permute-done.13.refs_2_ = bf16[96,1024]{1,0:T(8,128)(2,1)S(1)} collective-permute-done((bf16[96,1024]{1,0:T(8,128)(2,1)S(1)}, bf16[96,1024]{1,0:T(8,128)(2,1)S(1)}, u32[]{:S(2)}, u32[]{:S(2)}) %collective-permute-start.13) | collective-permute-done | bytes 196640 | tf_op jit(solution)/shard_map/ppermute | solution.py:244
  62.0 4.1 %collective-permute-done.10.refs_2_ = bf16[96,1024]{1,0:T(8,128)(2,1)S(1)} collective-permute-done((bf16[96,1024]{1,0:T(8,128)(2,1)S(1)}, bf16[96,1024]{1,0:T(8,128)(2,1)S(1)}, u32[]{:S(2)}, u32[]{:S(2)}) %collective-permute-start.10) | collective-permute-done | bytes 196640 | tf_op jit(solution)/shard_map/ppermute | solution.py:244
  66.1 0.8 %pad_maximum_fusion = bf16[96,2048]{1,0:T(8,128)(2,1)} fusion(bf16[96,1024]{1,0:T(8,128)(2,1)S(1)} %token_errors.3.refs_0_, bf16[96,1024]{1,0:T(8,128)(2,1)S(1)} %token_errors.2.refs_0_), kind=kLoop, calls=%fused_computation.1 | loop fusion | flops 786432 | bytes 786432 | tf_op jit(solution)/shard_map/concatenate | solution.py:271
  66.9 1.6 %collective-permute-done.14.refs_3_ = bf16[96,1024]{1,0:T(8,128)(2,1)S(1)} collective-permute-done((bf16[96,1024]{1,0:T(8,128)(2,1)S(1)}, bf16[96,1024]{1,0:T(8,128)(2,1)S(1)}, u32[]{:S(2)}, u32[]{:S(2)}) %collective-permute-start.14) | collective-permute-done | bytes 196640 | tf_op jit(solution)/shard_map/ppermute | solution.py:244
  68.6 3.9 %grad.2.refs_4_ = bf16[2048,2048]{1,0:T(8,128)(2,1)} custom-call(bf16[2048,384]{1,0:T(8,128)(2,1)S(1)} %maximum_bitcast_fusion.table_ref, bf16[96,1024]{1,0:T(8,128)(2,1)S(1)} %token_errors.2.refs_0_, bf16[96,1024]{1,0:T(8,128)(2,1)S(1)} %collective-permute-done.12.refs_1_, bf16[96,1024]{1,0:T(8,128)(2,1)S(1)} %collective-permute-done.13.refs_2_, ...), custom_call_target="tpu_custom_call" | custom-call | bytes 1048576 | tf_op jit(solution)/shard_map/grad/pallas_call | solution.py:219
  72.4 0.3 collective-permute-done.11.refs_3_
  72.7 3.9 %grad.3 = bf16[2048,2048]{1,0:T(8,128)(2,1)} custom-call(bf16[2048,384]{1,0:T(8,128)(2,1)S(1)} %maximum_bitcast_fusion.table_ref, bf16[96,1024]{1,0:T(8,128)(2,1)S(1)} %token_errors.3.refs_0_, bf16[96,1024]{1,0:T(8,128)(2,1)S(1)} %collective-permute-done.9.refs_1_, ...), custom_call_target="tpu_custom_call", output_to_operand_aliasing={{}: (5, {})} | custom-call | bytes 1048576 | tf_op jit(solution)/shard_map/grad/pallas_call | solution.py:219
  (12 shorter events, 0.0 us)
Async XLA Ops:
  0.6 0.8 copy-start.3
  1.4 0.7 copy-start.5
  2.3 7.1 %collective-permute-start = (f32[96,128]{1,0:T(8,128)S(1)}, f32[96,128]{1,0:T(8,128)S(1)}, u32[]{:S(2)}, u32[]{:S(2)}) collective-permute-start(f32[96,128]{1,0:T(8,128)S(1)} %pack.1.refs_2_), channel_id=1, source_target_pairs={{0,4},{4,12},{12,8},{8,0},{1,5},{5,13},{13,9},{9,1},{2,6},{6,14},{... | collective-permute-start | bytes 147464 | tf_op jit(solution)/shard_map/ppermute | solution.py:244
  5.4 6.2 %collective-permute-start.1 = (f32[96,128]{1,0:T(8,128)S(1)}, f32[96,128]{1,0:T(8,128)S(1)}, u32[]{:S(2)}, u32[]{:S(2)}) collective-permute-start(f32[96,128]{1,0:T(8,128)S(1)} %pack.1.refs_2_), channel_id=1, source_target_pairs={{0,12},{4,8},{12,0},{8,4},{1,13},{5,9},{13,1},{9,5},{2,14},{6,10},... | collective-permute-start | bytes 147464 | tf_op jit(solution)/shard_map/ppermute | solution.py:244
  7.8 4.2 %collective-permute-start.2 = (f32[96,128]{1,0:T(8,128)S(1)}, f32[96,128]{1,0:T(8,128)S(1)}, u32[]{:S(2)}, u32[]{:S(2)}) collective-permute-start(f32[96,128]{1,0:T(8,128)S(1)} %pack.1.refs_2_), channel_id=1, source_target_pairs={{0,8},{4,0},{12,4},{8,12},{1,9},{5,1},{13,5},{9,13},{2,10},{6,2},{... | collective-permute-start | bytes 147464 | tf_op jit(solution)/shard_map/ppermute | solution.py:244
  12.1 3.4 %copy-start = (bf16[2048,2048]{1,0:T(8,128)(2,1)S(1)}, bf16[2048,2048]{1,0:T(8,128)(2,1)}, u32[]{:S(2)}) copy-start(bf16[2048,2048]{1,0:T(8,128)(2,1)} %weight_ref.13) | copy-start | bytes 25165828
  15.4 3.4 %copy-start.1 = (bf16[2048,2048]{1,0:T(8,128)(2,1)S(1)}, bf16[2048,2048]{1,0:T(8,128)(2,1)}, u32[]{:S(2)}) copy-start(bf16[2048,2048]{1,0:T(8,128)(2,1)} %weight_ref.13) | copy-start | bytes 25165828
  16.8 8.5 %collective-permute-start.3 = (bf16[96,1024]{1,0:T(8,128)(2,1)S(1)}, bf16[96,1024]{1,0:T(8,128)(2,1)S(1)}, u32[]{:S(2)}, u32[]{:S(2)}) collective-permute-start(bf16[96,1024]{1,0:T(8,128)(2,1)S(1)} %get-tuple-element.26), channel_id=1, source_target_pairs={{0,4},{4,12},{12,8},{8,0},{1,5},{5,13},{13,9},{9,1},{2,6},{6,14},{... | collective-permute-start | bytes 589832 | tf_op jit(solution)/shard_map/ppermute | solution.py:244
  19.6 9.9 %collective-permute-start.6 = (bf16[96,1024]{1,0:T(8,128)(2,1)S(1)}, bf16[96,1024]{1,0:T(8,128)(2,1)S(1)}, u32[]{:S(2)}, u32[]{:S(2)}) collective-permute-start(bf16[96,1024]{1,0:T(8,128)(2,1)S(1)} %partial_sum.5), channel_id=1, source_target_pairs={{0,4},{4,12},{12,8},{8,0},{1,5},{5,13},{13,9},{9,1},{2,6},{6,14},{... | collective-permute-start | bytes 589832 | tf_op jit(solution)/shard_map/ppermute | solution.py:244
  26.1 8.6 %collective-permute-start.4 = (bf16[96,1024]{1,0:T(8,128)(2,1)S(1)}, bf16[96,1024]{1,0:T(8,128)(2,1)S(1)}, u32[]{:S(2)}, u32[]{:S(2)}) collective-permute-start(bf16[96,1024]{1,0:T(8,128)(2,1)S(1)} %partial_sum.6), channel_id=1, source_target_pairs={{0,4},{4,12},{12,8},{8,0},{1,5},{5,13},{13,9},{9,1},{2,6},{6,14},{... | collective-permute-start | bytes 589832 | tf_op jit(solution)/shard_map/ppermute | solution.py:244
  30.3 8.3 %collective-permute-start.7 = (bf16[96,1024]{1,0:T(8,128)(2,1)S(1)}, bf16[96,1024]{1,0:T(8,128)(2,1)S(1)}, u32[]{:S(2)}, u32[]{:S(2)}) collective-permute-start(bf16[96,1024]{1,0:T(8,128)(2,1)S(1)} %partial_sum.8), channel_id=1, source_target_pairs={{0,4},{4,12},{12,8},{8,0},{1,5},{5,13},{13,9},{9,1},{2,6},{6,14},{... | collective-permute-start | bytes 589832 | tf_op jit(solution)/shard_map/ppermute | solution.py:244
  35.5 7.4 %copy-start.2 = (bf16[96,2048]{1,0:T(8,128)(2,1)S(1)}, bf16[96,2048]{1,0:T(8,128)(2,1)}, u32[]{:S(2)}) copy-start(bf16[96,2048]{1,0:T(8,128)(2,1)} %tokens_ref.3) | copy-start | bytes 1179652
  35.6 7.4 %copy-start.4 = (f32[2048]{0:T(1024)S(1)}, f32[2048]{0:T(1024)}, u32[]{:S(2)}) copy-start(f32[2048]{0:T(1024)} %param.8) | copy-start | bytes 24580
  35.6 7.4 %collective-permute-start.5 = (bf16[96,1024]{1,0:T(8,128)(2,1)S(1)}, bf16[96,1024]{1,0:T(8,128)(2,1)S(1)}, u32[]{:S(2)}, u32[]{:S(2)}) collective-permute-start(bf16[96,1024]{1,0:T(8,128)(2,1)S(1)} %partial_sum.7), channel_id=1, source_target_pairs={{0,4},{4,12},{12,8},{8,0},{1,5},{5,13},{13,9},{9,1},{2,6},{6,14},{... | collective-permute-start | bytes 589832 | tf_op jit(solution)/shard_map/ppermute | solution.py:244
  39.4 8.8 %collective-permute-start.8 = (bf16[96,1024]{1,0:T(8,128)(2,1)S(1)}, bf16[96,1024]{1,0:T(8,128)(2,1)S(1)}, u32[]{:S(2)}, u32[]{:S(2)}) collective-permute-start(bf16[96,1024]{1,0:T(8,128)(2,1)S(1)} %partial_sum.9), channel_id=1, source_target_pairs={{0,4},{4,12},{12,8},{8,0},{1,5},{5,13},{13,9},{9,1},{2,6},{6,14},{... | collective-permute-start | bytes 589832 | tf_op jit(solution)/shard_map/ppermute | solution.py:244
  43.8 8.8 %collective-permute-start.12 = (bf16[96,1024]{1,0:T(8,128)(2,1)S(1)}, bf16[96,1024]{1,0:T(8,128)(2,1)S(1)}, u32[]{:S(2)}, u32[]{:S(2)}) collective-permute-start(bf16[96,1024]{1,0:T(8,128)(2,1)S(1)} %token_errors.2.refs_0_), channel_id=1, source_target_pairs={{0,4},{4,12},{12,8},{8,0},{1,5},{5,13},{13,9},{9,1},{2,6},{6,14},{... | collective-permute-start | bytes 589832 | tf_op jit(solution)/shard_map/ppermute | solution.py:244
  49.1 8.7 %collective-permute-start.9 = (bf16[96,1024]{1,0:T(8,128)(2,1)S(1)}, bf16[96,1024]{1,0:T(8,128)(2,1)S(1)}, u32[]{:S(2)}, u32[]{:S(2)}) collective-permute-start(bf16[96,1024]{1,0:T(8,128)(2,1)S(1)} %token_errors.3.refs_0_), channel_id=1, source_target_pairs={{0,4},{4,12},{12,8},{8,0},{1,5},{5,13},{13,9},{9,1},{2,6},{6,14},{... | collective-permute-start | bytes 589832 | tf_op jit(solution)/shard_map/ppermute | solution.py:244
  52.6 9.4 %collective-permute-start.13 = (bf16[96,1024]{1,0:T(8,128)(2,1)S(1)}, bf16[96,1024]{1,0:T(8,128)(2,1)S(1)}, u32[]{:S(2)}, u32[]{:S(2)}) collective-permute-start(bf16[96,1024]{1,0:T(8,128)(2,1)S(1)} %collective-permute-done.12.refs_1_), channel_id=1, source_target_pairs={{0,4},{4,12},{12,8},{8,0},{1,5},{5,13},{13,9},{9,1},{2,6},{6,14},{... | collective-permute-start | bytes 589832 | tf_op jit(solution)/shard_map/ppermute | solution.py:244
  57.8 8.4 %collective-permute-start.10 = (bf16[96,1024]{1,0:T(8,128)(2,1)S(1)}, bf16[96,1024]{1,0:T(8,128)(2,1)S(1)}, u32[]{:S(2)}, u32[]{:S(2)}) collective-permute-start(bf16[96,1024]{1,0:T(8,128)(2,1)S(1)} %collective-permute-done.9.refs_1_), channel_id=1, source_target_pairs={{0,4},{4,12},{12,8},{8,0},{1,5},{5,13},{13,9},{9,1},{2,6},{6,14},{... | collective-permute-start | bytes 589832 | tf_op jit(solution)/shard_map/ppermute | solution.py:244
  62.0 6.6 %collective-permute-start.14 = (bf16[96,1024]{1,0:T(8,128)(2,1)S(1)}, bf16[96,1024]{1,0:T(8,128)(2,1)S(1)}, u32[]{:S(2)}, u32[]{:S(2)}) collective-permute-start(bf16[96,1024]{1,0:T(8,128)(2,1)S(1)} %collective-permute-done.13.refs_2_), channel_id=1, source_target_pairs={{0,4},{4,12},{12,8},{8,0},{1,5},{5,13},{13,9},{9,1},{2,6},{6,14},{... | collective-permute-start | bytes 589832 | tf_op jit(solution)/shard_map/ppermute | solution.py:244
  66.1 6.6 %collective-permute-start.11 = (bf16[96,1024]{1,0:T(8,128)(2,1)S(1)}, bf16[96,1024]{1,0:T(8,128)(2,1)S(1)}, u32[]{:S(2)}, u32[]{:S(2)}) collective-permute-start(bf16[96,1024]{1,0:T(8,128)(2,1)S(1)} %collective-permute-done.10.refs_2_), channel_id=1, source_target_pairs={{0,4},{4,12},{12,8},{8,0},{1,5},{5,13},{13,9},{9,1},{2,6},{6,14},{... | collective-permute-start | bytes 589832 | tf_op jit(solution)/shard_map/ppermute | solution.py:244

commit v3 on v2

v3 whole, which is shorter than its diff:
```python
import functools

import jax
import jax.numpy as jnp
from jax import lax
from jax.experimental import pallas as pl
from jax.experimental.pallas import tpu as pltpu
from jax.sharding import PartitionSpec as P

LANES = 128
GROUP = 8
CHAINS = 2
TILE = 512
LOAD_PARTS = 8
VMEM_LIMIT = 24 * 1024 * 1024
IN_VMEM = pl.BlockSpec(memory_space=pltpu.VMEM)
IN_SMEM = pl.BlockSpec(memory_space=pltpu.SMEM)
IN_HBM = pl.BlockSpec(memory_space=pltpu.HBM)


def params():
    return pltpu.CompilerParams(vmem_limit_bytes=VMEM_LIMIT)


def in_hbm(array):
    return pltpu.with_memory_space_constraint(array, pltpu.HBM)


def cost(byte_count):
    return pl.CostEstimate(flops=0, bytes_accessed=byte_count, transcendentals=0)


def ring_order(count):
    return [0] + list(range(1, count, 2)) + list(range(count - 2 + count % 2, 0, -2))


def ring_shift(count, step):
    order = ring_order(count)
    return [(order[i], order[(i + step) % count]) for i in range(count)]


def pack_kernel(ids_in, values_in, out_ref, ids_ref, values_ref, wide_ref, sems):
    copies = [
        pltpu.make_async_copy(ids_in, ids_ref, sems.at[0]),
        pltpu.make_async_copy(values_in, values_ref, sems.at[1]),
    ]
    for copy in copies:
        copy.start()
    for copy in copies:
        copy.wait()
    active, rows = ids_ref.shape
    wide_ref[0:rows, :] = ids_ref[...].astype(jnp.float32).T
    wide_ref[rows:, :] = values_ref[...].astype(jnp.float32).T
    even = wide_ref[pl.ds(0, rows, stride=2), :]
    odd = wide_ref[pl.ds(1, rows, stride=2), :]
    out_ref[...] = jnp.concatenate([even, odd], axis=1)


def pack(ids, values):
    rows, active = ids.shape
    return pl.pallas_call(
        pack_kernel,
        in_specs=[IN_HBM, IN_HBM],
        out_specs=IN_VMEM,
        out_shape=jax.ShapeDtypeStruct((rows, 2 * active), jnp.float32),
        scratch_shapes=[
            pltpu.VMEM((active, rows), ids.dtype),
            pltpu.VMEM((active, rows), values.dtype),
            pltpu.VMEM((2 * rows, active), jnp.float32),
            pltpu.SemaphoreType.DMA((2,)),
        ],
        compiler_params=params(),
        cost_estimate=cost(1 << 20),
        name="pack",
    )(in_hbm(ids.T), in_hbm(values.T))


def build_table(first, packed_ref, table_ref, keys_ref):
    rows, width = table_ref.shape
    half = rows // 2
    per_row = 2
    rows_per_group = GROUP // per_row
    high_count = width // LANES
    ids = packed_ref[0:half, :].astype(jnp.int32) - first
    high = lax.shift_right_arithmetic(ids, 7)
    low = jnp.bitwise_and(ids, LANES - 1)
    row = lax.broadcasted_iota(jnp.int32, ids.shape, 0)
    lane = lax.broadcasted_iota(jnp.int32, ids.shape, 1)
    place = per_row * jnp.bitwise_and(row, rows_per_group - 1) + jnp.where(lane >= LANES // 2, 1, 0)
    inside = jnp.logical_and(ids >= 0, ids < width)
    key = jnp.where(inside, high * GROUP + place, -1)
    keys_ref[0:half, :] = key.astype(jnp.float32)
    keys_ref[half : 2 * half, :] = low.astype(jnp.float32)
    tall = lax.broadcasted_iota(jnp.int32, (high_count * GROUP, LANES), 0).astype(jnp.float32).astype(jnp.bfloat16)
    wide = lax.broadcasted_iota(jnp.int32, (LANES, LANES), 0).astype(jnp.float32).astype(jnp.bfloat16)
    zero, one = jnp.zeros((), jnp.bfloat16), jnp.ones((), jnp.bfloat16)

    def group_rows(r0):
        left, right = [], []
        for r in range(r0, r0 + rows_per_group):
            key = keys_ref[r : r + 1, :].astype(jnp.bfloat16)
            low = keys_ref[half + r : half + r + 1, :].astype(jnp.bfloat16)
            value = packed_ref[half + r : half + r + 1, :].astype(jnp.bfloat16)
            left.append(jnp.where(tall == key, value, zero))
            right.append(jnp.where(wide == low, one, zero))
        left = jnp.concatenate(left, axis=1)
        right = jnp.concatenate(right, axis=1)
        product = lax.dot_general(left, right, (((1,), (1,)), ((), ())), preferred_element_type=jnp.float32)
        pieces = [product[h * GROUP : (h + 1) * GROUP, :] for h in range(high_count)]
        return jnp.concatenate(pieces, axis=1)

    for i in range(rows // (2 * GROUP)):
        r0 = i * (2 * rows_per_group)
        both = jnp.concatenate([group_rows(r0), group_rows(r0 + rows_per_group)], axis=0)
        table_ref[i * 2 * GROUP : (i + 1) * 2 * GROUP, :] = both.astype(jnp.bfloat16)


def multiply(table_ref, weight_ref, write):
    columns = weight_ref.shape[1]
    tile = min(TILE, columns)
    for c in range(0, columns, tile):
        at = slice(c, c + tile)
        write(at, jnp.dot(table_ref[...], weight_ref[:, at], preferred_element_type=jnp.float32))


def load_and_multiply(weight_hbm, column0, weight_ref, sems, meanwhile, tables):
    width, columns = weight_ref.shape
    part = width // LOAD_PARTS
    spans = [slice(l, l + part) for l in range(0, width, part)]
    copies = [
        pltpu.make_async_copy(
            weight_hbm.at[pl.ds(at.start, part), pl.ds(column0, columns)],
            weight_ref.at[pl.ds(at.start, part), :],
            sems.at[i],
        )
        for i, at in enumerate(spans)
    ]
    for copy in copies:
        copy.start()
    meanwhile()
    total = None
    for copy, at in zip(copies, spans):
        copy.wait()
        stacked = jnp.concatenate([table_ref[:, at] for table_ref in tables], axis=0)
        product = jnp.dot(stacked, weight_ref[at, :], preferred_element_type=jnp.float32)
        total = product if total is None else total + product
    return total


def first_load_kernel(first_ref, packed_ref, weight_hbm, weight_ref, table_ref, out_ref, keys_ref, sems):
    def meanwhile():
        build_table(first_ref[0], packed_ref, table_ref, keys_ref)

    total = load_and_multiply(weight_hbm, 0, weight_ref, sems, meanwhile, [table_ref])
    out_ref[...] = total.astype(out_ref.dtype)


def first_load(first, packed, weight, columns):
    width = weight.shape[0]
    rows = packed.shape[0]
    return pl.pallas_call(
        first_load_kernel,
        in_specs=[IN_SMEM, IN_VMEM, IN_HBM],
        out_specs=[IN_VMEM] * 3,
        out_shape=[
            jax.ShapeDtypeStruct((width, columns), weight.dtype),
            jax.ShapeDtypeStruct((rows, width), jnp.bfloat16),
            jax.ShapeDtypeStruct((rows, columns), jnp.bfloat16),
        ],
        scratch_shapes=[pltpu.VMEM(packed.shape, jnp.float32), pltpu.SemaphoreType.DMA((LOAD_PARTS,))],
        compiler_params=params(),
        cost_estimate=cost(1 << 20),
        name="first_load",
    )(first, packed, in_hbm(weight))


def second_load_kernel(blocks, column0, first_ref, *refs):
    packed, (table1_ref, earlier_ref, weight_hbm) = refs[:blocks], refs[blocks : blocks + 3]
    outs = refs[blocks + 3 : -2]
    weight_ref, own_a_ref, own_b_ref, out_ref = outs[:4]
    tables = outs[4:]
    keys_ref, sems = refs[-2:]

    def meanwhile():
        for packed_ref, table_ref in zip(packed, tables):
            build_table(first_ref[0], packed_ref, table_ref, keys_ref)

        def write(at, product):
            own_a_ref[:, at] = product

        multiply(tables[0], earlier_ref, write)

    total = load_and_multiply(weight_hbm, column0, weight_ref, sems, meanwhile, [tables[0], table1_ref])
    rows = table1_ref.shape[0]
    own_b_ref[...] = total[:rows, :]
    out_ref[...] = total[rows:, :].astype(out_ref.dtype)


def second_load(first, packed, table1, earlier, weight):
    width, columns = earlier.shape
    rows = table1.shape[0]
    blocks = len(packed)
    wide = jax.ShapeDtypeStruct((rows, columns), jnp.float32)
    shapes = [jax.ShapeDtypeStruct((width, columns), weight.dtype), wide, wide]
    shapes += [jax.ShapeDtypeStruct((rows, columns), jnp.bfloat16)] + [table1] * blocks
    return pl.pallas_call(
        functools.partial(second_load_kernel, blocks, columns),
        in_specs=[IN_SMEM] + [IN_VMEM] * (blocks + 2) + [IN_HBM],
        out_specs=[IN_VMEM] * len(shapes),
        out_shape=[jax.ShapeDtypeStruct(x.shape, x.dtype) for x in shapes],
        scratch_shapes=[pltpu.VMEM(packed[0].shape, jnp.float32), pltpu.SemaphoreType.DMA((LOAD_PARTS,))],
        compiler_params=params(),
        cost_estimate=cost(1 << 20),
        name="second_load",
    )(first, *packed, table1, earlier, in_hbm(weight))


def partial_kernel(table_ref, weight_ref, arrived_ref, out_ref):
    def write(at, product):
        out_ref[:, at] = (product + arrived_ref[:, at].astype(jnp.float32)).astype(out_ref.dtype)

    multiply(table_ref, weight_ref, write)


def partial_sum(table, weight, arrived):
    return pl.pallas_call(
        partial_kernel,
        in_specs=[IN_VMEM] * 3,
        out_specs=IN_VMEM,
        out_shape=jax.ShapeDtypeStruct(arrived.shape, jnp.bfloat16),
        compiler_params=params(),
        cost_estimate=cost(1 << 20),
        name="partial_sum",
    )(table, weight, arrived)


def error_kernel(column0, arrived_ref, own_ref, bias_ref, tokens_ref, out_ref):
    part = slice(column0, column0 + out_ref.shape[1])
    total = arrived_ref[...].astype(jnp.float32) + own_ref[...] + bias_ref[:, part]
    out_ref[...] = (total - tokens_ref[:, part].astype(jnp.float32)).astype(out_ref.dtype)


def token_errors(column0, arrived, own_sum, bias, tokens):
    return pl.pallas_call(
        functools.partial(error_kernel, column0),
        in_specs=[IN_VMEM] * 4,
        out_specs=IN_VMEM,
        out_shape=jax.ShapeDtypeStruct(arrived.shape, jnp.bfloat16),
        compiler_params=params(),
        cost_estimate=cost(1 << 20),
        name="token_errors",
    )(arrived, own_sum, bias, tokens)


def grad_kernel(blocks, column0, tile, *refs):
    tables, errors = refs[:blocks], refs[blocks : 2 * blocks]
    error_out, grad_out, all_ref, made_ref, sems = refs[-5:]
    rows, columns = errors[0].shape
    width = tables[0].shape[1]
    at = pl.ds(column0, columns)
    copies = [pltpu.make_async_copy(errors[0], error_out.at[:, at], sems.at[width // tile])]
    copies[0].start()
    for b in range(blocks):
        all_ref[b * rows : (b + 1) * rows, :] = errors[b][...]
    for i, l in enumerate(range(0, width, tile)):
        table = jnp.concatenate([table_ref[:, l : l + tile] for table_ref in tables], axis=0)
        product = lax.dot_general(table, all_ref[...], (((0,), (0,)), ((), ())), preferred_element_type=jnp.float32)
        made_ref[l : l + tile, :] = product.astype(made_ref.dtype)
        copy = pltpu.make_async_copy(made_ref.at[pl.ds(l, tile), :], grad_out.at[pl.ds(l, tile), at], sems.at[i])
        copy.start()
        copies.append(copy)
    for copy in copies:
        copy.wait()


def grad_part(tables, errors, features, column0, previous, tile=256):
    width = tables[0].shape[1]
    rows, columns = errors[0].shape
    blocks = len(errors)
    in_specs = [IN_VMEM] * (2 * blocks)
    operands = [*tables, *errors]
    aliases = {}
    if previous is not None:
        aliases = {len(operands): 0, len(operands) + 1: 1}
        in_specs += [IN_HBM, IN_HBM]
        operands += previous
    return pl.pallas_call(
        functools.partial(grad_kernel, blocks, column0, tile),
        in_specs=in_specs,
        out_specs=[IN_HBM, IN_HBM],
        out_shape=[
            jax.ShapeDtypeStruct((rows, features), jnp.bfloat16),
            jax.ShapeDtypeStruct((width, features), jnp.bfloat16),
        ],
        scratch_shapes=[
            pltpu.VMEM((blocks * rows, columns), jnp.bfloat16),
            pltpu.VMEM((width, columns), jnp.bfloat16),
            pltpu.SemaphoreType.DMA((width // tile + 1,)),
        ],
        input_output_aliases=aliases,
        compiler_params=params(),
        cost_estimate=cost(1 << 20),
        name="grad",
    )(*operands)


def local(count, tokens, active_latent_index, latent_values, dec_bias, dec_weight):
    width, features = dec_weight.shape
    columns = features // CHAINS
    starts = [c * columns for c in range(CHAINS)]
    first = (lax.axis_index("latent") * width).astype(jnp.int32).reshape(1)
    def send(x, step=1):
        return lax.ppermute(x, "latent", ring_shift(count, step))

    own = pack(active_latent_index, latent_values)
    packed = [own] + [send(own, k) for k in range(1, count)]
    weight_a, table1, sent_a = first_load(first, packed[1], dec_weight, columns)
    made = second_load(first, packed[:1] + packed[2:], table1, weight_a, dec_weight)
    weights, own_sums, running = [weight_a, made[0]], made[1:3], [sent_a, made[3]]
    tables = [made[4], table1, *made[5:]]
    for k in range(2, count):
        for c in range(CHAINS):
            running[c] = partial_sum(tables[k], weights[c], send(running[c]))
    bias = dec_bias.reshape(1, features)
    errors = [[token_errors(at, send(running[c]), own_sums[c], bias, tokens)] for c, at in enumerate(starts)]
    for step in range(1, count):
        for c in range(CHAINS):
            errors[c].append(send(errors[c][-1]))
    made = None
    for c, at in enumerate(starts):
        made = grad_part(tables, errors[c], features, at, made)
    return tuple(made)


def solution(mesh):
    in_specs = (
        P(("groups", "latent"), ("dp", "mp")),
        P(("groups", "latent"), None),
        P(("groups", "latent"), None),
        P(("groups", "dp", "mp")),
        P(("groups", "latent"), ("dp", "mp")),
    )
    out_specs = (P(("groups", "latent"), ("dp", "mp")), P(("groups", "latent"), ("dp", "mp")))
    body = functools.partial(local, mesh.shape["latent"])
    return jax.shard_map(body, mesh=mesh, in_specs=in_specs, out_specs=out_specs, check_vma=False)
```

time: 77.1 us -> 71.5 us (0.927)
  starting transfers between devices: 10.1 us -> 27.6 us
  waiting for transfers between devices: 39 us -> 25.2 us
  local copies, waits for them, and re-layouts: 7.65 us -> 0.01 us
  other arithmetic: 2.77 us -> 0 us
  Pallas kernels: 16.3 us -> 17.8 us
    ppermute x15, starting transfers between devices: 10.1 us -> 27.6 us  [send(): return lax.ppermute(x, 'latent', ring_shift(count, step))]
    ppermute x15, waiting for transfers between devices: 39 us -> 25.2 us  [send(): return lax.ppermute(x, 'latent', ring_shift(count, step))]
    unnamed x12 -> x4, local copies, waits for them, and re-layouts: 5.82 us -> 0.01 us
    pallas_call x8 -> x7, Pallas kernels: 6.9 us -> 11.1 us  [the longest x1 4.48 us: second_load(): pl.pallas_call(functools.partial(second_load_kernel, blocks, columns), in...]
    transpose x1 -> x0, other arithmetic: 2 us -> none  [local(): table_t = jnp.concatenate(tables, axis=0).T]
    pallas_call x4 -> x0, local copies, waits for them, and re-layouts: 1.84 us -> none  [build(): pl.pallas_call(functools.partial(build_kernel, blocks, column0), in_specs...]
    pallas_call x2, Pallas kernels: 1.67 us -> 0.17 us  [token_errors(): pl.pallas_call(functools.partial(error_kernel, column0), in_specs=[IN_VME...]
    pallas_call x2, Pallas kernels: 7.73 us -> 6.52 us  [grad_part(): pl.pallas_call(functools.partial(grad_kernel, blocks, column0, tile), in_...]
  transfers between devices with their start and end apart: 15 -> 15, of which waited for: 14 -> 11; matrix products, arithmetic and copies ran while one was open for 6% -> 0% of each run, Pallas kernels for 14% -> 19%
where the time goes in v3:
time: 71.5 us; the launch traced here: 71.3 us
  starting transfers between devices  27.6 us (39%)
  waiting for transfers between devices  25.2 us (35%)
  Pallas kernels  17.8 us (25%)
    ppermute x15, starting transfers between devices, send(): return lax.ppermute(x, 'latent', ring_shift(count, step))  27.6 us
    ppermute x15, waiting for transfers between devices, send(): return lax.ppermute(x, 'latent', ring_shift(count, step))  25.2 us
    pallas_call x2, Pallas kernels, grad_part(): pl.pallas_call(functools.partial(grad_kernel, blocks, column0, tile), in_...  6.52 us
    pallas_call x1, Pallas kernels, second_load(): pl.pallas_call(functools.partial(second_load_kernel, blocks, columns), in...  4.48 us
    pallas_call x4, Pallas kernels, partial_sum(): pl.pallas_call(partial_kernel, in_specs=[IN_VMEM] * 3, out_specs=IN_VMEM,...  3.21 us
    pallas_call x1, Pallas kernels, first_load(): pl.pallas_call(first_load_kernel, in_specs=[IN_SMEM, IN_VMEM, IN_HBM], ou...  2.44 us
  transfers between devices with their start and end apart: 15, of which 11 were waited for; matrix products, arithmetic and copies ran while one was open for 0% of the time, Pallas kernels for 19%

profile of v3, /device:TPU:0, one launch (start us, length us, event | category | flops | bytes accessed | tf_op | source)
XLA Modules:
  0.0 71.3 jit_solution(17160987851224797918)
XLA Ops:
  0.6 1.0 %pack.1.refs_0_ = f32[96,128]{1,0:T(8,128)S(1)} custom-call(s32[64,96]{1,0:T(8,128)} %bitcast.6, bf16[64,96]{1,0:T(8,128)(2,1)} %bitcast.7), custom_call_target="tpu_custom_call" | custom-call | bytes 1048576 | tf_op jit(solution)/shard_map/pack/pallas_call | solution.py:61
  1.6 3.1 %collective-permute-start.2 = (f32[96,128]{1,0:T(8,128)S(1)}, f32[96,128]{1,0:T(8,128)S(1)}, u32[]{:S(2)}, u32[]{:S(2)}) collective-permute-start(f32[96,128]{1,0:T(8,128)S(1)} %pack.1.refs_0_), channel_id=1, source_target_pairs={{0,4},{4,12},{12,8},{8,0},{1,5},{5,13},{13,9},{9,1},{2,6},{6,14},{... | collective-permute-start | bytes 147464 | tf_op jit(solution)/shard_map/ppermute | solution.py:313
  4.7 1.1 %collective-permute-start.1 = (f32[96,128]{1,0:T(8,128)S(1)}, f32[96,128]{1,0:T(8,128)S(1)}, u32[]{:S(2)}, u32[]{:S(2)}) collective-permute-start(f32[96,128]{1,0:T(8,128)S(1)} %pack.1.refs_0_), channel_id=1, source_target_pairs={{0,8},{4,0},{12,4},{8,12},{1,9},{5,1},{13,5},{9,13},{2,10},{6,2},{... | collective-permute-start | bytes 147464 | tf_op jit(solution)/shard_map/ppermute | solution.py:313
  5.7 3.9 %collective-permute-start = (f32[96,128]{1,0:T(8,128)S(1)}, f32[96,128]{1,0:T(8,128)S(1)}, u32[]{:S(2)}, u32[]{:S(2)}) collective-permute-start(f32[96,128]{1,0:T(8,128)S(1)} %pack.1.refs_0_), channel_id=1, source_target_pairs={{0,12},{4,8},{12,0},{8,4},{1,13},{5,9},{13,1},{9,5},{2,14},{6,10},... | collective-permute-start | bytes 147464 | tf_op jit(solution)/shard_map/ppermute | solution.py:313
  9.6 0.0 collective-permute-done.2.packed_ref
  9.6 2.4 %first_load.1 = (bf16[2048,1024]{1,0:T(8,128)(2,1)S(1)}, bf16[96,2048]{1,0:T(8,128)(2,1)S(1)}, bf16[96,1024]{1,0:T(8,128)(2,1)S(1)}) custom-call(s32[1]{0:T(128)} %bitcast.first_ref, f32[96,128]{1,0:T(8,128)S(1)} %collective-permute-done.2.packed_ref, bf16[2048,2048]{1,0:T(8,128)(2,1)} %refs_5_.1), custom_call_target="tpu_custom_call" | custom-call | bytes 1048576 | tf_op jit(solution)/shard_map/first_load/pallas_call | solution.py:161
  12.1 0.2 collective-permute-start.9
  12.3 0.0 collective-permute-done.1.refs_2_
  12.3 0.0 collective-permute-done.refs_1_
  12.3 4.5 %second_load.1 = (bf16[2048,1024]{1,0:T(8,128)(2,1)S(1)}, f32[96,1024]{1,0:T(8,128)S(1)}, f32[96,1024]{1,0:T(8,128)S(1)}, bf16[96,1024]{1,0:T(8,128)(2,1)S(1)}, ...) custom-call(s32[1]{0:T(128)} %bitcast.first_ref, ...), custom_call_target="tpu_custom_call" | custom-call | bytes 1048576 | tf_op jit(solution)/shard_map/second_load/pallas_call | solution.py:206
  16.8 3.4 %collective-permute-start.3 = (bf16[96,1024]{1,0:T(8,128)(2,1)S(1)}, bf16[96,1024]{1,0:T(8,128)(2,1)S(1)}, u32[]{:S(2)}, u32[]{:S(2)}) collective-permute-start(bf16[96,1024]{1,0:T(8,128)(2,1)S(1)} %get-tuple-element.20), channel_id=1, source_target_pairs={{0,4},{4,12},{12,8},{8,0},{1,5},{5,13},{13,9},{9,1},{2,6},{6,14},{... | collective-permute-start | bytes 589832 | tf_op jit(solution)/shard_map/ppermute | solution.py:313
  20.2 0.0 collective-permute-done.9.arrived_ref
  20.2 0.8 %partial_sum.6 = bf16[96,1024]{1,0:T(8,128)(2,1)S(1)} custom-call(bf16[96,2048]{1,0:T(8,128)(2,1)S(1)} %get-tuple-element.17.table_ref.refs_2_, bf16[2048,1024]{1,0:T(8,128)(2,1)S(1)} %get-tuple-element.15.refs_4_.weight_ref, bf16[96,1024]{1,0:T(8,128)(2,1)S(1)} %collective-permute-done.9.arrived_ref), custom_call_target="tpu_custom_call" | custom-call | bytes 1048576 | tf_op jit(solution)/shard_map/partial_sum/pallas_call | solution.py:226
  21.0 0.0 copy-start
  21.0 0.0 copy-start.1
  21.1 0.4 collective-permute-start.10
  21.5 4.1 %collective-permute-done.3.arrived_ref = bf16[96,1024]{1,0:T(8,128)(2,1)S(1)} collective-permute-done((bf16[96,1024]{1,0:T(8,128)(2,1)S(1)}, bf16[96,1024]{1,0:T(8,128)(2,1)S(1)}, u32[]{:S(2)}, u32[]{:S(2)}) %collective-permute-start.3) | collective-permute-done | bytes 196640 | tf_op jit(solution)/shard_map/ppermute | solution.py:313
  25.6 0.8 %partial_sum.4 = bf16[96,1024]{1,0:T(8,128)(2,1)S(1)} custom-call(bf16[96,2048]{1,0:T(8,128)(2,1)S(1)} %get-tuple-element.17.table_ref.refs_2_, bf16[2048,1024]{1,0:T(8,128)(2,1)S(1)} %get-tuple-element.19.weight_ref, bf16[96,1024]{1,0:T(8,128)(2,1)S(1)} %collective-permute-done.3.arrived_ref), custom_call_target="tpu_custom_call" | custom-call | bytes 1048576 | tf_op jit(solution)/shard_map/partial_sum/pallas_call | solution.py:226
  26.4 2.5 %collective-permute-start.4 = (bf16[96,1024]{1,0:T(8,128)(2,1)S(1)}, bf16[96,1024]{1,0:T(8,128)(2,1)S(1)}, u32[]{:S(2)}, u32[]{:S(2)}) collective-permute-start(bf16[96,1024]{1,0:T(8,128)(2,1)S(1)} %partial_sum.4), channel_id=1, source_target_pairs={{0,4},{4,12},{12,8},{8,0},{1,5},{5,13},{13,9},{9,1},{2,6},{6,14},{... | collective-permute-start | bytes 589832 | tf_op jit(solution)/shard_map/ppermute | solution.py:313
  28.9 0.9 %collective-permute-done.10.arrived_ref = bf16[96,1024]{1,0:T(8,128)(2,1)S(1)} collective-permute-done((bf16[96,1024]{1,0:T(8,128)(2,1)S(1)}, bf16[96,1024]{1,0:T(8,128)(2,1)S(1)}, u32[]{:S(2)}, u32[]{:S(2)}) %collective-permute-start.10) | collective-permute-done | bytes 196640 | tf_op jit(solution)/shard_map/ppermute | solution.py:313
  29.8 0.8 %partial_sum.7 = bf16[96,1024]{1,0:T(8,128)(2,1)S(1)} custom-call(bf16[96,2048]{1,0:T(8,128)(2,1)S(1)} %get-tuple-element.18.table_ref.refs_3_, bf16[2048,1024]{1,0:T(8,128)(2,1)S(1)} %get-tuple-element.15.refs_4_.weight_ref, bf16[96,1024]{1,0:T(8,128)(2,1)S(1)} %collective-permute-done.10.arrived_ref), custom_call_target="tpu_custom_call" | custom-call | bytes 1048576 | tf_op jit(solution)/shard_map/partial_sum/pallas_call | solution.py:226
  30.6 2.5 %collective-permute-start.11 = (bf16[96,1024]{1,0:T(8,128)(2,1)S(1)}, bf16[96,1024]{1,0:T(8,128)(2,1)S(1)}, u32[]{:S(2)}, u32[]{:S(2)}) collective-permute-start(bf16[96,1024]{1,0:T(8,128)(2,1)S(1)} %partial_sum.7), channel_id=1, source_target_pairs={{0,4},{4,12},{12,8},{8,0},{1,5},{5,13},{13,9},{9,1},{2,6},{6,14},{... | collective-permute-start | bytes 589832 | tf_op jit(solution)/shard_map/ppermute | solution.py:313
  33.1 1.1 %collective-permute-done.4.arrived_ref = bf16[96,1024]{1,0:T(8,128)(2,1)S(1)} collective-permute-done((bf16[96,1024]{1,0:T(8,128)(2,1)S(1)}, bf16[96,1024]{1,0:T(8,128)(2,1)S(1)}, u32[]{:S(2)}, u32[]{:S(2)}) %collective-permute-start.4) | collective-permute-done | bytes 196640 | tf_op jit(solution)/shard_map/ppermute | solution.py:313
  34.3 0.8 %partial_sum.5 = bf16[96,1024]{1,0:T(8,128)(2,1)S(1)} custom-call(bf16[96,2048]{1,0:T(8,128)(2,1)S(1)} %get-tuple-element.18.table_ref.refs_3_, bf16[2048,1024]{1,0:T(8,128)(2,1)S(1)} %get-tuple-element.19.weight_ref, bf16[96,1024]{1,0:T(8,128)(2,1)S(1)} %collective-permute-done.4.arrived_ref), custom_call_target="tpu_custom_call" | custom-call | bytes 1048576 | tf_op jit(solution)/shard_map/partial_sum/pallas_call | solution.py:226
  35.1 2.5 %collective-permute-start.5 = (bf16[96,1024]{1,0:T(8,128)(2,1)S(1)}, bf16[96,1024]{1,0:T(8,128)(2,1)S(1)}, u32[]{:S(2)}, u32[]{:S(2)}) collective-permute-start(bf16[96,1024]{1,0:T(8,128)(2,1)S(1)} %partial_sum.5), channel_id=1, source_target_pairs={{0,4},{4,12},{12,8},{8,0},{1,5},{5,13},{13,9},{9,1},{2,6},{6,14},{... | collective-permute-start | bytes 589832 | tf_op jit(solution)/shard_map/ppermute | solution.py:313
  37.6 1.7 %collective-permute-done.11.arrived_ref = bf16[96,1024]{1,0:T(8,128)(2,1)S(1)} collective-permute-done((bf16[96,1024]{1,0:T(8,128)(2,1)S(1)}, bf16[96,1024]{1,0:T(8,128)(2,1)S(1)}, u32[]{:S(2)}, u32[]{:S(2)}) %collective-permute-start.11) | collective-permute-done | bytes 196640 | tf_op jit(solution)/shard_map/ppermute | solution.py:313
  39.3 0.0 copy-done
  39.3 0.0 copy-done.1
  39.3 0.1 token_errors.3.refs_4_
  39.4 1.7 %collective-permute-start.12 = (bf16[96,1024]{1,0:T(8,128)(2,1)S(1)}, bf16[96,1024]{1,0:T(8,128)(2,1)S(1)}, u32[]{:S(2)}, u32[]{:S(2)}) collective-permute-start(bf16[96,1024]{1,0:T(8,128)(2,1)S(1)} %token_errors.3.refs_4_), channel_id=1, source_target_pairs={{0,4},{4,12},{12,8},{8,0},{1,5},{5,13},{13,9},{9,1},{2,6},{6,14},{... | collective-permute-start | bytes 589832 | tf_op jit(solution)/shard_map/ppermute | solution.py:313
  41.1 2.8 %collective-permute-done.5.arrived_ref = bf16[96,1024]{1,0:T(8,128)(2,1)S(1)} collective-permute-done((bf16[96,1024]{1,0:T(8,128)(2,1)S(1)}, bf16[96,1024]{1,0:T(8,128)(2,1)S(1)}, u32[]{:S(2)}, u32[]{:S(2)}) %collective-permute-start.5) | collective-permute-done | bytes 196640 | tf_op jit(solution)/shard_map/ppermute | solution.py:313
  43.9 0.1 token_errors.2.refs_4_
  44.0 1.6 %collective-permute-start.6 = (bf16[96,1024]{1,0:T(8,128)(2,1)S(1)}, bf16[96,1024]{1,0:T(8,128)(2,1)S(1)}, u32[]{:S(2)}, u32[]{:S(2)}) collective-permute-start(bf16[96,1024]{1,0:T(8,128)(2,1)S(1)} %token_errors.2.refs_4_), channel_id=1, source_target_pairs={{0,4},{4,12},{12,8},{8,0},{1,5},{5,13},{13,9},{9,1},{2,6},{6,14},{... | collective-permute-start | bytes 589832 | tf_op jit(solution)/shard_map/ppermute | solution.py:313
  45.6 2.6 %collective-permute-done.12.refs_5_ = bf16[96,1024]{1,0:T(8,128)(2,1)S(1)} collective-permute-done((bf16[96,1024]{1,0:T(8,128)(2,1)S(1)}, bf16[96,1024]{1,0:T(8,128)(2,1)S(1)}, u32[]{:S(2)}, u32[]{:S(2)}) %collective-permute-start.12) | collective-permute-done | bytes 196640 | tf_op jit(solution)/shard_map/ppermute | solution.py:313
  48.2 1.5 %collective-permute-start.13 = (bf16[96,1024]{1,0:T(8,128)(2,1)S(1)}, bf16[96,1024]{1,0:T(8,128)(2,1)S(1)}, u32[]{:S(2)}, u32[]{:S(2)}) collective-permute-start(bf16[96,1024]{1,0:T(8,128)(2,1)S(1)} %collective-permute-done.12.refs_5_), channel_id=1, source_target_pairs={{0,4},{4,12},{12,8},{8,0},{1,5},{5,13},{13,9},{9,1},{2,6},{6,14},{... | collective-permute-start | bytes 589832 | tf_op jit(solution)/shard_map/ppermute | solution.py:313
  49.7 3.1 %collective-permute-done.6.refs_5_ = bf16[96,1024]{1,0:T(8,128)(2,1)S(1)} collective-permute-done((bf16[96,1024]{1,0:T(8,128)(2,1)S(1)}, bf16[96,1024]{1,0:T(8,128)(2,1)S(1)}, u32[]{:S(2)}, u32[]{:S(2)}) %collective-permute-start.6) | collective-permute-done | bytes 196640 | tf_op jit(solution)/shard_map/ppermute | solution.py:313
  52.8 1.1 %collective-permute-start.7 = (bf16[96,1024]{1,0:T(8,128)(2,1)S(1)}, bf16[96,1024]{1,0:T(8,128)(2,1)S(1)}, u32[]{:S(2)}, u32[]{:S(2)}) collective-permute-start(bf16[96,1024]{1,0:T(8,128)(2,1)S(1)} %collective-permute-done.6.refs_5_), channel_id=1, source_target_pairs={{0,4},{4,12},{12,8},{8,0},{1,5},{5,13},{13,9},{9,1},{2,6},{6,14},{... | collective-permute-start | bytes 589832 | tf_op jit(solution)/shard_map/ppermute | solution.py:313
  53.9 3.1 %collective-permute-done.13.refs_6_ = bf16[96,1024]{1,0:T(8,128)(2,1)S(1)} collective-permute-done((bf16[96,1024]{1,0:T(8,128)(2,1)S(1)}, bf16[96,1024]{1,0:T(8,128)(2,1)S(1)}, u32[]{:S(2)}, u32[]{:S(2)}) %collective-permute-start.13) | collective-permute-done | bytes 196640 | tf_op jit(solution)/shard_map/ppermute | solution.py:313
  57.0 1.1 %collective-permute-start.14 = (bf16[96,1024]{1,0:T(8,128)(2,1)S(1)}, bf16[96,1024]{1,0:T(8,128)(2,1)S(1)}, u32[]{:S(2)}, u32[]{:S(2)}) collective-permute-start(bf16[96,1024]{1,0:T(8,128)(2,1)S(1)} %collective-permute-done.13.refs_6_), channel_id=1, source_target_pairs={{0,4},{4,12},{12,8},{8,0},{1,5},{5,13},{13,9},{9,1},{2,6},{6,14},{... | collective-permute-start | bytes 589832 | tf_op jit(solution)/shard_map/ppermute | solution.py:313
  58.1 3.4 %collective-permute-done.7.refs_6_ = bf16[96,1024]{1,0:T(8,128)(2,1)S(1)} collective-permute-done((bf16[96,1024]{1,0:T(8,128)(2,1)S(1)}, bf16[96,1024]{1,0:T(8,128)(2,1)S(1)}, u32[]{:S(2)}, u32[]{:S(2)}) %collective-permute-start.7) | collective-permute-done | bytes 196640 | tf_op jit(solution)/shard_map/ppermute | solution.py:313
  61.5 0.8 %collective-permute-start.8 = (bf16[96,1024]{1,0:T(8,128)(2,1)S(1)}, bf16[96,1024]{1,0:T(8,128)(2,1)S(1)}, u32[]{:S(2)}, u32[]{:S(2)}) collective-permute-start(bf16[96,1024]{1,0:T(8,128)(2,1)S(1)} %collective-permute-done.7.refs_6_), channel_id=1, source_target_pairs={{0,4},{4,12},{12,8},{8,0},{1,5},{5,13},{13,9},{9,1},{2,6},{6,14},{... | collective-permute-start | bytes 589832 | tf_op jit(solution)/shard_map/ppermute | solution.py:313
  62.3 1.3 %collective-permute-done.14.refs_7_ = bf16[96,1024]{1,0:T(8,128)(2,1)S(1)} collective-permute-done((bf16[96,1024]{1,0:T(8,128)(2,1)S(1)}, bf16[96,1024]{1,0:T(8,128)(2,1)S(1)}, u32[]{:S(2)}, u32[]{:S(2)}) %collective-permute-start.14) | collective-permute-done | bytes 196640 | tf_op jit(solution)/shard_map/ppermute | solution.py:313
  63.6 3.3 %grad.2 = (bf16[96,2048]{1,0:T(8,128)(2,1)}, bf16[2048,2048]{1,0:T(8,128)(2,1)}) custom-call(bf16[96,2048]{1,0:T(8,128)(2,1)S(1)} %get-tuple-element.16.refs_0_, bf16[96,2048]{1,0:T(8,128)(2,1)S(1)} %get-tuple-element.14.refs_3_.refs_1_, bf16[96,2048]{1,0:T(8,128)(2,1)S(1)} %get-tuple-element.17.table_ref.refs_2_, ...), custom_call_target="tpu_custom_call" | custom-call | bytes 1048576 | tf_op jit(solution)/shard_map/grad/pallas_call | solution.py:287
  66.8 1.2 %collective-permute-done.8.refs_7_ = bf16[96,1024]{1,0:T(8,128)(2,1)S(1)} collective-permute-done((bf16[96,1024]{1,0:T(8,128)(2,1)S(1)}, bf16[96,1024]{1,0:T(8,128)(2,1)S(1)}, u32[]{:S(2)}, u32[]{:S(2)}) %collective-permute-start.8) | collective-permute-done | bytes 196640 | tf_op jit(solution)/shard_map/ppermute | solution.py:313
  68.0 3.3 %grad.3 = (bf16[96,2048]{1,0:T(8,128)(2,1)}, bf16[2048,2048]{1,0:T(8,128)(2,1)}) custom-call(bf16[96,2048]{1,0:T(8,128)(2,1)S(1)} %get-tuple-element.16.refs_0_, bf16[96,2048]{1,0:T(8,128)(2,1)S(1)} %get-tuple-element.14.refs_3_.refs_1_, bf16[96,2048]{1,0:T(8,128)(2,1)S(1)} %get-tuple-element.17.table_ref.refs_2_, ...), custom_call_target="tpu_custom_call", output_to_operand_aliasing={{0}: (8, {}), {1}: (9, {})} | custom-call | bytes 1048576 | tf_op jit(solution)/shard_map/grad/pallas_call | solution.py:287
Async XLA Ops:
  1.6 8.0 %collective-permute-start.2 = (f32[96,128]{1,0:T(8,128)S(1)}, f32[96,128]{1,0:T(8,128)S(1)}, u32[]{:S(2)}, u32[]{:S(2)}) collective-permute-start(f32[96,128]{1,0:T(8,128)S(1)} %pack.1.refs_0_), channel_id=1, source_target_pairs={{0,4},{4,12},{12,8},{8,0},{1,5},{5,13},{13,9},{9,1},{2,6},{6,14},{... | collective-permute-start | bytes 147464 | tf_op jit(solution)/shard_map/ppermute | solution.py:313
  4.7 7.6 %collective-permute-start.1 = (f32[96,128]{1,0:T(8,128)S(1)}, f32[96,128]{1,0:T(8,128)S(1)}, u32[]{:S(2)}, u32[]{:S(2)}) collective-permute-start(f32[96,128]{1,0:T(8,128)S(1)} %pack.1.refs_0_), channel_id=1, source_target_pairs={{0,8},{4,0},{12,4},{8,12},{1,9},{5,1},{13,5},{9,13},{2,10},{6,2},{... | collective-permute-start | bytes 147464 | tf_op jit(solution)/shard_map/ppermute | solution.py:313
  5.7 6.6 %collective-permute-start = (f32[96,128]{1,0:T(8,128)S(1)}, f32[96,128]{1,0:T(8,128)S(1)}, u32[]{:S(2)}, u32[]{:S(2)}) collective-permute-start(f32[96,128]{1,0:T(8,128)S(1)} %pack.1.refs_0_), channel_id=1, source_target_pairs={{0,12},{4,8},{12,0},{8,4},{1,13},{5,9},{13,1},{9,5},{2,14},{6,10},... | collective-permute-start | bytes 147464 | tf_op jit(solution)/shard_map/ppermute | solution.py:313
  12.1 8.2 %collective-permute-start.9 = (bf16[96,1024]{1,0:T(8,128)(2,1)S(1)}, bf16[96,1024]{1,0:T(8,128)(2,1)S(1)}, u32[]{:S(2)}, u32[]{:S(2)}) collective-permute-start(bf16[96,1024]{1,0:T(8,128)(2,1)S(1)} %get-tuple-element.22), channel_id=1, source_target_pairs={{0,4},{4,12},{12,8},{8,0},{1,5},{5,13},{13,9},{9,1},{2,6},{6,14},{... | collective-permute-start | bytes 589832 | tf_op jit(solution)/shard_map/ppermute | solution.py:313
  16.8 8.8 %collective-permute-start.3 = (bf16[96,1024]{1,0:T(8,128)(2,1)S(1)}, bf16[96,1024]{1,0:T(8,128)(2,1)S(1)}, u32[]{:S(2)}, u32[]{:S(2)}) collective-permute-start(bf16[96,1024]{1,0:T(8,128)(2,1)S(1)} %get-tuple-element.20), channel_id=1, source_target_pairs={{0,4},{4,12},{12,8},{8,0},{1,5},{5,13},{13,9},{9,1},{2,6},{6,14},{... | collective-permute-start | bytes 589832 | tf_op jit(solution)/shard_map/ppermute | solution.py:313
  21.0 18.3 %copy-start = (bf16[96,2048]{1,0:T(8,128)(2,1)S(1)}, bf16[96,2048]{1,0:T(8,128)(2,1)}, u32[]{:S(2)}) copy-start(bf16[96,2048]{1,0:T(8,128)(2,1)} %tokens_ref.3) | copy-start | bytes 1179652
  21.0 18.3 %copy-start.1 = (f32[2048]{0:T(1024)S(1)}, f32[2048]{0:T(1024)}, u32[]{:S(2)}) copy-start(f32[2048]{0:T(1024)} %param.8) | copy-start | bytes 24580
  21.1 8.7 %collective-permute-start.10 = (bf16[96,1024]{1,0:T(8,128)(2,1)S(1)}, bf16[96,1024]{1,0:T(8,128)(2,1)S(1)}, u32[]{:S(2)}, u32[]{:S(2)}) collective-permute-start(bf16[96,1024]{1,0:T(8,128)(2,1)S(1)} %partial_sum.6), channel_id=1, source_target_pairs={{0,4},{4,12},{12,8},{8,0},{1,5},{5,13},{13,9},{9,1},{2,6},{6,14},{... | collective-permute-start | bytes 589832 | tf_op jit(solution)/shard_map/ppermute | solution.py:313
  26.4 7.9 %collective-permute-start.4 = (bf16[96,1024]{1,0:T(8,128)(2,1)S(1)}, bf16[96,1024]{1,0:T(8,128)(2,1)S(1)}, u32[]{:S(2)}, u32[]{:S(2)}) collective-permute-start(bf16[96,1024]{1,0:T(8,128)(2,1)S(1)} %partial_sum.4), channel_id=1, source_target_pairs={{0,4},{4,12},{12,8},{8,0},{1,5},{5,13},{13,9},{9,1},{2,6},{6,14},{... | collective-permute-start | bytes 589832 | tf_op jit(solution)/shard_map/ppermute | solution.py:313
  30.6 8.7 %collective-permute-start.11 = (bf16[96,1024]{1,0:T(8,128)(2,1)S(1)}, bf16[96,1024]{1,0:T(8,128)(2,1)S(1)}, u32[]{:S(2)}, u32[]{:S(2)}) collective-permute-start(bf16[96,1024]{1,0:T(8,128)(2,1)S(1)} %partial_sum.7), channel_id=1, source_target_pairs={{0,4},{4,12},{12,8},{8,0},{1,5},{5,13},{13,9},{9,1},{2,6},{6,14},{... | collective-permute-start | bytes 589832 | tf_op jit(solution)/shard_map/ppermute | solution.py:313
  35.1 8.8 %collective-permute-start.5 = (bf16[96,1024]{1,0:T(8,128)(2,1)S(1)}, bf16[96,1024]{1,0:T(8,128)(2,1)S(1)}, u32[]{:S(2)}, u32[]{:S(2)}) collective-permute-start(bf16[96,1024]{1,0:T(8,128)(2,1)S(1)} %partial_sum.5), channel_id=1, source_target_pairs={{0,4},{4,12},{12,8},{8,0},{1,5},{5,13},{13,9},{9,1},{2,6},{6,14},{... | collective-permute-start | bytes 589832 | tf_op jit(solution)/shard_map/ppermute | solution.py:313
  39.4 8.8 %collective-permute-start.12 = (bf16[96,1024]{1,0:T(8,128)(2,1)S(1)}, bf16[96,1024]{1,0:T(8,128)(2,1)S(1)}, u32[]{:S(2)}, u32[]{:S(2)}) collective-permute-start(bf16[96,1024]{1,0:T(8,128)(2,1)S(1)} %token_errors.3.refs_4_), channel_id=1, source_target_pairs={{0,4},{4,12},{12,8},{8,0},{1,5},{5,13},{13,9},{9,1},{2,6},{6,14},{... | collective-permute-start | bytes 589832 | tf_op jit(solution)/shard_map/ppermute | solution.py:313
  44.0 8.8 %collective-permute-start.6 = (bf16[96,1024]{1,0:T(8,128)(2,1)S(1)}, bf16[96,1024]{1,0:T(8,128)(2,1)S(1)}, u32[]{:S(2)}, u32[]{:S(2)}) collective-permute-start(bf16[96,1024]{1,0:T(8,128)(2,1)S(1)} %token_errors.2.refs_4_), channel_id=1, source_target_pairs={{0,4},{4,12},{12,8},{8,0},{1,5},{5,13},{13,9},{9,1},{2,6},{6,14},{... | collective-permute-start | bytes 589832 | tf_op jit(solution)/shard_map/ppermute | solution.py:313
  48.2 8.8 %collective-permute-start.13 = (bf16[96,1024]{1,0:T(8,128)(2,1)S(1)}, bf16[96,1024]{1,0:T(8,128)(2,1)S(1)}, u32[]{:S(2)}, u32[]{:S(2)}) collective-permute-start(bf16[96,1024]{1,0:T(8,128)(2,1)S(1)} %collective-permute-done.12.refs_5_), channel_id=1, source_target_pairs={{0,4},{4,12},{12,8},{8,0},{1,5},{5,13},{13,9},{9,1},{2,6},{6,14},{... | collective-permute-start | bytes 589832 | tf_op jit(solution)/shard_map/ppermute | solution.py:313
  52.8 8.7 %collective-permute-start.7 = (bf16[96,1024]{1,0:T(8,128)(2,1)S(1)}, bf16[96,1024]{1,0:T(8,128)(2,1)S(1)}, u32[]{:S(2)}, u32[]{:S(2)}) collective-permute-start(bf16[96,1024]{1,0:T(8,128)(2,1)S(1)} %collective-permute-done.6.refs_5_), channel_id=1, source_target_pairs={{0,4},{4,12},{12,8},{8,0},{1,5},{5,13},{13,9},{9,1},{2,6},{6,14},{... | collective-permute-start | bytes 589832 | tf_op jit(solution)/shard_map/ppermute | solution.py:313
  57.0 6.6 %collective-permute-start.14 = (bf16[96,1024]{1,0:T(8,128)(2,1)S(1)}, bf16[96,1024]{1,0:T(8,128)(2,1)S(1)}, u32[]{:S(2)}, u32[]{:S(2)}) collective-permute-start(bf16[96,1024]{1,0:T(8,128)(2,1)S(1)} %collective-permute-done.13.refs_6_), channel_id=1, source_target_pairs={{0,4},{4,12},{12,8},{8,0},{1,5},{5,13},{13,9},{9,1},{2,6},{6,14},{... | collective-permute-start | bytes 589832 | tf_op jit(solution)/shard_map/ppermute | solution.py:313
  61.5 6.6 %collective-permute-start.8 = (bf16[96,1024]{1,0:T(8,128)(2,1)S(1)}, bf16[96,1024]{1,0:T(8,128)(2,1)S(1)}, u32[]{:S(2)}, u32[]{:S(2)}) collective-permute-start(bf16[96,1024]{1,0:T(8,128)(2,1)S(1)} %collective-permute-done.7.refs_6_), channel_id=1, source_target_pairs={{0,4},{4,12},{12,8},{8,0},{1,5},{5,13},{13,9},{9,1},{2,6},{6,14},{... | collective-permute-start | bytes 589832 | tf_op jit(solution)/shard_map/ppermute | solution.py:313

commit v4 on v3

v4 whole, which is shorter than its diff:
```python
import functools

import jax
import jax.numpy as jnp
from jax import lax
from jax.experimental import pallas as pl
from jax.experimental.pallas import tpu as pltpu
from jax.sharding import PartitionSpec as P

LANES = 128
EXPONENT_BITS = (1, 2, 4, 8, 16, 32, 64)
GROUP = 8
TILE = 512
LOAD_PARTS = 8
VMEM_LIMIT = 24 * 1024 * 1024
IN_VMEM = pl.BlockSpec(memory_space=pltpu.VMEM)
IN_SMEM = pl.BlockSpec(memory_space=pltpu.SMEM)
IN_HBM = pl.BlockSpec(memory_space=pltpu.HBM)


def params():
    return pltpu.CompilerParams(vmem_limit_bytes=VMEM_LIMIT)


def in_hbm(array):
    return pltpu.with_memory_space_constraint(array, pltpu.HBM)


def cost(byte_count):
    return pl.CostEstimate(flops=0, bytes_accessed=byte_count, transcendentals=0)


def ring_order(count):
    return [0] + list(range(1, count, 2)) + list(range(count - 2 + count % 2, 0, -2))


def ring_next(count):
    order = ring_order(count)
    return [(order[i], order[(i + 1) % count]) for i in range(count)]


def pack(ids, values, wide_ref):
    active, rows = ids.shape
    high = lax.shift_right_logical(ids, 7)
    low = jnp.bitwise_and(ids, LANES - 1)
    coded = 1.0 + low.astype(jnp.float32) * (1.0 / LANES)
    for bit in EXPONENT_BITS:
        coded = jnp.where(jnp.bitwise_and(high, bit) != 0, coded * 2.0**bit, coded)
    coded = jnp.where(high >= LANES, -coded, coded)
    wide_ref[0:rows, :] = coded.T
    wide_ref[rows:, :] = values.astype(jnp.float32).T
    even = wide_ref[pl.ds(0, rows, stride=2), :]
    odd = wide_ref[pl.ds(1, rows, stride=2), :]
    return jnp.concatenate([even, odd], axis=1)


def unpack_ids(coded):
    rest = jnp.abs(coded)
    high = jnp.where(coded < 0, LANES, 0)
    for bit in reversed(EXPONENT_BITS):
        over = rest >= 2.0**bit
        rest = jnp.where(over, rest * 2.0**-bit, rest)
        high = high + jnp.where(over, bit, 0)
    return high, ((rest - 1.0) * LANES).astype(jnp.int32)


def build_table(first, packed, table_ref, keys_ref):
    rows, width = table_ref.shape
    half = rows // 2
    per_row = 2
    rows_per_group = GROUP // per_row
    high_count = width // LANES
    high, low = unpack_ids(packed[0:half, :])
    high = high - first
    row = lax.broadcasted_iota(jnp.int32, high.shape, 0)
    lane = lax.broadcasted_iota(jnp.int32, high.shape, 1)
    place = per_row * jnp.bitwise_and(row, rows_per_group - 1) + jnp.where(lane >= LANES // 2, 1, 0)
    inside = jnp.logical_and(high >= 0, high < high_count)
    key = jnp.where(inside, high * GROUP + place, -1)
    keys_ref[0:half, :] = key.astype(jnp.float32)
    keys_ref[half : 2 * half, :] = low.astype(jnp.float32)
    keys_ref[2 * half :, :] = packed[half:, :]
    tall = lax.broadcasted_iota(jnp.int32, (high_count * GROUP, LANES), 0).astype(jnp.float32).astype(jnp.bfloat16)
    wide = lax.broadcasted_iota(jnp.int32, (LANES, LANES), 0).astype(jnp.float32).astype(jnp.bfloat16)
    zero, one = jnp.zeros((), jnp.bfloat16), jnp.ones((), jnp.bfloat16)

    def group_rows(r0):
        left, right = [], []
        for r in range(r0, r0 + rows_per_group):
            key = keys_ref[r : r + 1, :].astype(jnp.bfloat16)
            low = keys_ref[half + r : half + r + 1, :].astype(jnp.bfloat16)
            value = keys_ref[2 * half + r : 2 * half + r + 1, :].astype(jnp.bfloat16)
            left.append(jnp.where(tall == key, value, zero))
            right.append(jnp.where(wide == low, one, zero))
        left = jnp.concatenate(left, axis=1)
        right = jnp.concatenate(right, axis=1)
        product = lax.dot_general(left, right, (((1,), (1,)), ((), ())), preferred_element_type=jnp.float32)
        pieces = [product[h * GROUP : (h + 1) * GROUP, :] for h in range(high_count)]
        return jnp.concatenate(pieces, axis=1)

    for i in range(rows // (2 * GROUP)):
        r0 = i * (2 * rows_per_group)
        both = jnp.concatenate([group_rows(r0), group_rows(r0 + rows_per_group)], axis=0)
        table_ref[i * 2 * GROUP : (i + 1) * 2 * GROUP, :] = both.astype(jnp.bfloat16)


def multiply(table_ref, weight_ref, write):
    columns = weight_ref.shape[1]
    tile = min(TILE, columns)
    for c in range(0, columns, tile):
        at = slice(c, c + tile)
        write(at, jnp.dot(table_ref[...], weight_ref[:, at], preferred_element_type=jnp.float32))


def keys_scratch(rows):
    return pltpu.VMEM((rows + rows // 2, LANES), jnp.float32)


def start_loads(weight_hbm, tokens_hbm, column0, weight_ref, tokens_ref, sems):
    width, columns = weight_ref.shape
    part = width // LOAD_PARTS
    copies = []
    for i in range(LOAD_PARTS):
        rows = pl.ds(i * part, part)
        copies.append(
            pltpu.make_async_copy(weight_hbm.at[rows, pl.ds(column0, columns)], weight_ref.at[rows, :], sems.at[i])
        )
    copies.append(pltpu.make_async_copy(tokens_hbm.at[:, pl.ds(column0, columns)], tokens_ref, sems.at[LOAD_PARTS]))
    for copy in copies:
        copy.start()
    return copies


def multiply_loaded(copies, table_ref, weight_ref, tokens_ref):
    part = weight_ref.shape[0] // LOAD_PARTS
    total = None
    for i in range(LOAD_PARTS):
        copies[i].wait()
        at = slice(i * part, (i + 1) * part)
        product = jnp.dot(table_ref[:, at], weight_ref[at, :], preferred_element_type=jnp.float32)
        total = product if total is None else total + product
    copies[LOAD_PARTS].wait()
    return total - tokens_ref[...].astype(jnp.float32)


def begin_kernel(
    first_ref, ids_hbm, values_hbm, weight_hbm, tokens_hbm,
    weight_ref, table_ref, message_ref,
    ids_ref, values_ref, wide_ref, keys_ref, tokens_ref, sems,
):
    small = [
        pltpu.make_async_copy(ids_hbm, ids_ref, sems.at[LOAD_PARTS + 1]),
        pltpu.make_async_copy(values_hbm, values_ref, sems.at[LOAD_PARTS + 2]),
    ]
    for copy in small:
        copy.start()
    copies = start_loads(weight_hbm, tokens_hbm, 0, weight_ref, tokens_ref, sems)
    for copy in small:
        copy.wait()
    packed = pack(ids_ref[...], values_ref[...], wide_ref)
    columns = weight_ref.shape[1]
    message_ref[:, columns:] = packed.astype(message_ref.dtype)
    build_table(first_ref[0], packed, table_ref, keys_ref)
    total = multiply_loaded(copies, table_ref, weight_ref, tokens_ref)
    message_ref[:, :columns] = total.astype(message_ref.dtype)


def begin(first, ids, values, weight, tokens, columns):
    width = weight.shape[0]
    rows, active = ids.shape
    return pl.pallas_call(
        begin_kernel,
        in_specs=[IN_SMEM] + [IN_HBM] * 4,
        out_specs=[IN_VMEM] * 3,
        out_shape=[
            jax.ShapeDtypeStruct((width, columns), weight.dtype),
            jax.ShapeDtypeStruct((rows, width), jnp.bfloat16),
            jax.ShapeDtypeStruct((rows, columns + 2 * active), jnp.bfloat16),
        ],
        scratch_shapes=[
            pltpu.VMEM((active, rows), ids.dtype),
            pltpu.VMEM((active, rows), values.dtype),
            pltpu.VMEM((2 * rows, active), jnp.float32),
            keys_scratch(rows),
            pltpu.VMEM((rows, columns), tokens.dtype),
            pltpu.SemaphoreType.DMA((LOAD_PARTS + 3,)),
        ],
        compiler_params=params(),
        cost_estimate=cost(1 << 20),
        name="begin",
    )(first, in_hbm(ids.T), in_hbm(values.T), in_hbm(weight), in_hbm(tokens))


def second_kernel(column0, table_ref, weight_hbm, tokens_hbm, weight_ref, out_ref, tokens_ref, sems):
    copies = start_loads(weight_hbm, tokens_hbm, column0, weight_ref, tokens_ref, sems)
    out_ref[...] = multiply_loaded(copies, table_ref, weight_ref, tokens_ref).astype(out_ref.dtype)


def second(table, weight, tokens, column0, columns):
    width = weight.shape[0]
    rows = tokens.shape[0]
    return pl.pallas_call(
        functools.partial(second_kernel, column0),
        in_specs=[IN_VMEM, IN_HBM, IN_HBM],
        out_specs=[IN_VMEM] * 2,
        out_shape=[
            jax.ShapeDtypeStruct((width, columns), weight.dtype),
            jax.ShapeDtypeStruct((rows, columns), jnp.bfloat16),
        ],
        scratch_shapes=[
            pltpu.VMEM((rows, columns), tokens.dtype),
            pltpu.SemaphoreType.DMA((LOAD_PARTS + 1,)),
        ],
        compiler_params=params(),
        cost_estimate=cost(1 << 20),
        name="second",
    )(table, in_hbm(weight), in_hbm(tokens))


def step_kernel(column0, builds, last, *refs):
    if builds:
        first_ref, arrived_ref, weight_ref, bias_ref, table_ref, out_ref, keys_ref = refs
    else:
        table_ref, arrived_ref, weight_ref, bias_ref, out_ref = refs
    columns = weight_ref.shape[1]
    if builds:
        build_table(first_ref[0], arrived_ref[:, columns:].astype(jnp.float32), table_ref, keys_ref)
        if not last:
            out_ref[:, columns:] = arrived_ref[:, columns:]

    def write(at, product):
        total = product + arrived_ref[:, at].astype(jnp.float32)
        if last:
            total = total + bias_ref[:, column0 + at.start : column0 + at.stop]
        out_ref[:, at] = total.astype(out_ref.dtype)

    multiply(table_ref, weight_ref, write)


def step_a(first, arrived, weight, bias, last):
    width, columns = weight.shape
    rows = arrived.shape[0]
    return pl.pallas_call(
        functools.partial(step_kernel, 0, True, last),
        in_specs=[IN_SMEM] + [IN_VMEM] * 3,
        out_specs=[IN_VMEM] * 2,
        out_shape=[
            jax.ShapeDtypeStruct((rows, width), jnp.bfloat16),
            jax.ShapeDtypeStruct((rows, columns if last else arrived.shape[1]), jnp.bfloat16),
        ],
        scratch_shapes=[keys_scratch(rows)],
        compiler_params=params(),
        cost_estimate=cost(1 << 20),
        name="step_a",
    )(first, arrived, weight, bias)


def step_b(table, arrived, weight, bias, column0, last):
    return pl.pallas_call(
        functools.partial(step_kernel, column0, False, last),
        in_specs=[IN_VMEM] * 4,
        out_specs=IN_VMEM,
        out_shape=jax.ShapeDtypeStruct(arrived.shape, jnp.bfloat16),
        compiler_params=params(),
        cost_estimate=cost(1 << 20),
        name="step_b",
    )(table, arrived, weight, bias)


def grad_kernel(blocks, column0, tile, *refs):
    tables, errors = refs[:blocks], refs[blocks : 2 * blocks]
    error_out, grad_out, all_ref, made_ref, sems = refs[-5:]
    rows, columns = errors[0].shape
    width = tables[0].shape[1]
    at = pl.ds(column0, columns)
    copies = [pltpu.make_async_copy(errors[1], error_out.at[:, at], sems.at[width // tile])]
    copies[0].start()
    for b in range(blocks):
        all_ref[b * rows : (b + 1) * rows, :] = errors[b][...]
    for i, l in enumerate(range(0, width, tile)):
        table = jnp.concatenate([table_ref[:, l : l + tile] for table_ref in tables], axis=0)
        product = lax.dot_general(table, all_ref[...], (((0,), (0,)), ((), ())), preferred_element_type=jnp.float32)
        made_ref[l : l + tile, :] = product.astype(made_ref.dtype)
        copy = pltpu.make_async_copy(made_ref.at[pl.ds(l, tile), :], grad_out.at[pl.ds(l, tile), at], sems.at[i])
        copy.start()
        copies.append(copy)
    for copy in copies:
        copy.wait()


def grad_part(tables, errors, features, column0, previous, tile=256):
    width = tables[0].shape[1]
    rows, columns = errors[0].shape
    blocks = len(errors)
    in_specs = [IN_VMEM] * (2 * blocks)
    operands = [*tables, *errors]
    aliases = {}
    if previous is not None:
        aliases = {len(operands): 0, len(operands) + 1: 1}
        in_specs += [IN_HBM, IN_HBM]
        operands += previous
    return pl.pallas_call(
        functools.partial(grad_kernel, blocks, column0, tile),
        in_specs=in_specs,
        out_specs=[IN_HBM, IN_HBM],
        out_shape=[
            jax.ShapeDtypeStruct((rows, features), jnp.bfloat16),
            jax.ShapeDtypeStruct((width, features), jnp.bfloat16),
        ],
        scratch_shapes=[
            pltpu.VMEM((blocks * rows, columns), jnp.bfloat16),
            pltpu.VMEM((width, columns), jnp.bfloat16),
            pltpu.SemaphoreType.DMA((width // tile + 1,)),
        ],
        input_output_aliases=aliases,
        compiler_params=params(),
        cost_estimate=cost(1 << 20),
        name="grad",
    )(*operands)


def local(count, tokens, active_latent_index, latent_values, dec_bias, dec_weight):
    width, features = dec_weight.shape
    columns = features // 2
    first = (lax.axis_index("latent") * (width // LANES)).astype(jnp.int32).reshape(1)
    bias = dec_bias.reshape(1, features)

    def send(x):
        return lax.ppermute(x, "latent", ring_next(count))

    weight_a, own_table, a = begin(first, active_latent_index, latent_values, dec_weight, tokens, columns)
    weight_b, b = second(own_table, dec_weight, tokens, columns, columns)
    tables = [own_table]
    for k in range(1, count):
        last = k == count - 1
        table, a = step_a(first, send(a), weight_a, bias, last)
        b = step_b(table, send(b), weight_b, bias, columns, last)
        tables.append(table)
    errors_a, errors_b = [a], [b]
    for step in range(1, count):
        errors_a.append(send(errors_a[-1]))
        errors_b.append(send(errors_b[-1]))
    tables = [tables[-1]] + tables[:-1]
    made = grad_part(tables, errors_a, features, 0, None)
    made = grad_part(tables, errors_b, features, columns, made)
    return tuple(made)


def solution(mesh):
    in_specs = (
        P(("groups", "latent"), ("dp", "mp")),
        P(("groups", "latent"), None),
        P(("groups", "latent"), None),
        P(("groups", "dp", "mp")),
        P(("groups", "latent"), ("dp", "mp")),
    )
    out_specs = (P(("groups", "latent"), ("dp", "mp")), P(("groups", "latent"), ("dp", "mp")))
    body = functools.partial(local, mesh.shape["latent"])
    return jax.shard_map(body, mesh=mesh, in_specs=in_specs, out_specs=out_specs, check_vma=False)
```

time: 71.5 us -> 66.3 us (0.927)
  starting transfers between devices: 27.6 us -> 19.1 us
  waiting for transfers between devices: 25.2 us -> 28.1 us
    ppermute x15 -> x12, starting transfers between devices: 27.6 us -> 19.1 us  [send(): return lax.ppermute(x, 'latent', ring_next(count))]
    ppermute x15 -> x12, waiting for transfers between devices: 25.2 us -> 28.1 us  [send(): return lax.ppermute(x, 'latent', ring_next(count))]
    pallas_call x9 -> x8, Pallas kernels: 11.3 us -> 11.7 us  [the longest x3 4.03 us: step_a(): pl.pallas_call(functools.partial(step_kernel, 0, True, last), in_specs=[I...]
  transfers between devices with their start and end apart: 15 -> 12, of which waited for: 11 -> 12; matrix products, arithmetic and copies ran while one was open for 0% -> 0% of each run, Pallas kernels for 19% -> 18%
where the time goes in v4:
time: 66.3 us; the launch traced here: 66.1 us
  waiting for transfers between devices  28.1 us (42%)
  starting transfers between devices  19.1 us (29%)
  Pallas kernels  18.2 us (27%)
  between operations  0.69 us (1%)
    ppermute x12, waiting for transfers between devices, send(): return lax.ppermute(x, 'latent', ring_next(count))  28.1 us
    ppermute x12, starting transfers between devices, send(): return lax.ppermute(x, 'latent', ring_next(count))  19.1 us
    pallas_call x2, Pallas kernels, grad_part(): pl.pallas_call(functools.partial(grad_kernel, blocks, column0, tile), in_...  6.51 us
    pallas_call x3, Pallas kernels, step_a(): pl.pallas_call(functools.partial(step_kernel, 0, True, last), in_specs=[I...  4.03 us
    pallas_call x1, Pallas kernels, begin(): pl.pallas_call(begin_kernel, in_specs=[IN_SMEM] + [IN_HBM] * 4, out_specs...  2.77 us
    pallas_call x1, Pallas kernels, second(): pl.pallas_call(functools.partial(second_kernel, column0), in_specs=[IN_VM...  2.49 us
    pallas_call x3, Pallas kernels, step_b(): pl.pallas_call(functools.partial(step_kernel, column0, False, last), in_s...  2.44 us
  transfers between devices with their start and end apart: 12, of which 12 were waited for; matrix products, arithmetic and copies ran while one was open for 0% of the time, Pallas kernels for 18%

profile of v4, /device:TPU:0, one launch (start us, length us, event | category | flops | bytes accessed | tf_op | source)
XLA Modules:
  0.0 66.1 jit_solution(13214511575033863160)
XLA Ops:
  0.6 0.0 copy-start
  0.6 2.8 %begin.1 = (bf16[2048,1024]{1,0:T(8,128)(2,1)S(1)}, bf16[96,2048]{1,0:T(8,128)(2,1)S(1)}, bf16[96,1152]{1,0:T(8,128)(2,1)S(1)}) custom-call(s32[1]{0:T(128)} %bitcast.first_ref.refs_0_, s32[64,96]{1,0:T(8,128)} %bitcast.10, bf16[64,96]{1,0:T(8,128)(2,1)} %bitcast.11, bf16[2048,2048]{1,0:T(8,128)(2,1)} %weight_hbm.3, bf16[96,2048]{1,0:T(8,128)(2,1)} %tokens_hbm.3), custom_call_target="tpu_custom_call" | custom-call | bytes 1048576 | tf_op jit(solution)/shard_map/begin/pallas_call | solution.py:171
  3.4 3.1 %collective-permute-start = (bf16[96,1152]{1,0:T(8,128)(2,1)S(1)}, bf16[96,1152]{1,0:T(8,128)(2,1)S(1)}, u32[]{:S(2)}, u32[]{:S(2)}) collective-permute-start(bf16[96,1152]{1,0:T(8,128)(2,1)S(1)} %get-tuple-element.15), channel_id=1, source_target_pairs={{0,4},{4,12},{12,8},{8,0},{1,5},{5,13},{13,9},{9,1},{2,6},{6,14},{... | collective-permute-start | bytes 663560 | tf_op jit(solution)/shard_map/ppermute | solution.py:329
  6.5 2.5 %second.1 = (bf16[2048,1024]{1,0:T(8,128)(2,1)S(1)}, bf16[96,1024]{1,0:T(8,128)(2,1)S(1)}) custom-call(bf16[96,2048]{1,0:T(8,128)(2,1)S(1)} %get-tuple-element.20.table_ref.refs_1_, bf16[2048,2048]{1,0:T(8,128)(2,1)} %weight_hbm.3, bf16[96,2048]{1,0:T(8,128)(2,1)} %tokens_hbm.3), custom_call_target="tpu_custom_call" | custom-call | bytes 1048576 | tf_op jit(solution)/shard_map/second/pallas_call | solution.py:202
  9.0 2.6 %collective-permute-start.3 = (bf16[96,1024]{1,0:T(8,128)(2,1)S(1)}, bf16[96,1024]{1,0:T(8,128)(2,1)S(1)}, u32[]{:S(2)}, u32[]{:S(2)}) collective-permute-start(bf16[96,1024]{1,0:T(8,128)(2,1)S(1)} %get-tuple-element.23), channel_id=1, source_target_pairs={{0,4},{4,12},{12,8},{8,0},{1,5},{5,13},{13,9},{9,1},{2,6},{6,14},{... | collective-permute-start | bytes 589832 | tf_op jit(solution)/shard_map/ppermute | solution.py:329
  11.6 2.1 %collective-permute-done.refs_1_ = bf16[96,1152]{1,0:T(8,128)(2,1)S(1)} collective-permute-done((bf16[96,1152]{1,0:T(8,128)(2,1)S(1)}, bf16[96,1152]{1,0:T(8,128)(2,1)S(1)}, u32[]{:S(2)}, u32[]{:S(2)}) %collective-permute-start) | collective-permute-done | bytes 221216 | tf_op jit(solution)/shard_map/ppermute | solution.py:329
  13.8 0.0 copy-done
  13.8 1.3 %step_a.3 = (bf16[96,2048]{1,0:T(8,128)(2,1)S(1)}, bf16[96,1152]{1,0:T(8,128)(2,1)S(1)}) custom-call(s32[1]{0:T(128)} %bitcast.first_ref.refs_0_, bf16[96,1152]{1,0:T(8,128)(2,1)S(1)} %collective-permute-done.refs_1_, bf16[2048,1024]{1,0:T(8,128)(2,1)S(1)} %get-tuple-element.16.refs_2_, f32[1,2048]{1,0:T(1,128)S(1)} %bitcast.4), custom_call_target="tpu_custom_call" | custom-call | bytes 1048576 | tf_op jit(solution)/shard_map/step_a/pallas_call | solution.py:243
  15.1 1.2 %collective-permute-start.1 = (bf16[96,1152]{1,0:T(8,128)(2,1)S(1)}, bf16[96,1152]{1,0:T(8,128)(2,1)S(1)}, u32[]{:S(2)}, u32[]{:S(2)}) collective-permute-start(bf16[96,1152]{1,0:T(8,128)(2,1)S(1)} %get-tuple-element.17), channel_id=1, source_target_pairs={{0,4},{4,12},{12,8},{8,0},{1,5},{5,13},{13,9},{9,1},{2,6},{6,14},{... | collective-permute-start | bytes 663560 | tf_op jit(solution)/shard_map/ppermute | solution.py:329
  16.3 0.8 %collective-permute-done.3.refs_1_ = bf16[96,1024]{1,0:T(8,128)(2,1)S(1)} collective-permute-done((bf16[96,1024]{1,0:T(8,128)(2,1)S(1)}, bf16[96,1024]{1,0:T(8,128)(2,1)S(1)}, u32[]{:S(2)}, u32[]{:S(2)}) %collective-permute-start.3) | collective-permute-done | bytes 196640 | tf_op jit(solution)/shard_map/ppermute | solution.py:329
  17.2 0.8 %step_b.3 = bf16[96,1024]{1,0:T(8,128)(2,1)S(1)} custom-call(bf16[96,2048]{1,0:T(8,128)(2,1)S(1)} %get-tuple-element.21.refs_0_.refs_2_, bf16[96,1024]{1,0:T(8,128)(2,1)S(1)} %collective-permute-done.3.refs_1_, bf16[2048,1024]{1,0:T(8,128)(2,1)S(1)} %get-tuple-element.24.refs_2_, f32[1,2048]{1,0:T(1,128)S(1)} %bitcast.5), custom_call_target="tpu_custom_call" | custom-call | bytes 1048576 | tf_op jit(solution)/shard_map/step_b/pallas_call | solution.py:259
  18.0 2.6 %collective-permute-start.4 = (bf16[96,1024]{1,0:T(8,128)(2,1)S(1)}, bf16[96,1024]{1,0:T(8,128)(2,1)S(1)}, u32[]{:S(2)}, u32[]{:S(2)}) collective-permute-start(bf16[96,1024]{1,0:T(8,128)(2,1)S(1)} %step_b.3), channel_id=1, source_target_pairs={{0,4},{4,12},{12,8},{8,0},{1,5},{5,13},{13,9},{9,1},{2,6},{6,14},{... | collective-permute-start | bytes 589832 | tf_op jit(solution)/shard_map/ppermute | solution.py:329
  20.6 2.6 %collective-permute-done.1.refs_1_ = bf16[96,1152]{1,0:T(8,128)(2,1)S(1)} collective-permute-done((bf16[96,1152]{1,0:T(8,128)(2,1)S(1)}, bf16[96,1152]{1,0:T(8,128)(2,1)S(1)}, u32[]{:S(2)}, u32[]{:S(2)}) %collective-permute-start.1) | collective-permute-done | bytes 221216 | tf_op jit(solution)/shard_map/ppermute | solution.py:329
  23.2 1.3 %step_a.4 = (bf16[96,2048]{1,0:T(8,128)(2,1)S(1)}, bf16[96,1152]{1,0:T(8,128)(2,1)S(1)}) custom-call(s32[1]{0:T(128)} %bitcast.first_ref.refs_0_, bf16[96,1152]{1,0:T(8,128)(2,1)S(1)} %collective-permute-done.1.refs_1_, bf16[2048,1024]{1,0:T(8,128)(2,1)S(1)} %get-tuple-element.16.refs_2_, f32[1,2048]{1,0:T(1,128)S(1)} %bitcast.6), custom_call_target="tpu_custom_call" | custom-call | bytes 1048576 | tf_op jit(solution)/shard_map/step_a/pallas_call | solution.py:243
  24.5 1.9 %collective-permute-start.2 = (bf16[96,1152]{1,0:T(8,128)(2,1)S(1)}, bf16[96,1152]{1,0:T(8,128)(2,1)S(1)}, u32[]{:S(2)}, u32[]{:S(2)}) collective-permute-start(bf16[96,1152]{1,0:T(8,128)(2,1)S(1)} %get-tuple-element.18), channel_id=1, source_target_pairs={{0,4},{4,12},{12,8},{8,0},{1,5},{5,13},{13,9},{9,1},{2,6},{6,14},{... | collective-permute-start | bytes 663560 | tf_op jit(solution)/shard_map/ppermute | solution.py:329
  26.5 0.9 %collective-permute-done.4.refs_1_ = bf16[96,1024]{1,0:T(8,128)(2,1)S(1)} collective-permute-done((bf16[96,1024]{1,0:T(8,128)(2,1)S(1)}, bf16[96,1024]{1,0:T(8,128)(2,1)S(1)}, u32[]{:S(2)}, u32[]{:S(2)}) %collective-permute-start.4) | collective-permute-done | bytes 196640 | tf_op jit(solution)/shard_map/ppermute | solution.py:329
  27.4 0.8 %step_b.4 = bf16[96,1024]{1,0:T(8,128)(2,1)S(1)} custom-call(bf16[96,2048]{1,0:T(8,128)(2,1)S(1)} %get-tuple-element.22.refs_0_.refs_3_, bf16[96,1024]{1,0:T(8,128)(2,1)S(1)} %collective-permute-done.4.refs_1_, bf16[2048,1024]{1,0:T(8,128)(2,1)S(1)} %get-tuple-element.24.refs_2_, f32[1,2048]{1,0:T(1,128)S(1)} %bitcast.7), custom_call_target="tpu_custom_call" | custom-call | bytes 1048576 | tf_op jit(solution)/shard_map/step_b/pallas_call | solution.py:259
  28.2 2.5 %collective-permute-start.5 = (bf16[96,1024]{1,0:T(8,128)(2,1)S(1)}, bf16[96,1024]{1,0:T(8,128)(2,1)S(1)}, u32[]{:S(2)}, u32[]{:S(2)}) collective-permute-start(bf16[96,1024]{1,0:T(8,128)(2,1)S(1)} %step_b.4), channel_id=1, source_target_pairs={{0,4},{4,12},{12,8},{8,0},{1,5},{5,13},{13,9},{9,1},{2,6},{6,14},{... | collective-permute-start | bytes 589832 | tf_op jit(solution)/shard_map/ppermute | solution.py:329
  30.7 2.7 %collective-permute-done.2.refs_1_ = bf16[96,1152]{1,0:T(8,128)(2,1)S(1)} collective-permute-done((bf16[96,1152]{1,0:T(8,128)(2,1)S(1)}, bf16[96,1152]{1,0:T(8,128)(2,1)S(1)}, u32[]{:S(2)}, u32[]{:S(2)}) %collective-permute-start.2) | collective-permute-done | bytes 221216 | tf_op jit(solution)/shard_map/ppermute | solution.py:329
  33.4 1.3 %step_a.5 = (bf16[96,2048]{1,0:T(8,128)(2,1)S(1)}, bf16[96,1024]{1,0:T(8,128)(2,1)S(1)}) custom-call(s32[1]{0:T(128)} %bitcast.first_ref.refs_0_, bf16[96,1152]{1,0:T(8,128)(2,1)S(1)} %collective-permute-done.2.refs_1_, bf16[2048,1024]{1,0:T(8,128)(2,1)S(1)} %get-tuple-element.16.refs_2_, f32[1,2048]{1,0:T(1,128)S(1)} %bitcast.8), custom_call_target="tpu_custom_call" | custom-call | bytes 1048576 | tf_op jit(solution)/shard_map/step_a/pallas_call | solution.py:243
  34.8 1.0 %collective-permute-start.9 = (bf16[96,1024]{1,0:T(8,128)(2,1)S(1)}, bf16[96,1024]{1,0:T(8,128)(2,1)S(1)}, u32[]{:S(2)}, u32[]{:S(2)}) collective-permute-start(bf16[96,1024]{1,0:T(8,128)(2,1)S(1)} %get-tuple-element.25.refs_4_), channel_id=1, source_target_pairs={{0,4},{4,12},{12,8},{8,0},{1,5},{5,13},{13,9},{9,1},{2,6},{6,14},{... | collective-permute-start | bytes 589832 | tf_op jit(solution)/shard_map/ppermute | solution.py:329
  35.8 1.8 %collective-permute-done.5.refs_1_ = bf16[96,1024]{1,0:T(8,128)(2,1)S(1)} collective-permute-done((bf16[96,1024]{1,0:T(8,128)(2,1)S(1)}, bf16[96,1024]{1,0:T(8,128)(2,1)S(1)}, u32[]{:S(2)}, u32[]{:S(2)}) %collective-permute-start.5) | collective-permute-done | bytes 196640 | tf_op jit(solution)/shard_map/ppermute | solution.py:329
  37.6 0.8 %step_b.5.refs_4_ = bf16[96,1024]{1,0:T(8,128)(2,1)S(1)} custom-call(bf16[96,2048]{1,0:T(8,128)(2,1)S(1)} %get-tuple-element.19.refs_0_, bf16[96,1024]{1,0:T(8,128)(2,1)S(1)} %collective-permute-done.5.refs_1_, bf16[2048,1024]{1,0:T(8,128)(2,1)S(1)} %get-tuple-element.24.refs_2_, f32[1,2048]{1,0:T(1,128)S(1)} %bitcast.9), custom_call_target="tpu_custom_call" | custom-call | bytes 1048576 | tf_op jit(solution)/shard_map/step_b/pallas_call | solution.py:259
  38.4 1.6 %collective-permute-start.6 = (bf16[96,1024]{1,0:T(8,128)(2,1)S(1)}, bf16[96,1024]{1,0:T(8,128)(2,1)S(1)}, u32[]{:S(2)}, u32[]{:S(2)}) collective-permute-start(bf16[96,1024]{1,0:T(8,128)(2,1)S(1)} %step_b.5.refs_4_), channel_id=1, source_target_pairs={{0,4},{4,12},{12,8},{8,0},{1,5},{5,13},{13,9},{9,1},{2,6},{6,14},{... | collective-permute-start | bytes 589832 | tf_op jit(solution)/shard_map/ppermute | solution.py:329
  40.1 3.3 %collective-permute-done.9.refs_5_ = bf16[96,1024]{1,0:T(8,128)(2,1)S(1)} collective-permute-done((bf16[96,1024]{1,0:T(8,128)(2,1)S(1)}, bf16[96,1024]{1,0:T(8,128)(2,1)S(1)}, u32[]{:S(2)}, u32[]{:S(2)}) %collective-permute-start.9) | collective-permute-done | bytes 196640 | tf_op jit(solution)/shard_map/ppermute | solution.py:329
  43.4 0.2 collective-permute-start.10
  43.6 4.0 %collective-permute-done.6.refs_5_ = bf16[96,1024]{1,0:T(8,128)(2,1)S(1)} collective-permute-done((bf16[96,1024]{1,0:T(8,128)(2,1)S(1)}, bf16[96,1024]{1,0:T(8,128)(2,1)S(1)}, u32[]{:S(2)}, u32[]{:S(2)}) %collective-permute-start.6) | collective-permute-done | bytes 196640 | tf_op jit(solution)/shard_map/ppermute | solution.py:329
  47.6 0.9 %collective-permute-start.7 = (bf16[96,1024]{1,0:T(8,128)(2,1)S(1)}, bf16[96,1024]{1,0:T(8,128)(2,1)S(1)}, u32[]{:S(2)}, u32[]{:S(2)}) collective-permute-start(bf16[96,1024]{1,0:T(8,128)(2,1)S(1)} %collective-permute-done.6.refs_5_), channel_id=1, source_target_pairs={{0,4},{4,12},{12,8},{8,0},{1,5},{5,13},{13,9},{9,1},{2,6},{6,14},{... | collective-permute-start | bytes 589832 | tf_op jit(solution)/shard_map/ppermute | solution.py:329
  48.4 3.7 %collective-permute-done.10.refs_6_ = bf16[96,1024]{1,0:T(8,128)(2,1)S(1)} collective-permute-done((bf16[96,1024]{1,0:T(8,128)(2,1)S(1)}, bf16[96,1024]{1,0:T(8,128)(2,1)S(1)}, u32[]{:S(2)}, u32[]{:S(2)}) %collective-permute-start.10) | collective-permute-done | bytes 196640 | tf_op jit(solution)/shard_map/ppermute | solution.py:329
  52.1 0.6 collective-permute-start.11
  52.7 3.7 %collective-permute-done.7.refs_6_ = bf16[96,1024]{1,0:T(8,128)(2,1)S(1)} collective-permute-done((bf16[96,1024]{1,0:T(8,128)(2,1)S(1)}, bf16[96,1024]{1,0:T(8,128)(2,1)S(1)}, u32[]{:S(2)}, u32[]{:S(2)}) %collective-permute-start.7) | collective-permute-done | bytes 196640 | tf_op jit(solution)/shard_map/ppermute | solution.py:329
  56.3 0.9 %collective-permute-start.8 = (bf16[96,1024]{1,0:T(8,128)(2,1)S(1)}, bf16[96,1024]{1,0:T(8,128)(2,1)S(1)}, u32[]{:S(2)}, u32[]{:S(2)}) collective-permute-start(bf16[96,1024]{1,0:T(8,128)(2,1)S(1)} %collective-permute-done.7.refs_6_), channel_id=1, source_target_pairs={{0,4},{4,12},{12,8},{8,0},{1,5},{5,13},{13,9},{9,1},{2,6},{6,14},{... | collective-permute-start | bytes 589832 | tf_op jit(solution)/shard_map/ppermute | solution.py:329
  57.2 2.0 %collective-permute-done.11.refs_7_ = bf16[96,1024]{1,0:T(8,128)(2,1)S(1)} collective-permute-done((bf16[96,1024]{1,0:T(8,128)(2,1)S(1)}, bf16[96,1024]{1,0:T(8,128)(2,1)S(1)}, u32[]{:S(2)}, u32[]{:S(2)}) %collective-permute-start.11) | collective-permute-done | bytes 196640 | tf_op jit(solution)/shard_map/ppermute | solution.py:329
  59.2 3.3 %grad.2 = (bf16[96,2048]{1,0:T(8,128)(2,1)}, bf16[2048,2048]{1,0:T(8,128)(2,1)}) custom-call(bf16[96,2048]{1,0:T(8,128)(2,1)S(1)} %get-tuple-element.19.refs_0_, bf16[96,2048]{1,0:T(8,128)(2,1)S(1)} %get-tuple-element.20.table_ref.refs_1_, bf16[96,2048]{1,0:T(8,128)(2,1)S(1)} %get-tuple-element.21.refs_0_.refs_2_, ...), custom_call_target="tpu_custom_call" | custom-call | bytes 1048576 | tf_op jit(solution)/shard_map/grad/pallas_call | solution.py:302
  62.4 0.4 collective-permute-done.8.refs_7_
  62.9 3.3 %grad.3 = (bf16[96,2048]{1,0:T(8,128)(2,1)}, bf16[2048,2048]{1,0:T(8,128)(2,1)}) custom-call(bf16[96,2048]{1,0:T(8,128)(2,1)S(1)} %get-tuple-element.19.refs_0_, bf16[96,2048]{1,0:T(8,128)(2,1)S(1)} %get-tuple-element.20.table_ref.refs_1_, bf16[96,2048]{1,0:T(8,128)(2,1)S(1)} %get-tuple-element.21.refs_0_.refs_2_, ...), custom_call_target="tpu_custom_call", output_to_operand_aliasing={{0}: (8, {}), {1}: (9, {})} | custom-call | bytes 1048576 | tf_op jit(solution)/shard_map/grad/pallas_call | solution.py:302
Async XLA Ops:
  0.6 13.1 %copy-start = (f32[2048]{0:T(1024)S(1)}, f32[2048]{0:T(1024)}, u32[]{:S(2)}) copy-start(f32[2048]{0:T(1024)} %param.8) | copy-start | bytes 24580
  3.4 10.3 %collective-permute-start = (bf16[96,1152]{1,0:T(8,128)(2,1)S(1)}, bf16[96,1152]{1,0:T(8,128)(2,1)S(1)}, u32[]{:S(2)}, u32[]{:S(2)}) collective-permute-start(bf16[96,1152]{1,0:T(8,128)(2,1)S(1)} %get-tuple-element.15), channel_id=1, source_target_pairs={{0,4},{4,12},{12,8},{8,0},{1,5},{5,13},{13,9},{9,1},{2,6},{6,14},{... | collective-permute-start | bytes 663560 | tf_op jit(solution)/shard_map/ppermute | solution.py:329
  9.0 8.2 %collective-permute-start.3 = (bf16[96,1024]{1,0:T(8,128)(2,1)S(1)}, bf16[96,1024]{1,0:T(8,128)(2,1)S(1)}, u32[]{:S(2)}, u32[]{:S(2)}) collective-permute-start(bf16[96,1024]{1,0:T(8,128)(2,1)S(1)} %get-tuple-element.23), channel_id=1, source_target_pairs={{0,4},{4,12},{12,8},{8,0},{1,5},{5,13},{13,9},{9,1},{2,6},{6,14},{... | collective-permute-start | bytes 589832 | tf_op jit(solution)/shard_map/ppermute | solution.py:329
  15.1 8.1 %collective-permute-start.1 = (bf16[96,1152]{1,0:T(8,128)(2,1)S(1)}, bf16[96,1152]{1,0:T(8,128)(2,1)S(1)}, u32[]{:S(2)}, u32[]{:S(2)}) collective-permute-start(bf16[96,1152]{1,0:T(8,128)(2,1)S(1)} %get-tuple-element.17), channel_id=1, source_target_pairs={{0,4},{4,12},{12,8},{8,0},{1,5},{5,13},{13,9},{9,1},{2,6},{6,14},{... | collective-permute-start | bytes 663560 | tf_op jit(solution)/shard_map/ppermute | solution.py:329
  18.0 9.4 %collective-permute-start.4 = (bf16[96,1024]{1,0:T(8,128)(2,1)S(1)}, bf16[96,1024]{1,0:T(8,128)(2,1)S(1)}, u32[]{:S(2)}, u32[]{:S(2)}) collective-permute-start(bf16[96,1024]{1,0:T(8,128)(2,1)S(1)} %step_b.3), channel_id=1, source_target_pairs={{0,4},{4,12},{12,8},{8,0},{1,5},{5,13},{13,9},{9,1},{2,6},{6,14},{... | collective-permute-start | bytes 589832 | tf_op jit(solution)/shard_map/ppermute | solution.py:329
  24.5 8.9 %collective-permute-start.2 = (bf16[96,1152]{1,0:T(8,128)(2,1)S(1)}, bf16[96,1152]{1,0:T(8,128)(2,1)S(1)}, u32[]{:S(2)}, u32[]{:S(2)}) collective-permute-start(bf16[96,1152]{1,0:T(8,128)(2,1)S(1)} %get-tuple-element.18), channel_id=1, source_target_pairs={{0,4},{4,12},{12,8},{8,0},{1,5},{5,13},{13,9},{9,1},{2,6},{6,14},{... | collective-permute-start | bytes 663560 | tf_op jit(solution)/shard_map/ppermute | solution.py:329
  28.2 9.4 %collective-permute-start.5 = (bf16[96,1024]{1,0:T(8,128)(2,1)S(1)}, bf16[96,1024]{1,0:T(8,128)(2,1)S(1)}, u32[]{:S(2)}, u32[]{:S(2)}) collective-permute-start(bf16[96,1024]{1,0:T(8,128)(2,1)S(1)} %step_b.4), channel_id=1, source_target_pairs={{0,4},{4,12},{12,8},{8,0},{1,5},{5,13},{13,9},{9,1},{2,6},{6,14},{... | collective-permute-start | bytes 589832 | tf_op jit(solution)/shard_map/ppermute | solution.py:329
  34.8 8.6 %collective-permute-start.9 = (bf16[96,1024]{1,0:T(8,128)(2,1)S(1)}, bf16[96,1024]{1,0:T(8,128)(2,1)S(1)}, u32[]{:S(2)}, u32[]{:S(2)}) collective-permute-start(bf16[96,1024]{1,0:T(8,128)(2,1)S(1)} %get-tuple-element.25.refs_4_), channel_id=1, source_target_pairs={{0,4},{4,12},{12,8},{8,0},{1,5},{5,13},{13,9},{9,1},{2,6},{6,14},{... | collective-permute-start | bytes 589832 | tf_op jit(solution)/shard_map/ppermute | solution.py:329
  38.4 9.1 %collective-permute-start.6 = (bf16[96,1024]{1,0:T(8,128)(2,1)S(1)}, bf16[96,1024]{1,0:T(8,128)(2,1)S(1)}, u32[]{:S(2)}, u32[]{:S(2)}) collective-permute-start(bf16[96,1024]{1,0:T(8,128)(2,1)S(1)} %step_b.5.refs_4_), channel_id=1, source_target_pairs={{0,4},{4,12},{12,8},{8,0},{1,5},{5,13},{13,9},{9,1},{2,6},{6,14},{... | collective-permute-start | bytes 589832 | tf_op jit(solution)/shard_map/ppermute | solution.py:329
  43.4 8.7 %collective-permute-start.10 = (bf16[96,1024]{1,0:T(8,128)(2,1)S(1)}, bf16[96,1024]{1,0:T(8,128)(2,1)S(1)}, u32[]{:S(2)}, u32[]{:S(2)}) collective-permute-start(bf16[96,1024]{1,0:T(8,128)(2,1)S(1)} %collective-permute-done.9.refs_5_), channel_id=1, source_target_pairs={{0,4},{4,12},{12,8},{8,0},{1,5},{5,13},{13,9},{9,1},{2,6},{6,14},{... | collective-permute-start | bytes 589832 | tf_op jit(solution)/shard_map/ppermute | solution.py:329
  47.6 8.7 %collective-permute-start.7 = (bf16[96,1024]{1,0:T(8,128)(2,1)S(1)}, bf16[96,1024]{1,0:T(8,128)(2,1)S(1)}, u32[]{:S(2)}, u32[]{:S(2)}) collective-permute-start(bf16[96,1024]{1,0:T(8,128)(2,1)S(1)} %collective-permute-done.6.refs_5_), channel_id=1, source_target_pairs={{0,4},{4,12},{12,8},{8,0},{1,5},{5,13},{13,9},{9,1},{2,6},{6,14},{... | collective-permute-start | bytes 589832 | tf_op jit(solution)/shard_map/ppermute | solution.py:329
  52.1 7.1 %collective-permute-start.11 = (bf16[96,1024]{1,0:T(8,128)(2,1)S(1)}, bf16[96,1024]{1,0:T(8,128)(2,1)S(1)}, u32[]{:S(2)}, u32[]{:S(2)}) collective-permute-start(bf16[96,1024]{1,0:T(8,128)(2,1)S(1)} %collective-permute-done.10.refs_6_), channel_id=1, source_target_pairs={{0,4},{4,12},{12,8},{8,0},{1,5},{5,13},{13,9},{9,1},{2,6},{6,14},{... | collective-permute-start | bytes 589832 | tf_op jit(solution)/shard_map/ppermute | solution.py:329
  56.3 6.6 %collective-permute-start.8 = (bf16[96,1024]{1,0:T(8,128)(2,1)S(1)}, bf16[96,1024]{1,0:T(8,128)(2,1)S(1)}, u32[]{:S(2)}, u32[]{:S(2)}) collective-permute-start(bf16[96,1024]{1,0:T(8,128)(2,1)S(1)} %collective-permute-done.7.refs_6_), channel_id=1, source_target_pairs={{0,4},{4,12},{12,8},{8,0},{1,5},{5,13},{13,9},{9,1},{2,6},{6,14},{... | collective-permute-start | bytes 589832 | tf_op jit(solution)/shard_map/ppermute | solution.py:329

commit v5 on v4

--- a/solution.py
+++ b/solution.py
@@ -267,33 +267,67 @@
     )(table, arrived, weight, bias)
 
 
+def contract_tokens(tables, all_ref, at):
+    table = jnp.concatenate([table_ref[:, at] for table_ref in tables], axis=0)
+    return lax.dot_general(table, all_ref[...], (((0,), (0,)), ((), ())), preferred_element_type=jnp.float32)
+
+
+def gather_errors(errors, all_ref):
+    rows = errors[0].shape[0]
+    for b, error_ref in enumerate(errors):
+        all_ref[b * rows : (b + 1) * rows, :] = error_ref[...]
+
+
+def early_kernel(blocks, tile, *refs):
+    tables, errors, out_ref, all_ref = refs[:blocks], refs[blocks : 2 * blocks], refs[-2], refs[-1]
+    gather_errors(errors, all_ref)
+    for l in range(0, out_ref.shape[0], tile):
+        at = slice(l, l + tile)
+        out_ref[at, :] = contract_tokens(tables, all_ref, at)
+
+
+def early_grad(tables, errors, tile=256):
+    width = tables[0].shape[1]
+    rows, columns = errors[0].shape
+    blocks = len(errors)
+    return pl.pallas_call(
+        functools.partial(early_kernel, blocks, tile),
+        in_specs=[IN_VMEM] * (2 * blocks),
+        out_specs=IN_VMEM,
+        out_shape=jax.ShapeDtypeStruct((width, columns), jnp.float32),
+        scratch_shapes=[pltpu.VMEM((blocks * rows, columns), jnp.bfloat16)],
+        compiler_params=params(),
+        cost_estimate=cost(1 << 20),
+        name="early_grad",
+    )(*tables, *errors)
+
+
 def grad_kernel(blocks, column0, tile, *refs):
-    tables, errors = refs[:blocks], refs[blocks : 2 * blocks]
+    tables, errors, (own_ref, early_ref) = refs[:blocks], refs[blocks : 2 * blocks], refs[2 * blocks : 2 * blocks + 2]
     error_out, grad_out, all_ref, made_ref, sems = refs[-5:]
     rows, columns = errors[0].shape
     width = tables[0].shape[1]
-    at = pl.ds(column0, columns)
-    copies = [pltpu.make_async_copy(errors[1], error_out.at[:, at], sems.at[width // tile])]
+    part = pl.ds(column0, columns)
+    copies = [pltpu.make_async_copy(own_ref, error_out.at[:, part], sems.at[width // tile])]
     copies[0].start()
-    for b in range(blocks):
-        all_ref[b * rows : (b + 1) * rows, :] = errors[b][...]
+    gather_errors(errors, all_ref)
     for i, l in enumerate(range(0, width, tile)):
-        table = jnp.concatenate([table_ref[:, l : l + tile] for table_ref in tables], axis=0)
-        product = lax.dot_general(table, all_ref[...], (((0,), (0,)), ((), ())), preferred_element_type=jnp.float32)
-        made_ref[l : l + tile, :] = product.astype(made_ref.dtype)
-        copy = pltpu.make_async_copy(made_ref.at[pl.ds(l, tile), :], grad_out.at[pl.ds(l, tile), at], sems.at[i])
+        at = slice(l, l + tile)
+        product = contract_tokens(tables, all_ref, at) + early_ref[at, :]
+        made_ref[at, :] = product.astype(made_ref.dtype)
+        copy = pltpu.make_async_copy(made_ref.at[pl.ds(l, tile), :], grad_out.at[pl.ds(l, tile), part], sems.at[i])
         copy.start()
         copies.append(copy)
     for copy in copies:
         copy.wait()
 
 
-def grad_part(tables, errors, features, column0, previous, tile=256):
+def grad_part(tables, errors, own, early, features, column0, previous, tile=256):
     width = tables[0].shape[1]
     rows, columns = errors[0].shape
     blocks = len(errors)
-    in_specs = [IN_VMEM] * (2 * blocks)
-    operands = [*tables, *errors]
+    in_specs = [IN_VMEM] * (2 * blocks + 2)
+    operands = [*tables, *errors, own, early]
     aliases = {}
     if previous is not None:
         aliases = {len(operands): 0, len(operands) + 1: 1}
@@ -336,13 +370,19 @@
         table, a = step_a(first, send(a), weight_a, bias, last)
         b = step_b(table, send(b), weight_b, bias, columns, last)
         tables.append(table)
-    errors_a, errors_b = [a], [b]
-    for step in range(1, count):
-        errors_a.append(send(errors_a[-1]))
-        errors_b.append(send(errors_b[-1]))
+    errors = [[a], [b]]
     tables = [tables[-1]] + tables[:-1]
-    made = grad_part(tables, errors_a, features, 0, None)
-    made = grad_part(tables, errors_b, features, columns, made)
+    split = max(1, count - 2)
+    early = [None, None]
+    for arrived in range(1, count):
+        for c, chain in enumerate(errors):
+            if arrived == count - 1:
+                early[c] = early_grad(tables[:split], chain[:split])
+                chain[-1], early[c] = lax.optimization_barrier((chain[-1], early[c]))
+            chain.append(send(chain[-1]))
+    made = None
+    for chain, part, at in zip(errors, early, (0, columns)):
+        made = grad_part(tables[split:], chain[split:], chain[1], part, features, at, made)
     return tuple(made)
 
 

time: 66.3 us -> 65.2 us (0.983)
  waiting for transfers between devices: 28.1 us -> 21.4 us
  starting transfers between devices: 19.1 us -> 23.7 us
  Pallas kernels: 18.2 us -> 19.1 us
    ppermute x12, waiting for transfers between devices: 28.1 us -> 21.4 us  [send(): return lax.ppermute(x, 'latent', ring_next(count))]
    ppermute x12, starting transfers between devices: 19.1 us -> 23.7 us  [send(): return lax.ppermute(x, 'latent', ring_next(count))]
    pallas_call x0 -> x2, Pallas kernels: none -> 2.59 us  [early_grad(): pl.pallas_call(functools.partial(early_kernel, blocks, tile), in_specs=[I...]
    pallas_call x2, Pallas kernels: 6.51 us -> 4.82 us  [grad_part(): pl.pallas_call(functools.partial(grad_kernel, blocks, column0, tile), in_...]
  transfers between devices with their start and end apart: 12 -> 12, of which waited for: 12 -> 12; matrix products, arithmetic and copies ran while one was open for 0% -> 0% of each run, Pallas kernels for 18% -> 21%
where the time goes in v5:
time: 65.2 us; the launch traced here: 65.1 us
  starting transfers between devices  23.7 us (36%)
  waiting for transfers between devices  21.4 us (33%)
  Pallas kernels  19.1 us (29%)
  between operations  0.86 us (1%)
    ppermute x12, starting transfers between devices, send(): return lax.ppermute(x, 'latent', ring_next(count))  23.7 us
    ppermute x12, waiting for transfers between devices, send(): return lax.ppermute(x, 'latent', ring_next(count))  21.4 us
    pallas_call x2, Pallas kernels, grad_part(): pl.pallas_call(functools.partial(grad_kernel, blocks, column0, tile), in_...  4.82 us
    pallas_call x3, Pallas kernels, step_a(): pl.pallas_call(functools.partial(step_kernel, 0, True, last), in_specs=[I...  4.04 us
    pallas_call x1, Pallas kernels, begin(): pl.pallas_call(begin_kernel, in_specs=[IN_SMEM] + [IN_HBM] * 4, out_specs...  2.77 us
    pallas_call x2, Pallas kernels, early_grad(): pl.pallas_call(functools.partial(early_kernel, blocks, tile), in_specs=[I...  2.59 us
    pallas_call x1, Pallas kernels, second(): pl.pallas_call(functools.partial(second_kernel, column0), in_specs=[IN_VM...  2.49 us
    pallas_call x3, Pallas kernels, step_b(): pl.pallas_call(functools.partial(step_kernel, column0, False, last), in_s...  2.44 us
  transfers between devices with their start and end apart: 12, of which 12 were waited for; matrix products, arithmetic and copies ran while one was open for 0% of the time, Pallas kernels for 21%

profile of v5, /device:TPU:0, one launch (start us, length us, event | category | flops | bytes accessed | tf_op | source)
XLA Modules:
  0.0 65.1 jit_solution(9327296111666379516)
XLA Ops:
  0.6 0.0 copy-start
  0.6 2.8 %begin.1 = (bf16[2048,1024]{1,0:T(8,128)(2,1)S(1)}, bf16[96,2048]{1,0:T(8,128)(2,1)S(1)}, bf16[96,1152]{1,0:T(8,128)(2,1)S(1)}) custom-call(s32[1]{0:T(128)} %bitcast.first_ref.refs_0_, s32[64,96]{1,0:T(8,128)} %bitcast.10, bf16[64,96]{1,0:T(8,128)(2,1)} %bitcast.11, bf16[2048,2048]{1,0:T(8,128)(2,1)} %weight_hbm.3, bf16[96,2048]{1,0:T(8,128)(2,1)} %tokens_hbm.3), custom_call_target="tpu_custom_call" | custom-call | bytes 1048576 | tf_op jit(solution)/shard_map/begin/pallas_call | solution.py:171
  3.4 3.1 %collective-permute-start = (bf16[96,1152]{1,0:T(8,128)(2,1)S(1)}, bf16[96,1152]{1,0:T(8,128)(2,1)S(1)}, u32[]{:S(2)}, u32[]{:S(2)}) collective-permute-start(bf16[96,1152]{1,0:T(8,128)(2,1)S(1)} %get-tuple-element.19), channel_id=1, source_target_pairs={{0,4},{4,12},{12,8},{8,0},{1,5},{5,13},{13,9},{9,1},{2,6},{6,14},{... | collective-permute-start | bytes 663560 | tf_op jit(solution)/shard_map/ppermute | solution.py:363
  6.5 2.5 %second.1 = (bf16[2048,1024]{1,0:T(8,128)(2,1)S(1)}, bf16[96,1024]{1,0:T(8,128)(2,1)S(1)}) custom-call(bf16[96,2048]{1,0:T(8,128)(2,1)S(1)} %get-tuple-element.26.table_ref.refs_1_, bf16[2048,2048]{1,0:T(8,128)(2,1)} %weight_hbm.3, bf16[96,2048]{1,0:T(8,128)(2,1)} %tokens_hbm.3), custom_call_target="tpu_custom_call" | custom-call | bytes 1048576 | tf_op jit(solution)/shard_map/second/pallas_call | solution.py:202
  9.0 2.6 %collective-permute-start.3 = (bf16[96,1024]{1,0:T(8,128)(2,1)S(1)}, bf16[96,1024]{1,0:T(8,128)(2,1)S(1)}, u32[]{:S(2)}, u32[]{:S(2)}) collective-permute-start(bf16[96,1024]{1,0:T(8,128)(2,1)S(1)} %get-tuple-element.27), channel_id=1, source_target_pairs={{0,4},{4,12},{12,8},{8,0},{1,5},{5,13},{13,9},{9,1},{2,6},{6,14},{... | collective-permute-start | bytes 589832 | tf_op jit(solution)/shard_map/ppermute | solution.py:363
  11.6 2.1 %collective-permute-done.refs_1_ = bf16[96,1152]{1,0:T(8,128)(2,1)S(1)} collective-permute-done((bf16[96,1152]{1,0:T(8,128)(2,1)S(1)}, bf16[96,1152]{1,0:T(8,128)(2,1)S(1)}, u32[]{:S(2)}, u32[]{:S(2)}) %collective-permute-start) | collective-permute-done | bytes 221216 | tf_op jit(solution)/shard_map/ppermute | solution.py:363
  13.7 0.0 copy-done
  13.7 1.3 %step_a.3 = (bf16[96,2048]{1,0:T(8,128)(2,1)S(1)}, bf16[96,1152]{1,0:T(8,128)(2,1)S(1)}) custom-call(s32[1]{0:T(128)} %bitcast.first_ref.refs_0_, bf16[96,1152]{1,0:T(8,128)(2,1)S(1)} %collective-permute-done.refs_1_, bf16[2048,1024]{1,0:T(8,128)(2,1)S(1)} %get-tuple-element.20.refs_2_, f32[1,2048]{1,0:T(1,128)S(1)} %bitcast.4), custom_call_target="tpu_custom_call" | custom-call | bytes 1048576 | tf_op jit(solution)/shard_map/step_a/pallas_call | solution.py:243
  15.1 1.3 %collective-permute-start.1 = (bf16[96,1152]{1,0:T(8,128)(2,1)S(1)}, bf16[96,1152]{1,0:T(8,128)(2,1)S(1)}, u32[]{:S(2)}, u32[]{:S(2)}) collective-permute-start(bf16[96,1152]{1,0:T(8,128)(2,1)S(1)} %get-tuple-element.22), channel_id=1, source_target_pairs={{0,4},{4,12},{12,8},{8,0},{1,5},{5,13},{13,9},{9,1},{2,6},{6,14},{... | collective-permute-start | bytes 663560 | tf_op jit(solution)/shard_map/ppermute | solution.py:363
  16.3 0.8 %collective-permute-done.3.refs_1_ = bf16[96,1024]{1,0:T(8,128)(2,1)S(1)} collective-permute-done((bf16[96,1024]{1,0:T(8,128)(2,1)S(1)}, bf16[96,1024]{1,0:T(8,128)(2,1)S(1)}, u32[]{:S(2)}, u32[]{:S(2)}) %collective-permute-start.3) | collective-permute-done | bytes 196640 | tf_op jit(solution)/shard_map/ppermute | solution.py:363
  17.1 0.8 %step_b.3 = bf16[96,1024]{1,0:T(8,128)(2,1)S(1)} custom-call(bf16[96,2048]{1,0:T(8,128)(2,1)S(1)} %get-tuple-element.21.refs_0_, bf16[96,1024]{1,0:T(8,128)(2,1)S(1)} %collective-permute-done.3.refs_1_, bf16[2048,1024]{1,0:T(8,128)(2,1)S(1)} %get-tuple-element.28.refs_2_, f32[1,2048]{1,0:T(1,128)S(1)} %bitcast.5), custom_call_target="tpu_custom_call" | custom-call | bytes 1048576 | tf_op jit(solution)/shard_map/step_b/pallas_call | solution.py:259
  18.0 2.6 %collective-permute-start.4 = (bf16[96,1024]{1,0:T(8,128)(2,1)S(1)}, bf16[96,1024]{1,0:T(8,128)(2,1)S(1)}, u32[]{:S(2)}, u32[]{:S(2)}) collective-permute-start(bf16[96,1024]{1,0:T(8,128)(2,1)S(1)} %step_b.3), channel_id=1, source_target_pairs={{0,4},{4,12},{12,8},{8,0},{1,5},{5,13},{13,9},{9,1},{2,6},{6,14},{... | collective-permute-start | bytes 589832 | tf_op jit(solution)/shard_map/ppermute | solution.py:363
  20.6 2.4 %collective-permute-done.1.refs_1_ = bf16[96,1152]{1,0:T(8,128)(2,1)S(1)} collective-permute-done((bf16[96,1152]{1,0:T(8,128)(2,1)S(1)}, bf16[96,1152]{1,0:T(8,128)(2,1)S(1)}, u32[]{:S(2)}, u32[]{:S(2)}) %collective-permute-start.1) | collective-permute-done | bytes 221216 | tf_op jit(solution)/shard_map/ppermute | solution.py:363
  23.0 1.3 %step_a.4 = (bf16[96,2048]{1,0:T(8,128)(2,1)S(1)}, bf16[96,1152]{1,0:T(8,128)(2,1)S(1)}) custom-call(s32[1]{0:T(128)} %bitcast.first_ref.refs_0_, bf16[96,1152]{1,0:T(8,128)(2,1)S(1)} %collective-permute-done.1.refs_1_, bf16[2048,1024]{1,0:T(8,128)(2,1)S(1)} %get-tuple-element.20.refs_2_, f32[1,2048]{1,0:T(1,128)S(1)} %bitcast.6), custom_call_target="tpu_custom_call" | custom-call | bytes 1048576 | tf_op jit(solution)/shard_map/step_a/pallas_call | solution.py:243
  24.4 2.1 %collective-permute-start.2 = (bf16[96,1152]{1,0:T(8,128)(2,1)S(1)}, bf16[96,1152]{1,0:T(8,128)(2,1)S(1)}, u32[]{:S(2)}, u32[]{:S(2)}) collective-permute-start(bf16[96,1152]{1,0:T(8,128)(2,1)S(1)} %get-tuple-element.24), channel_id=1, source_target_pairs={{0,4},{4,12},{12,8},{8,0},{1,5},{5,13},{13,9},{9,1},{2,6},{6,14},{... | collective-permute-start | bytes 663560 | tf_op jit(solution)/shard_map/ppermute | solution.py:363
  26.5 0.8 %collective-permute-done.4.refs_1_ = bf16[96,1024]{1,0:T(8,128)(2,1)S(1)} collective-permute-done((bf16[96,1024]{1,0:T(8,128)(2,1)S(1)}, bf16[96,1024]{1,0:T(8,128)(2,1)S(1)}, u32[]{:S(2)}, u32[]{:S(2)}) %collective-permute-start.4) | collective-permute-done | bytes 196640 | tf_op jit(solution)/shard_map/ppermute | solution.py:363
  27.2 0.8 %step_b.4 = bf16[96,1024]{1,0:T(8,128)(2,1)S(1)} custom-call(bf16[96,2048]{1,0:T(8,128)(2,1)S(1)} %get-tuple-element.23.refs_0_.refs_1_, bf16[96,1024]{1,0:T(8,128)(2,1)S(1)} %collective-permute-done.4.refs_1_, bf16[2048,1024]{1,0:T(8,128)(2,1)S(1)} %get-tuple-element.28.refs_2_, f32[1,2048]{1,0:T(1,128)S(1)} %bitcast.7), custom_call_target="tpu_custom_call" | custom-call | bytes 1048576 | tf_op jit(solution)/shard_map/step_b/pallas_call | solution.py:259
  28.0 2.7 %collective-permute-start.5 = (bf16[96,1024]{1,0:T(8,128)(2,1)S(1)}, bf16[96,1024]{1,0:T(8,128)(2,1)S(1)}, u32[]{:S(2)}, u32[]{:S(2)}) collective-permute-start(bf16[96,1024]{1,0:T(8,128)(2,1)S(1)} %step_b.4), channel_id=1, source_target_pairs={{0,4},{4,12},{12,8},{8,0},{1,5},{5,13},{13,9},{9,1},{2,6},{6,14},{... | collective-permute-start | bytes 589832 | tf_op jit(solution)/shard_map/ppermute | solution.py:363
  30.7 2.3 %collective-permute-done.2.refs_1_ = bf16[96,1152]{1,0:T(8,128)(2,1)S(1)} collective-permute-done((bf16[96,1152]{1,0:T(8,128)(2,1)S(1)}, bf16[96,1152]{1,0:T(8,128)(2,1)S(1)}, u32[]{:S(2)}, u32[]{:S(2)}) %collective-permute-start.2) | collective-permute-done | bytes 221216 | tf_op jit(solution)/shard_map/ppermute | solution.py:363
  33.0 1.3 %step_a.5 = (bf16[96,2048]{1,0:T(8,128)(2,1)S(1)}, bf16[96,1024]{1,0:T(8,128)(2,1)S(1)}) custom-call(s32[1]{0:T(128)} %bitcast.first_ref.refs_0_, bf16[96,1152]{1,0:T(8,128)(2,1)S(1)} %collective-permute-done.2.refs_1_, bf16[2048,1024]{1,0:T(8,128)(2,1)S(1)} %get-tuple-element.20.refs_2_, f32[1,2048]{1,0:T(1,128)S(1)} %bitcast.8), custom_call_target="tpu_custom_call" | custom-call | bytes 1048576 | tf_op jit(solution)/shard_map/step_a/pallas_call | solution.py:243
  34.3 1.5 %collective-permute-start.9 = (bf16[96,1024]{1,0:T(8,128)(2,1)S(1)}, bf16[96,1024]{1,0:T(8,128)(2,1)S(1)}, u32[]{:S(2)}, u32[]{:S(2)}) collective-permute-start(bf16[96,1024]{1,0:T(8,128)(2,1)S(1)} %get-tuple-element.31.refs_2_), channel_id=1, source_target_pairs={{0,4},{4,12},{12,8},{8,0},{1,5},{5,13},{13,9},{9,1},{2,6},{6,14},{... | collective-permute-start | bytes 589832 | tf_op jit(solution)/shard_map/ppermute | solution.py:363
  35.8 1.4 %collective-permute-done.5.refs_1_ = bf16[96,1024]{1,0:T(8,128)(2,1)S(1)} collective-permute-done((bf16[96,1024]{1,0:T(8,128)(2,1)S(1)}, bf16[96,1024]{1,0:T(8,128)(2,1)S(1)}, u32[]{:S(2)}, u32[]{:S(2)}) %collective-permute-start.5) | collective-permute-done | bytes 196640 | tf_op jit(solution)/shard_map/ppermute | solution.py:363
  37.2 0.8 %step_b.5.refs_2_ = bf16[96,1024]{1,0:T(8,128)(2,1)S(1)} custom-call(bf16[96,2048]{1,0:T(8,128)(2,1)S(1)} %get-tuple-element.25.refs_0_, bf16[96,1024]{1,0:T(8,128)(2,1)S(1)} %collective-permute-done.5.refs_1_, bf16[2048,1024]{1,0:T(8,128)(2,1)S(1)} %get-tuple-element.28.refs_2_, f32[1,2048]{1,0:T(1,128)S(1)} %bitcast.9), custom_call_target="tpu_custom_call" | custom-call | bytes 1048576 | tf_op jit(solution)/shard_map/step_b/pallas_call | solution.py:259
  38.0 2.1 %collective-permute-start.6 = (bf16[96,1024]{1,0:T(8,128)(2,1)S(1)}, bf16[96,1024]{1,0:T(8,128)(2,1)S(1)}, u32[]{:S(2)}, u32[]{:S(2)}) collective-permute-start(bf16[96,1024]{1,0:T(8,128)(2,1)S(1)} %step_b.5.refs_2_), channel_id=1, source_target_pairs={{0,4},{4,12},{12,8},{8,0},{1,5},{5,13},{13,9},{9,1},{2,6},{6,14},{... | collective-permute-start | bytes 589832 | tf_op jit(solution)/shard_map/ppermute | solution.py:363
  40.1 2.9 %collective-permute-done.9.refs_3_.refs_4_ = bf16[96,1024]{1,0:T(8,128)(2,1)S(1)} collective-permute-done((bf16[96,1024]{1,0:T(8,128)(2,1)S(1)}, bf16[96,1024]{1,0:T(8,128)(2,1)S(1)}, u32[]{:S(2)}, u32[]{:S(2)}) %collective-permute-start.9) | collective-permute-done | bytes 196640 | tf_op jit(solution)/shard_map/ppermute | solution.py:363
  43.0 0.6 collective-permute-start.10
  43.6 3.6 %collective-permute-done.6.refs_3_.refs_4_ = bf16[96,1024]{1,0:T(8,128)(2,1)S(1)} collective-permute-done((bf16[96,1024]{1,0:T(8,128)(2,1)S(1)}, bf16[96,1024]{1,0:T(8,128)(2,1)S(1)}, u32[]{:S(2)}, u32[]{:S(2)}) %collective-permute-start.6) | collective-permute-done | bytes 196640 | tf_op jit(solution)/shard_map/ppermute | solution.py:363
  47.2 1.2 %collective-permute-start.7 = (bf16[96,1024]{1,0:T(8,128)(2,1)S(1)}, bf16[96,1024]{1,0:T(8,128)(2,1)S(1)}, u32[]{:S(2)}, u32[]{:S(2)}) collective-permute-start(bf16[96,1024]{1,0:T(8,128)(2,1)S(1)} %collective-permute-done.6.refs_3_.refs_4_), channel_id=1, source_target_pairs={{0,4},{4,12},{12,8},{8,0},{1,5},{5,13},{13,9},{9,1},{2,6},{6,14},{... | collective-permute-start | bytes 589832 | tf_op jit(solution)/shard_map/ppermute | solution.py:363
  48.4 1.3 %early_grad.3.refs_5_ = f32[2048,1024]{1,0:T(8,128)S(1)} custom-call(bf16[96,2048]{1,0:T(8,128)(2,1)S(1)} %get-tuple-element.25.refs_0_, bf16[96,2048]{1,0:T(8,128)(2,1)S(1)} %get-tuple-element.26.table_ref.refs_1_, bf16[96,1024]{1,0:T(8,128)(2,1)S(1)} %get-tuple-element.31.refs_2_, bf16[96,1024]{1,0:T(8,128)(2,1)S(1)} %collective-permute-done.9.refs_3_.refs_4_), custom_call_target="tpu_custom_call" | custom-call | bytes 1048576 | tf_op jit(solution)/shard_map/early_grad/pallas_call | solution.py:293
  49.7 1.3 %early_grad.2.refs_5_ = f32[2048,1024]{1,0:T(8,128)S(1)} custom-call(bf16[96,2048]{1,0:T(8,128)(2,1)S(1)} %get-tuple-element.25.refs_0_, bf16[96,2048]{1,0:T(8,128)(2,1)S(1)} %get-tuple-element.26.table_ref.refs_1_, bf16[96,1024]{1,0:T(8,128)(2,1)S(1)} %step_b.5.refs_2_, bf16[96,1024]{1,0:T(8,128)(2,1)S(1)} %collective-permute-done.6.refs_3_.refs_4_), custom_call_target="tpu_custom_call" | custom-call | bytes 1048576 | tf_op jit(solution)/shard_map/early_grad/pallas_call | solution.py:293
  51.0 0.7 %collective-permute-done.10.refs_2_ = bf16[96,1024]{1,0:T(8,128)(2,1)S(1)} collective-permute-done((bf16[96,1024]{1,0:T(8,128)(2,1)S(1)}, bf16[96,1024]{1,0:T(8,128)(2,1)S(1)}, u32[]{:S(2)}, u32[]{:S(2)}) %collective-permute-start.10) | collective-permute-done | bytes 196640 | tf_op jit(solution)/shard_map/ppermute | solution.py:363
  51.7 2.7 %collective-permute-start.11 = (bf16[96,1024]{1,0:T(8,128)(2,1)S(1)}, bf16[96,1024]{1,0:T(8,128)(2,1)S(1)}, u32[]{:S(2)}, u32[]{:S(2)}) collective-permute-start(bf16[96,1024]{1,0:T(8,128)(2,1)S(1)} %collective-permute-done.10.refs_2_), channel_id=1, source_target_pairs={{0,4},{4,12},{12,8},{8,0},{1,5},{5,13},{13,9},{9,1},{2,6},{6,14},{... | collective-permute-start | bytes 589832 | tf_op jit(solution)/shard_map/ppermute | solution.py:363
  54.5 1.5 %collective-permute-done.7.refs_2_ = bf16[96,1024]{1,0:T(8,128)(2,1)S(1)} collective-permute-done((bf16[96,1024]{1,0:T(8,128)(2,1)S(1)}, bf16[96,1024]{1,0:T(8,128)(2,1)S(1)}, u32[]{:S(2)}, u32[]{:S(2)}) %collective-permute-start.7) | collective-permute-done | bytes 196640 | tf_op jit(solution)/shard_map/ppermute | solution.py:363
  55.9 1.2 %collective-permute-start.8 = (bf16[96,1024]{1,0:T(8,128)(2,1)S(1)}, bf16[96,1024]{1,0:T(8,128)(2,1)S(1)}, u32[]{:S(2)}, u32[]{:S(2)}) collective-permute-start(bf16[96,1024]{1,0:T(8,128)(2,1)S(1)} %collective-permute-done.7.refs_2_), channel_id=1, source_target_pairs={{0,4},{4,12},{12,8},{8,0},{1,5},{5,13},{13,9},{9,1},{2,6},{6,14},{... | collective-permute-start | bytes 589832 | tf_op jit(solution)/shard_map/ppermute | solution.py:363
  57.2 2.1 %collective-permute-done.11.refs_3_ = bf16[96,1024]{1,0:T(8,128)(2,1)S(1)} collective-permute-done((bf16[96,1024]{1,0:T(8,128)(2,1)S(1)}, bf16[96,1024]{1,0:T(8,128)(2,1)S(1)}, u32[]{:S(2)}, u32[]{:S(2)}) %collective-permute-start.11) | collective-permute-done | bytes 196640 | tf_op jit(solution)/shard_map/ppermute | solution.py:363
  59.3 2.4 %grad.2 = (bf16[96,2048]{1,0:T(8,128)(2,1)}, bf16[2048,2048]{1,0:T(8,128)(2,1)}) custom-call(bf16[96,2048]{1,0:T(8,128)(2,1)S(1)} %get-tuple-element.21.refs_0_, bf16[96,2048]{1,0:T(8,128)(2,1)S(1)} %get-tuple-element.23.refs_0_.refs_1_, bf16[96,1024]{1,0:T(8,128)(2,1)S(1)} %collective-permute-done.10.refs_2_, ...), custom_call_target="tpu_custom_call" | custom-call | bytes 1048576 | tf_op jit(solution)/shard_map/grad/pallas_call | solution.py:336
  61.7 0.8 %collective-permute-done.8.refs_3_ = bf16[96,1024]{1,0:T(8,128)(2,1)S(1)} collective-permute-done((bf16[96,1024]{1,0:T(8,128)(2,1)S(1)}, bf16[96,1024]{1,0:T(8,128)(2,1)S(1)}, u32[]{:S(2)}, u32[]{:S(2)}) %collective-permute-start.8) | collective-permute-done | bytes 196640 | tf_op jit(solution)/shard_map/ppermute | solution.py:363
  62.5 2.4 %grad.3 = (bf16[96,2048]{1,0:T(8,128)(2,1)}, bf16[2048,2048]{1,0:T(8,128)(2,1)}) custom-call(bf16[96,2048]{1,0:T(8,128)(2,1)S(1)} %get-tuple-element.21.refs_0_, bf16[96,2048]{1,0:T(8,128)(2,1)S(1)} %get-tuple-element.23.refs_0_.refs_1_, bf16[96,1024]{1,0:T(8,128)(2,1)S(1)} %collective-permute-done.7.refs_2_, ...), custom_call_target="tpu_custom_call", output_to_operand_aliasing={{0}: (6, {}), {1}: (7, {})} | custom-call | bytes 1048576 | tf_op jit(solution)/shard_map/grad/pallas_call | solution.py:336
Async XLA Ops:
  0.6 13.1 %copy-start = (f32[2048]{0:T(1024)S(1)}, f32[2048]{0:T(1024)}, u32[]{:S(2)}) copy-start(f32[2048]{0:T(1024)} %param.8) | copy-start | bytes 24580
  3.4 10.3 %collective-permute-start = (bf16[96,1152]{1,0:T(8,128)(2,1)S(1)}, bf16[96,1152]{1,0:T(8,128)(2,1)S(1)}, u32[]{:S(2)}, u32[]{:S(2)}) collective-permute-start(bf16[96,1152]{1,0:T(8,128)(2,1)S(1)} %get-tuple-element.19), channel_id=1, source_target_pairs={{0,4},{4,12},{12,8},{8,0},{1,5},{5,13},{13,9},{9,1},{2,6},{6,14},{... | collective-permute-start | bytes 663560 | tf_op jit(solution)/shard_map/ppermute | solution.py:363
  9.0 8.2 %collective-permute-start.3 = (bf16[96,1024]{1,0:T(8,128)(2,1)S(1)}, bf16[96,1024]{1,0:T(8,128)(2,1)S(1)}, u32[]{:S(2)}, u32[]{:S(2)}) collective-permute-start(bf16[96,1024]{1,0:T(8,128)(2,1)S(1)} %get-tuple-element.27), channel_id=1, source_target_pairs={{0,4},{4,12},{12,8},{8,0},{1,5},{5,13},{13,9},{9,1},{2,6},{6,14},{... | collective-permute-start | bytes 589832 | tf_op jit(solution)/shard_map/ppermute | solution.py:363
  15.1 7.9 %collective-permute-start.1 = (bf16[96,1152]{1,0:T(8,128)(2,1)S(1)}, bf16[96,1152]{1,0:T(8,128)(2,1)S(1)}, u32[]{:S(2)}, u32[]{:S(2)}) collective-permute-start(bf16[96,1152]{1,0:T(8,128)(2,1)S(1)} %get-tuple-element.22), channel_id=1, source_target_pairs={{0,4},{4,12},{12,8},{8,0},{1,5},{5,13},{13,9},{9,1},{2,6},{6,14},{... | collective-permute-start | bytes 663560 | tf_op jit(solution)/shard_map/ppermute | solution.py:363
  18.0 9.3 %collective-permute-start.4 = (bf16[96,1024]{1,0:T(8,128)(2,1)S(1)}, bf16[96,1024]{1,0:T(8,128)(2,1)S(1)}, u32[]{:S(2)}, u32[]{:S(2)}) collective-permute-start(bf16[96,1024]{1,0:T(8,128)(2,1)S(1)} %step_b.3), channel_id=1, source_target_pairs={{0,4},{4,12},{12,8},{8,0},{1,5},{5,13},{13,9},{9,1},{2,6},{6,14},{... | collective-permute-start | bytes 589832 | tf_op jit(solution)/shard_map/ppermute | solution.py:363
  24.4 8.6 %collective-permute-start.2 = (bf16[96,1152]{1,0:T(8,128)(2,1)S(1)}, bf16[96,1152]{1,0:T(8,128)(2,1)S(1)}, u32[]{:S(2)}, u32[]{:S(2)}) collective-permute-start(bf16[96,1152]{1,0:T(8,128)(2,1)S(1)} %get-tuple-element.24), channel_id=1, source_target_pairs={{0,4},{4,12},{12,8},{8,0},{1,5},{5,13},{13,9},{9,1},{2,6},{6,14},{... | collective-permute-start | bytes 663560 | tf_op jit(solution)/shard_map/ppermute | solution.py:363
  28.0 9.1 %collective-permute-start.5 = (bf16[96,1024]{1,0:T(8,128)(2,1)S(1)}, bf16[96,1024]{1,0:T(8,128)(2,1)S(1)}, u32[]{:S(2)}, u32[]{:S(2)}) collective-permute-start(bf16[96,1024]{1,0:T(8,128)(2,1)S(1)} %step_b.4), channel_id=1, source_target_pairs={{0,4},{4,12},{12,8},{8,0},{1,5},{5,13},{13,9},{9,1},{2,6},{6,14},{... | collective-permute-start | bytes 589832 | tf_op jit(solution)/shard_map/ppermute | solution.py:363
  34.3 8.7 %collective-permute-start.9 = (bf16[96,1024]{1,0:T(8,128)(2,1)S(1)}, bf16[96,1024]{1,0:T(8,128)(2,1)S(1)}, u32[]{:S(2)}, u32[]{:S(2)}) collective-permute-start(bf16[96,1024]{1,0:T(8,128)(2,1)S(1)} %get-tuple-element.31.refs_2_), channel_id=1, source_target_pairs={{0,4},{4,12},{12,8},{8,0},{1,5},{5,13},{13,9},{9,1},{2,6},{6,14},{... | collective-permute-start | bytes 589832 | tf_op jit(solution)/shard_map/ppermute | solution.py:363
  38.0 9.2 %collective-permute-start.6 = (bf16[96,1024]{1,0:T(8,128)(2,1)S(1)}, bf16[96,1024]{1,0:T(8,128)(2,1)S(1)}, u32[]{:S(2)}, u32[]{:S(2)}) collective-permute-start(bf16[96,1024]{1,0:T(8,128)(2,1)S(1)} %step_b.5.refs_2_), channel_id=1, source_target_pairs={{0,4},{4,12},{12,8},{8,0},{1,5},{5,13},{13,9},{9,1},{2,6},{6,14},{... | collective-permute-start | bytes 589832 | tf_op jit(solution)/shard_map/ppermute | solution.py:363
  43.0 8.7 %collective-permute-start.10 = (bf16[96,1024]{1,0:T(8,128)(2,1)S(1)}, bf16[96,1024]{1,0:T(8,128)(2,1)S(1)}, u32[]{:S(2)}, u32[]{:S(2)}) collective-permute-start(bf16[96,1024]{1,0:T(8,128)(2,1)S(1)} %collective-permute-done.9.refs_3_.refs_4_), channel_id=1, source_target_pairs={{0,4},{4,12},{12,8},{8,0},{1,5},{5,13},{13,9},{9,1},{2,6},{6,14},{... | collective-permute-start | bytes 589832 | tf_op jit(solution)/shard_map/ppermute | solution.py:363
  47.2 8.7 %collective-permute-start.7 = (bf16[96,1024]{1,0:T(8,128)(2,1)S(1)}, bf16[96,1024]{1,0:T(8,128)(2,1)S(1)}, u32[]{:S(2)}, u32[]{:S(2)}) collective-permute-start(bf16[96,1024]{1,0:T(8,128)(2,1)S(1)} %collective-permute-done.6.refs_3_.refs_4_), channel_id=1, source_target_pairs={{0,4},{4,12},{12,8},{8,0},{1,5},{5,13},{13,9},{9,1},{2,6},{6,14},{... | collective-permute-start | bytes 589832 | tf_op jit(solution)/shard_map/ppermute | solution.py:363
  51.7 7.5 %collective-permute-start.11 = (bf16[96,1024]{1,0:T(8,128)(2,1)S(1)}, bf16[96,1024]{1,0:T(8,128)(2,1)S(1)}, u32[]{:S(2)}, u32[]{:S(2)}) collective-permute-start(bf16[96,1024]{1,0:T(8,128)(2,1)S(1)} %collective-permute-done.10.refs_2_), channel_id=1, source_target_pairs={{0,4},{4,12},{12,8},{8,0},{1,5},{5,13},{13,9},{9,1},{2,6},{6,14},{... | collective-permute-start | bytes 589832 | tf_op jit(solution)/shard_map/ppermute | solution.py:363
  55.9 6.6 %collective-permute-start.8 = (bf16[96,1024]{1,0:T(8,128)(2,1)S(1)}, bf16[96,1024]{1,0:T(8,128)(2,1)S(1)}, u32[]{:S(2)}, u32[]{:S(2)}) collective-permute-start(bf16[96,1024]{1,0:T(8,128)(2,1)S(1)} %collective-permute-done.7.refs_2_), channel_id=1, source_target_pairs={{0,4},{4,12},{12,8},{8,0},{1,5},{5,13},{13,9},{9,1},{2,6},{6,14},{... | collective-permute-start | bytes 589832 | tf_op jit(solution)/shard_map/ppermute | solution.py:363

commit v6 on v5

--- a/solution.py
+++ b/solution.py
@@ -11,7 +11,7 @@
 EXPONENT_BITS = (1, 2, 4, 8, 16, 32, 64)
 GROUP = 8
 TILE = 512
-LOAD_PARTS = 8
+LOAD_PARTS = 4
 VMEM_LIMIT = 24 * 1024 * 1024
 IN_VMEM = pl.BlockSpec(memory_space=pltpu.VMEM)
 IN_SMEM = pl.BlockSpec(memory_space=pltpu.SMEM)
@@ -31,7 +31,7 @@
 
 
 def ring_order(count):
-    return [0] + list(range(1, count, 2)) + list(range(count - 2 + count % 2, 0, -2))
+    return [0] + list(range(2, count, 2)) + list(range(count - 1 - count % 2, 0, -2))
 
 
 def ring_next(count):

time: 65.2 us -> 64.2 us (0.985)
  waiting for transfers between devices: 21.4 us -> 9.31 us
  starting transfers between devices: 23.7 us -> 34.8 us
    ppermute x12, waiting for transfers between devices: 21.4 us -> 9.31 us  [send(): return lax.ppermute(x, 'latent', ring_next(count))]
    ppermute x12, starting transfers between devices: 23.7 us -> 34.8 us  [send(): return lax.ppermute(x, 'latent', ring_next(count))]
  transfers between devices with their start and end apart: 12 -> 12, of which waited for: 12 -> 9; matrix products, arithmetic and copies ran while one was open for 0% -> 0% of each run, Pallas kernels for 21% -> 22%
where the time goes in v6:
time: 64.2 us; the launch traced here: 64.1 us
  starting transfers between devices  34.8 us (54%)
  Pallas kernels  19.1 us (30%)
  waiting for transfers between devices  9.31 us (15%)
  between operations  0.86 us (1%)
    ppermute x12, starting transfers between devices, send(): return lax.ppermute(x, 'latent', ring_next(count))  34.8 us
    ppermute x12, waiting for transfers between devices, send(): return lax.ppermute(x, 'latent', ring_next(count))  9.31 us
    pallas_call x2, Pallas kernels, grad_part(): pl.pallas_call(functools.partial(grad_kernel, blocks, column0, tile), in_...  4.82 us
    pallas_call x3, Pallas kernels, step_a(): pl.pallas_call(functools.partial(step_kernel, 0, True, last), in_specs=[I...  4.03 us
    pallas_call x1, Pallas kernels, begin(): pl.pallas_call(begin_kernel, in_specs=[IN_SMEM] + [IN_HBM] * 4, out_specs...  2.65 us
    pallas_call x2, Pallas kernels, early_grad(): pl.pallas_call(functools.partial(early_kernel, blocks, tile), in_specs=[I...  2.59 us
    pallas_call x1, Pallas kernels, second(): pl.pallas_call(functools.partial(second_kernel, column0), in_specs=[IN_VM...  2.55 us
    pallas_call x3, Pallas kernels, step_b(): pl.pallas_call(functools.partial(step_kernel, column0, False, last), in_s...  2.44 us
  transfers between devices with their start and end apart: 12, of which 9 were waited for; matrix products, arithmetic and copies ran while one was open for 0% of the time, Pallas kernels for 22%

profile of v6, /device:TPU:0, one launch (start us, length us, event | category | flops | bytes accessed | tf_op | source)
XLA Modules:
  0.0 64.1 jit_solution(5529818752157387564)
XLA Ops:
  0.6 0.0 copy-start
  0.6 2.6 %begin.1 = (bf16[2048,1024]{1,0:T(8,128)(2,1)S(1)}, bf16[96,2048]{1,0:T(8,128)(2,1)S(1)}, bf16[96,1152]{1,0:T(8,128)(2,1)S(1)}) custom-call(s32[1]{0:T(128)} %bitcast.first_ref.refs_0_, s32[64,96]{1,0:T(8,128)} %bitcast.10, bf16[64,96]{1,0:T(8,128)(2,1)} %bitcast.11, bf16[2048,2048]{1,0:T(8,128)(2,1)} %weight_hbm.3, bf16[96,2048]{1,0:T(8,128)(2,1)} %tokens_hbm.3), custom_call_target="tpu_custom_call" | custom-call | bytes 1048576 | tf_op jit(solution)/shard_map/begin/pallas_call | solution.py:171
  3.3 4.1 %collective-permute-start = (bf16[96,1152]{1,0:T(8,128)(2,1)S(1)}, bf16[96,1152]{1,0:T(8,128)(2,1)S(1)}, u32[]{:S(2)}, u32[]{:S(2)}) collective-permute-start(bf16[96,1152]{1,0:T(8,128)(2,1)S(1)} %get-tuple-element.19), channel_id=1, source_target_pairs={{0,8},{8,12},{12,4},{4,0},{1,9},{9,13},{13,5},{5,1},{2,10},{10,14}... | collective-permute-start | bytes 663560 | tf_op jit(solution)/shard_map/ppermute | solution.py:363
  7.4 2.6 %second.1 = (bf16[2048,1024]{1,0:T(8,128)(2,1)S(1)}, bf16[96,1024]{1,0:T(8,128)(2,1)S(1)}) custom-call(bf16[96,2048]{1,0:T(8,128)(2,1)S(1)} %get-tuple-element.26.table_ref.refs_1_, bf16[2048,2048]{1,0:T(8,128)(2,1)} %weight_hbm.3, bf16[96,2048]{1,0:T(8,128)(2,1)} %tokens_hbm.3), custom_call_target="tpu_custom_call" | custom-call | bytes 1048576 | tf_op jit(solution)/shard_map/second/pallas_call | solution.py:202
  10.0 1.6 %collective-permute-start.3 = (bf16[96,1024]{1,0:T(8,128)(2,1)S(1)}, bf16[96,1024]{1,0:T(8,128)(2,1)S(1)}, u32[]{:S(2)}, u32[]{:S(2)}) collective-permute-start(bf16[96,1024]{1,0:T(8,128)(2,1)S(1)} %get-tuple-element.27), channel_id=1, source_target_pairs={{0,8},{8,12},{12,4},{4,0},{1,9},{9,13},{13,5},{5,1},{2,10},{10,14}... | collective-permute-start | bytes 589832 | tf_op jit(solution)/shard_map/ppermute | solution.py:363
  11.6 1.2 %collective-permute-done.refs_1_ = bf16[96,1152]{1,0:T(8,128)(2,1)S(1)} collective-permute-done((bf16[96,1152]{1,0:T(8,128)(2,1)S(1)}, bf16[96,1152]{1,0:T(8,128)(2,1)S(1)}, u32[]{:S(2)}, u32[]{:S(2)}) %collective-permute-start) | collective-permute-done | bytes 221216 | tf_op jit(solution)/shard_map/ppermute | solution.py:363
  12.8 0.0 copy-done
  12.8 1.3 %step_a.3 = (bf16[96,2048]{1,0:T(8,128)(2,1)S(1)}, bf16[96,1152]{1,0:T(8,128)(2,1)S(1)}) custom-call(s32[1]{0:T(128)} %bitcast.first_ref.refs_0_, bf16[96,1152]{1,0:T(8,128)(2,1)S(1)} %collective-permute-done.refs_1_, bf16[2048,1024]{1,0:T(8,128)(2,1)S(1)} %get-tuple-element.20.refs_2_, f32[1,2048]{1,0:T(1,128)S(1)} %bitcast.4), custom_call_target="tpu_custom_call" | custom-call | bytes 1048576 | tf_op jit(solution)/shard_map/step_a/pallas_call | solution.py:243
  14.2 3.4 %collective-permute-start.1 = (bf16[96,1152]{1,0:T(8,128)(2,1)S(1)}, bf16[96,1152]{1,0:T(8,128)(2,1)S(1)}, u32[]{:S(2)}, u32[]{:S(2)}) collective-permute-start(bf16[96,1152]{1,0:T(8,128)(2,1)S(1)} %get-tuple-element.22), channel_id=1, source_target_pairs={{0,8},{8,12},{12,4},{4,0},{1,9},{9,13},{13,5},{5,1},{2,10},{10,14}... | collective-permute-start | bytes 663560 | tf_op jit(solution)/shard_map/ppermute | solution.py:363
  17.6 0.0 collective-permute-done.3.refs_1_
  17.6 0.8 %step_b.3 = bf16[96,1024]{1,0:T(8,128)(2,1)S(1)} custom-call(bf16[96,2048]{1,0:T(8,128)(2,1)S(1)} %get-tuple-element.21.refs_0_, bf16[96,1024]{1,0:T(8,128)(2,1)S(1)} %collective-permute-done.3.refs_1_, bf16[2048,1024]{1,0:T(8,128)(2,1)S(1)} %get-tuple-element.28.refs_2_, f32[1,2048]{1,0:T(1,128)S(1)} %bitcast.5), custom_call_target="tpu_custom_call" | custom-call | bytes 1048576 | tf_op jit(solution)/shard_map/step_b/pallas_call | solution.py:259
  18.4 2.4 %collective-permute-start.4 = (bf16[96,1024]{1,0:T(8,128)(2,1)S(1)}, bf16[96,1024]{1,0:T(8,128)(2,1)S(1)}, u32[]{:S(2)}, u32[]{:S(2)}) collective-permute-start(bf16[96,1024]{1,0:T(8,128)(2,1)S(1)} %step_b.3), channel_id=1, source_target_pairs={{0,8},{8,12},{12,4},{4,0},{1,9},{9,13},{13,5},{5,1},{2,10},{10,14}... | collective-permute-start | bytes 589832 | tf_op jit(solution)/shard_map/ppermute | solution.py:363
  20.8 2.1 %collective-permute-done.1.refs_1_ = bf16[96,1152]{1,0:T(8,128)(2,1)S(1)} collective-permute-done((bf16[96,1152]{1,0:T(8,128)(2,1)S(1)}, bf16[96,1152]{1,0:T(8,128)(2,1)S(1)}, u32[]{:S(2)}, u32[]{:S(2)}) %collective-permute-start.1) | collective-permute-done | bytes 221216 | tf_op jit(solution)/shard_map/ppermute | solution.py:363
  22.9 1.3 %step_a.4 = (bf16[96,2048]{1,0:T(8,128)(2,1)S(1)}, bf16[96,1152]{1,0:T(8,128)(2,1)S(1)}) custom-call(s32[1]{0:T(128)} %bitcast.first_ref.refs_0_, bf16[96,1152]{1,0:T(8,128)(2,1)S(1)} %collective-permute-done.1.refs_1_, bf16[2048,1024]{1,0:T(8,128)(2,1)S(1)} %get-tuple-element.20.refs_2_, f32[1,2048]{1,0:T(1,128)S(1)} %bitcast.6), custom_call_target="tpu_custom_call" | custom-call | bytes 1048576 | tf_op jit(solution)/shard_map/step_a/pallas_call | solution.py:243
  24.3 2.6 %collective-permute-start.2 = (bf16[96,1152]{1,0:T(8,128)(2,1)S(1)}, bf16[96,1152]{1,0:T(8,128)(2,1)S(1)}, u32[]{:S(2)}, u32[]{:S(2)}) collective-permute-start(bf16[96,1152]{1,0:T(8,128)(2,1)S(1)} %get-tuple-element.24), channel_id=1, source_target_pairs={{0,8},{8,12},{12,4},{4,0},{1,9},{9,13},{13,5},{5,1},{2,10},{10,14}... | collective-permute-start | bytes 663560 | tf_op jit(solution)/shard_map/ppermute | solution.py:363
  26.9 0.1 collective-permute-done.4.refs_1_
  27.0 0.8 %step_b.4 = bf16[96,1024]{1,0:T(8,128)(2,1)S(1)} custom-call(bf16[96,2048]{1,0:T(8,128)(2,1)S(1)} %get-tuple-element.23.refs_0_.refs_1_, bf16[96,1024]{1,0:T(8,128)(2,1)S(1)} %collective-permute-done.4.refs_1_, bf16[2048,1024]{1,0:T(8,128)(2,1)S(1)} %get-tuple-element.28.refs_2_, f32[1,2048]{1,0:T(1,128)S(1)} %bitcast.7), custom_call_target="tpu_custom_call" | custom-call | bytes 1048576 | tf_op jit(solution)/shard_map/step_b/pallas_call | solution.py:259
  27.8 2.8 %collective-permute-start.5 = (bf16[96,1024]{1,0:T(8,128)(2,1)S(1)}, bf16[96,1024]{1,0:T(8,128)(2,1)S(1)}, u32[]{:S(2)}, u32[]{:S(2)}) collective-permute-start(bf16[96,1024]{1,0:T(8,128)(2,1)S(1)} %step_b.4), channel_id=1, source_target_pairs={{0,8},{8,12},{12,4},{4,0},{1,9},{9,13},{13,5},{5,1},{2,10},{10,14}... | collective-permute-start | bytes 589832 | tf_op jit(solution)/shard_map/ppermute | solution.py:363
  30.6 1.9 %collective-permute-done.2.refs_1_ = bf16[96,1152]{1,0:T(8,128)(2,1)S(1)} collective-permute-done((bf16[96,1152]{1,0:T(8,128)(2,1)S(1)}, bf16[96,1152]{1,0:T(8,128)(2,1)S(1)}, u32[]{:S(2)}, u32[]{:S(2)}) %collective-permute-start.2) | collective-permute-done | bytes 221216 | tf_op jit(solution)/shard_map/ppermute | solution.py:363
  32.4 1.3 %step_a.5 = (bf16[96,2048]{1,0:T(8,128)(2,1)S(1)}, bf16[96,1024]{1,0:T(8,128)(2,1)S(1)}) custom-call(s32[1]{0:T(128)} %bitcast.first_ref.refs_0_, bf16[96,1152]{1,0:T(8,128)(2,1)S(1)} %collective-permute-done.2.refs_1_, bf16[2048,1024]{1,0:T(8,128)(2,1)S(1)} %get-tuple-element.20.refs_2_, f32[1,2048]{1,0:T(1,128)S(1)} %bitcast.8), custom_call_target="tpu_custom_call" | custom-call | bytes 1048576 | tf_op jit(solution)/shard_map/step_a/pallas_call | solution.py:243
  33.8 3.0 %collective-permute-start.9 = (bf16[96,1024]{1,0:T(8,128)(2,1)S(1)}, bf16[96,1024]{1,0:T(8,128)(2,1)S(1)}, u32[]{:S(2)}, u32[]{:S(2)}) collective-permute-start(bf16[96,1024]{1,0:T(8,128)(2,1)S(1)} %get-tuple-element.31.refs_2_), channel_id=1, source_target_pairs={{0,8},{8,12},{12,4},{4,0},{1,9},{9,13},{13,5},{5,1},{2,10},{10,14}... | collective-permute-start | bytes 589832 | tf_op jit(solution)/shard_map/ppermute | solution.py:363
  36.8 0.0 collective-permute-done.5.refs_1_
  36.8 0.8 %step_b.5.refs_2_ = bf16[96,1024]{1,0:T(8,128)(2,1)S(1)} custom-call(bf16[96,2048]{1,0:T(8,128)(2,1)S(1)} %get-tuple-element.25.refs_0_, bf16[96,1024]{1,0:T(8,128)(2,1)S(1)} %collective-permute-done.5.refs_1_, bf16[2048,1024]{1,0:T(8,128)(2,1)S(1)} %get-tuple-element.28.refs_2_, f32[1,2048]{1,0:T(1,128)S(1)} %bitcast.9), custom_call_target="tpu_custom_call" | custom-call | bytes 1048576 | tf_op jit(solution)/shard_map/step_b/pallas_call | solution.py:259
  37.6 2.9 %collective-permute-start.6 = (bf16[96,1024]{1,0:T(8,128)(2,1)S(1)}, bf16[96,1024]{1,0:T(8,128)(2,1)S(1)}, u32[]{:S(2)}, u32[]{:S(2)}) collective-permute-start(bf16[96,1024]{1,0:T(8,128)(2,1)S(1)} %step_b.5.refs_2_), channel_id=1, source_target_pairs={{0,8},{8,12},{12,4},{4,0},{1,9},{9,13},{13,5},{5,1},{2,10},{10,14}... | collective-permute-start | bytes 589832 | tf_op jit(solution)/shard_map/ppermute | solution.py:363
  40.4 1.5 %collective-permute-done.9.refs_3_.refs_4_ = bf16[96,1024]{1,0:T(8,128)(2,1)S(1)} collective-permute-done((bf16[96,1024]{1,0:T(8,128)(2,1)S(1)}, bf16[96,1024]{1,0:T(8,128)(2,1)S(1)}, u32[]{:S(2)}, u32[]{:S(2)}) %collective-permute-start.9) | collective-permute-done | bytes 196640 | tf_op jit(solution)/shard_map/ppermute | solution.py:363
  42.0 3.4 %collective-permute-start.10 = (bf16[96,1024]{1,0:T(8,128)(2,1)S(1)}, bf16[96,1024]{1,0:T(8,128)(2,1)S(1)}, u32[]{:S(2)}, u32[]{:S(2)}) collective-permute-start(bf16[96,1024]{1,0:T(8,128)(2,1)S(1)} %collective-permute-done.9.refs_3_.refs_4_), channel_id=1, source_target_pairs={{0,8},{8,12},{12,4},{4,0},{1,9},{9,13},{13,5},{5,1},{2,10},{10,14}... | collective-permute-start | bytes 589832 | tf_op jit(solution)/shard_map/ppermute | solution.py:363
  45.4 0.8 %collective-permute-done.6.refs_3_.refs_4_ = bf16[96,1024]{1,0:T(8,128)(2,1)S(1)} collective-permute-done((bf16[96,1024]{1,0:T(8,128)(2,1)S(1)}, bf16[96,1024]{1,0:T(8,128)(2,1)S(1)}, u32[]{:S(2)}, u32[]{:S(2)}) %collective-permute-start.6) | collective-permute-done | bytes 196640 | tf_op jit(solution)/shard_map/ppermute | solution.py:363
  46.2 3.4 %collective-permute-start.7 = (bf16[96,1024]{1,0:T(8,128)(2,1)S(1)}, bf16[96,1024]{1,0:T(8,128)(2,1)S(1)}, u32[]{:S(2)}, u32[]{:S(2)}) collective-permute-start(bf16[96,1024]{1,0:T(8,128)(2,1)S(1)} %collective-permute-done.6.refs_3_.refs_4_), channel_id=1, source_target_pairs={{0,8},{8,12},{12,4},{4,0},{1,9},{9,13},{13,5},{5,1},{2,10},{10,14}... | collective-permute-start | bytes 589832 | tf_op jit(solution)/shard_map/ppermute | solution.py:363
  49.6 1.3 %early_grad.3.refs_5_ = f32[2048,1024]{1,0:T(8,128)S(1)} custom-call(bf16[96,2048]{1,0:T(8,128)(2,1)S(1)} %get-tuple-element.25.refs_0_, bf16[96,2048]{1,0:T(8,128)(2,1)S(1)} %get-tuple-element.26.table_ref.refs_1_, bf16[96,1024]{1,0:T(8,128)(2,1)S(1)} %get-tuple-element.31.refs_2_, bf16[96,1024]{1,0:T(8,128)(2,1)S(1)} %collective-permute-done.9.refs_3_.refs_4_), custom_call_target="tpu_custom_call" | custom-call | bytes 1048576 | tf_op jit(solution)/shard_map/early_grad/pallas_call | solution.py:293
  50.9 1.3 %early_grad.2.refs_5_ = f32[2048,1024]{1,0:T(8,128)S(1)} custom-call(bf16[96,2048]{1,0:T(8,128)(2,1)S(1)} %get-tuple-element.25.refs_0_, bf16[96,2048]{1,0:T(8,128)(2,1)S(1)} %get-tuple-element.26.table_ref.refs_1_, bf16[96,1024]{1,0:T(8,128)(2,1)S(1)} %step_b.5.refs_2_, bf16[96,1024]{1,0:T(8,128)(2,1)S(1)} %collective-permute-done.6.refs_3_.refs_4_), custom_call_target="tpu_custom_call" | custom-call | bytes 1048576 | tf_op jit(solution)/shard_map/early_grad/pallas_call | solution.py:293
  52.2 0.0 collective-permute-done.10.refs_2_
  52.2 1.9 %collective-permute-start.11 = (bf16[96,1024]{1,0:T(8,128)(2,1)S(1)}, bf16[96,1024]{1,0:T(8,128)(2,1)S(1)}, u32[]{:S(2)}, u32[]{:S(2)}) collective-permute-start(bf16[96,1024]{1,0:T(8,128)(2,1)S(1)} %collective-permute-done.10.refs_2_), channel_id=1, source_target_pairs={{0,8},{8,12},{12,4},{4,0},{1,9},{9,13},{13,5},{5,1},{2,10},{10,14}... | collective-permute-start | bytes 589832 | tf_op jit(solution)/shard_map/ppermute | solution.py:363
  54.1 0.8 %collective-permute-done.7.refs_2_ = bf16[96,1024]{1,0:T(8,128)(2,1)S(1)} collective-permute-done((bf16[96,1024]{1,0:T(8,128)(2,1)S(1)}, bf16[96,1024]{1,0:T(8,128)(2,1)S(1)}, u32[]{:S(2)}, u32[]{:S(2)}) %collective-permute-start.7) | collective-permute-done | bytes 196640 | tf_op jit(solution)/shard_map/ppermute | solution.py:363
  54.9 3.4 %collective-permute-start.8 = (bf16[96,1024]{1,0:T(8,128)(2,1)S(1)}, bf16[96,1024]{1,0:T(8,128)(2,1)S(1)}, u32[]{:S(2)}, u32[]{:S(2)}) collective-permute-start(bf16[96,1024]{1,0:T(8,128)(2,1)S(1)} %collective-permute-done.7.refs_2_), channel_id=1, source_target_pairs={{0,8},{8,12},{12,4},{4,0},{1,9},{9,13},{13,5},{5,1},{2,10},{10,14}... | collective-permute-start | bytes 589832 | tf_op jit(solution)/shard_map/ppermute | solution.py:363
  58.3 0.1 collective-permute-done.11.refs_3_
  58.4 2.4 %grad.2 = (bf16[96,2048]{1,0:T(8,128)(2,1)}, bf16[2048,2048]{1,0:T(8,128)(2,1)}) custom-call(bf16[96,2048]{1,0:T(8,128)(2,1)S(1)} %get-tuple-element.21.refs_0_, bf16[96,2048]{1,0:T(8,128)(2,1)S(1)} %get-tuple-element.23.refs_0_.refs_1_, bf16[96,1024]{1,0:T(8,128)(2,1)S(1)} %collective-permute-done.10.refs_2_, ...), custom_call_target="tpu_custom_call" | custom-call | bytes 1048576 | tf_op jit(solution)/shard_map/grad/pallas_call | solution.py:336
  60.9 0.7 %collective-permute-done.8.refs_3_ = bf16[96,1024]{1,0:T(8,128)(2,1)S(1)} collective-permute-done((bf16[96,1024]{1,0:T(8,128)(2,1)S(1)}, bf16[96,1024]{1,0:T(8,128)(2,1)S(1)}, u32[]{:S(2)}, u32[]{:S(2)}) %collective-permute-start.8) | collective-permute-done | bytes 196640 | tf_op jit(solution)/shard_map/ppermute | solution.py:363
  61.5 2.4 %grad.3 = (bf16[96,2048]{1,0:T(8,128)(2,1)}, bf16[2048,2048]{1,0:T(8,128)(2,1)}) custom-call(bf16[96,2048]{1,0:T(8,128)(2,1)S(1)} %get-tuple-element.21.refs_0_, bf16[96,2048]{1,0:T(8,128)(2,1)S(1)} %get-tuple-element.23.refs_0_.refs_1_, bf16[96,1024]{1,0:T(8,128)(2,1)S(1)} %collective-permute-done.7.refs_2_, ...), custom_call_target="tpu_custom_call", output_to_operand_aliasing={{0}: (6, {}), {1}: (7, {})} | custom-call | bytes 1048576 | tf_op jit(solution)/shard_map/grad/pallas_call | solution.py:336
Async XLA Ops:
  0.6 12.2 %copy-start = (f32[2048]{0:T(1024)S(1)}, f32[2048]{0:T(1024)}, u32[]{:S(2)}) copy-start(f32[2048]{0:T(1024)} %param.8) | copy-start | bytes 24580
  3.3 9.5 %collective-permute-start = (bf16[96,1152]{1,0:T(8,128)(2,1)S(1)}, bf16[96,1152]{1,0:T(8,128)(2,1)S(1)}, u32[]{:S(2)}, u32[]{:S(2)}) collective-permute-start(bf16[96,1152]{1,0:T(8,128)(2,1)S(1)} %get-tuple-element.19), channel_id=1, source_target_pairs={{0,8},{8,12},{12,4},{4,0},{1,9},{9,13},{13,5},{5,1},{2,10},{10,14}... | collective-permute-start | bytes 663560 | tf_op jit(solution)/shard_map/ppermute | solution.py:363
  10.0 7.7 %collective-permute-start.3 = (bf16[96,1024]{1,0:T(8,128)(2,1)S(1)}, bf16[96,1024]{1,0:T(8,128)(2,1)S(1)}, u32[]{:S(2)}, u32[]{:S(2)}) collective-permute-start(bf16[96,1024]{1,0:T(8,128)(2,1)S(1)} %get-tuple-element.27), channel_id=1, source_target_pairs={{0,8},{8,12},{12,4},{4,0},{1,9},{9,13},{13,5},{5,1},{2,10},{10,14}... | collective-permute-start | bytes 589832 | tf_op jit(solution)/shard_map/ppermute | solution.py:363
  14.2 8.7 %collective-permute-start.1 = (bf16[96,1152]{1,0:T(8,128)(2,1)S(1)}, bf16[96,1152]{1,0:T(8,128)(2,1)S(1)}, u32[]{:S(2)}, u32[]{:S(2)}) collective-permute-start(bf16[96,1152]{1,0:T(8,128)(2,1)S(1)} %get-tuple-element.22), channel_id=1, source_target_pairs={{0,8},{8,12},{12,4},{4,0},{1,9},{9,13},{13,5},{5,1},{2,10},{10,14}... | collective-permute-start | bytes 663560 | tf_op jit(solution)/shard_map/ppermute | solution.py:363
  18.4 8.5 %collective-permute-start.4 = (bf16[96,1024]{1,0:T(8,128)(2,1)S(1)}, bf16[96,1024]{1,0:T(8,128)(2,1)S(1)}, u32[]{:S(2)}, u32[]{:S(2)}) collective-permute-start(bf16[96,1024]{1,0:T(8,128)(2,1)S(1)} %step_b.3), channel_id=1, source_target_pairs={{0,8},{8,12},{12,4},{4,0},{1,9},{9,13},{13,5},{5,1},{2,10},{10,14}... | collective-permute-start | bytes 589832 | tf_op jit(solution)/shard_map/ppermute | solution.py:363
  24.3 8.2 %collective-permute-start.2 = (bf16[96,1152]{1,0:T(8,128)(2,1)S(1)}, bf16[96,1152]{1,0:T(8,128)(2,1)S(1)}, u32[]{:S(2)}, u32[]{:S(2)}) collective-permute-start(bf16[96,1152]{1,0:T(8,128)(2,1)S(1)} %get-tuple-element.24), channel_id=1, source_target_pairs={{0,8},{8,12},{12,4},{4,0},{1,9},{9,13},{13,5},{5,1},{2,10},{10,14}... | collective-permute-start | bytes 663560 | tf_op jit(solution)/shard_map/ppermute | solution.py:363
  27.8 9.0 %collective-permute-start.5 = (bf16[96,1024]{1,0:T(8,128)(2,1)S(1)}, bf16[96,1024]{1,0:T(8,128)(2,1)S(1)}, u32[]{:S(2)}, u32[]{:S(2)}) collective-permute-start(bf16[96,1024]{1,0:T(8,128)(2,1)S(1)} %step_b.4), channel_id=1, source_target_pairs={{0,8},{8,12},{12,4},{4,0},{1,9},{9,13},{13,5},{5,1},{2,10},{10,14}... | collective-permute-start | bytes 589832 | tf_op jit(solution)/shard_map/ppermute | solution.py:363
  33.8 8.2 %collective-permute-start.9 = (bf16[96,1024]{1,0:T(8,128)(2,1)S(1)}, bf16[96,1024]{1,0:T(8,128)(2,1)S(1)}, u32[]{:S(2)}, u32[]{:S(2)}) collective-permute-start(bf16[96,1024]{1,0:T(8,128)(2,1)S(1)} %get-tuple-element.31.refs_2_), channel_id=1, source_target_pairs={{0,8},{8,12},{12,4},{4,0},{1,9},{9,13},{13,5},{5,1},{2,10},{10,14}... | collective-permute-start | bytes 589832 | tf_op jit(solution)/shard_map/ppermute | solution.py:363
  37.6 8.6 %collective-permute-start.6 = (bf16[96,1024]{1,0:T(8,128)(2,1)S(1)}, bf16[96,1024]{1,0:T(8,128)(2,1)S(1)}, u32[]{:S(2)}, u32[]{:S(2)}) collective-permute-start(bf16[96,1024]{1,0:T(8,128)(2,1)S(1)} %step_b.5.refs_2_), channel_id=1, source_target_pairs={{0,8},{8,12},{12,4},{4,0},{1,9},{9,13},{13,5},{5,1},{2,10},{10,14}... | collective-permute-start | bytes 589832 | tf_op jit(solution)/shard_map/ppermute | solution.py:363
  42.0 10.2 %collective-permute-start.10 = (bf16[96,1024]{1,0:T(8,128)(2,1)S(1)}, bf16[96,1024]{1,0:T(8,128)(2,1)S(1)}, u32[]{:S(2)}, u32[]{:S(2)}) collective-permute-start(bf16[96,1024]{1,0:T(8,128)(2,1)S(1)} %collective-permute-done.9.refs_3_.refs_4_), channel_id=1, source_target_pairs={{0,8},{8,12},{12,4},{4,0},{1,9},{9,13},{13,5},{5,1},{2,10},{10,14}... | collective-permute-start | bytes 589832 | tf_op jit(solution)/shard_map/ppermute | solution.py:363
  46.2 8.7 %collective-permute-start.7 = (bf16[96,1024]{1,0:T(8,128)(2,1)S(1)}, bf16[96,1024]{1,0:T(8,128)(2,1)S(1)}, u32[]{:S(2)}, u32[]{:S(2)}) collective-permute-start(bf16[96,1024]{1,0:T(8,128)(2,1)S(1)} %collective-permute-done.6.refs_3_.refs_4_), channel_id=1, source_target_pairs={{0,8},{8,12},{12,4},{4,0},{1,9},{9,13},{13,5},{5,1},{2,10},{10,14}... | collective-permute-start | bytes 589832 | tf_op jit(solution)/shard_map/ppermute | solution.py:363
  52.2 6.3 %collective-permute-start.11 = (bf16[96,1024]{1,0:T(8,128)(2,1)S(1)}, bf16[96,1024]{1,0:T(8,128)(2,1)S(1)}, u32[]{:S(2)}, u32[]{:S(2)}) collective-permute-start(bf16[96,1024]{1,0:T(8,128)(2,1)S(1)} %collective-permute-done.10.refs_2_), channel_id=1, source_target_pairs={{0,8},{8,12},{12,4},{4,0},{1,9},{9,13},{13,5},{5,1},{2,10},{10,14}... | collective-permute-start | bytes 589832 | tf_op jit(solution)/shard_map/ppermute | solution.py:363
  54.9 6.6 %collective-permute-start.8 = (bf16[96,1024]{1,0:T(8,128)(2,1)S(1)}, bf16[96,1024]{1,0:T(8,128)(2,1)S(1)}, u32[]{:S(2)}, u32[]{:S(2)}) collective-permute-start(bf16[96,1024]{1,0:T(8,128)(2,1)S(1)} %collective-permute-done.7.refs_2_), channel_id=1, source_target_pairs={{0,8},{8,12},{12,4},{4,0},{1,9},{9,13},{13,5},{5,1},{2,10},{10,14}... | collective-permute-start | bytes 589832 | tf_op jit(solution)/shard_map/ppermute | solution.py:363

commit v7 on v6

--- a/solution.py
+++ b/solution.py
@@ -217,21 +217,16 @@
     )(table, in_hbm(weight), in_hbm(tokens))
 
 
-def step_kernel(column0, builds, last, *refs):
-    if builds:
-        first_ref, arrived_ref, weight_ref, bias_ref, table_ref, out_ref, keys_ref = refs
-    else:
-        table_ref, arrived_ref, weight_ref, bias_ref, out_ref = refs
+def step_kernel(last, first_ref, arrived_ref, weight_ref, bias_ref, table_ref, out_ref, keys_ref):
     columns = weight_ref.shape[1]
-    if builds:
-        build_table(first_ref[0], arrived_ref[:, columns:].astype(jnp.float32), table_ref, keys_ref)
-        if not last:
-            out_ref[:, columns:] = arrived_ref[:, columns:]
+    build_table(first_ref[0], arrived_ref[:, columns:].astype(jnp.float32), table_ref, keys_ref)
+    if not last:
+        out_ref[:, columns:] = arrived_ref[:, columns:]
 
     def write(at, product):
         total = product + arrived_ref[:, at].astype(jnp.float32)
         if last:
-            total = total + bias_ref[:, column0 + at.start : column0 + at.stop]
+            total = total + bias_ref[:, at]
         out_ref[:, at] = total.astype(out_ref.dtype)
 
     multiply(table_ref, weight_ref, write)
@@ -241,7 +236,7 @@
     width, columns = weight.shape
     rows = arrived.shape[0]
     return pl.pallas_call(
-        functools.partial(step_kernel, 0, True, last),
+        functools.partial(step_kernel, last),
         in_specs=[IN_SMEM] + [IN_VMEM] * 3,
         out_specs=[IN_VMEM] * 2,
         out_shape=[
@@ -255,16 +250,40 @@
     )(first, arrived, weight, bias)
 
 
+def multiply_kernel(table_ref, weight_ref, out_ref):
+    def write(at, product):
+        out_ref[:, at] = product
+
+    multiply(table_ref, weight_ref, write)
+
+
+def add_kernel(column0, last, part_ref, arrived_ref, bias_ref, out_ref):
+    total = part_ref[...] + arrived_ref[...].astype(jnp.float32)
+    if last:
+        total = total + bias_ref[:, column0 : column0 + part_ref.shape[1]]
+    out_ref[...] = total.astype(out_ref.dtype)
+
+
 def step_b(table, arrived, weight, bias, column0, last):
-    return pl.pallas_call(
-        functools.partial(step_kernel, column0, False, last),
-        in_specs=[IN_VMEM] * 4,
+    shape = arrived.shape
+    part = pl.pallas_call(
+        multiply_kernel,
+        in_specs=[IN_VMEM] * 2,
         out_specs=IN_VMEM,
-        out_shape=jax.ShapeDtypeStruct(arrived.shape, jnp.bfloat16),
-        compiler_params=params(),
-        cost_estimate=cost(1 << 20),
-        name="step_b",
-    )(table, arrived, weight, bias)
+        out_shape=jax.ShapeDtypeStruct(shape, jnp.float32),
+        compiler_params=params(),
+        cost_estimate=cost(1 << 20),
+        name="multiply",
+    )(table, weight)
+    return pl.pallas_call(
+        functools.partial(add_kernel, column0, last),
+        in_specs=[IN_VMEM] * 3,
+        out_specs=IN_VMEM,
+        out_shape=jax.ShapeDtypeStruct(shape, jnp.bfloat16),
+        compiler_params=params(),
+        cost_estimate=cost(1 << 20),
+        name="add",
+    )(part, arrived, bias)
 
 
 def contract_tokens(tables, all_ref, at):

time: 64.2 us -> 63.6 us (level)
  starting transfers between devices: 34.8 us -> 32.6 us
  waiting for transfers between devices: 9.31 us -> 10.8 us
    ppermute x12, starting transfers between devices: 34.8 us -> 32.6 us  [send(): return lax.ppermute(x, 'latent', ring_next(count))]
    ppermute x12, waiting for transfers between devices: 9.31 us -> 10.8 us  [send(): return lax.ppermute(x, 'latent', ring_next(count))]
    pallas_call x6 -> x9, Pallas kernels: 6.46 us -> 6.59 us  [the longest x3 4.03 us: step_a(): pl.pallas_call(functools.partial(step_kernel, last), in_specs=[IN_SMEM] +...]
  transfers between devices with their start and end apart: 12 -> 12, of which waited for: 9 -> 7; matrix products, arithmetic and copies ran while one was open for 0% -> 0% of each run, Pallas kernels for 22% -> 22%
where the time goes in v7:
time: 63.6 us; the launch traced here: 63.5 us
  starting transfers between devices  32.6 us (51%)
  Pallas kernels  19.2 us (30%)
  waiting for transfers between devices  10.8 us (17%)
  between operations  0.9 us (1%)
    ppermute x12, starting transfers between devices, send(): return lax.ppermute(x, 'latent', ring_next(count))  32.6 us
    ppermute x12, waiting for transfers between devices, send(): return lax.ppermute(x, 'latent', ring_next(count))  10.8 us
    pallas_call x2, Pallas kernels, grad_part(): pl.pallas_call(functools.partial(grad_kernel, blocks, column0, tile), in_...  4.82 us
    pallas_call x3, Pallas kernels, step_a(): pl.pallas_call(functools.partial(step_kernel, last), in_specs=[IN_SMEM] +...  4.03 us
    pallas_call x1, Pallas kernels, begin(): pl.pallas_call(begin_kernel, in_specs=[IN_SMEM] + [IN_HBM] * 4, out_specs...  2.65 us
    pallas_call x2, Pallas kernels, early_grad(): pl.pallas_call(functools.partial(early_kernel, blocks, tile), in_specs=[I...  2.58 us
    pallas_call x1, Pallas kernels, second(): pl.pallas_call(functools.partial(second_kernel, column0), in_specs=[IN_VM...  2.56 us
    pallas_call x3, Pallas kernels, step_b(): pl.pallas_call(multiply_kernel, in_specs=[IN_VMEM] * 2, out_specs=IN_VMEM...  2.4 us
  transfers between devices with their start and end apart: 12, of which 7 were waited for; matrix products, arithmetic and copies ran while one was open for 0% of the time, Pallas kernels for 22%

profile of v7, /device:TPU:0, one launch (start us, length us, event | category | flops | bytes accessed | tf_op | source)
XLA Modules:
  0.0 63.5 jit_solution(9684408729180599871)
XLA Ops:
  0.6 0.0 copy-start
  0.6 2.6 %begin.1 = (bf16[2048,1024]{1,0:T(8,128)(2,1)S(1)}, bf16[96,2048]{1,0:T(8,128)(2,1)S(1)}, bf16[96,1152]{1,0:T(8,128)(2,1)S(1)}) custom-call(s32[1]{0:T(128)} %bitcast.first_ref, s32[64,96]{1,0:T(8,128)} %bitcast.10, bf16[64,96]{1,0:T(8,128)(2,1)} %bitcast.11, bf16[2048,2048]{1,0:T(8,128)(2,1)} %weight_hbm.3, bf16[96,2048]{1,0:T(8,128)(2,1)} %tokens_hbm.3), custom_call_target="tpu_custom_call" | custom-call | bytes 1048576 | tf_op jit(solution)/shard_map/begin/pallas_call | solution.py:171
  3.3 4.1 %collective-permute-start = (bf16[96,1152]{1,0:T(8,128)(2,1)S(1)}, bf16[96,1152]{1,0:T(8,128)(2,1)S(1)}, u32[]{:S(2)}, u32[]{:S(2)}) collective-permute-start(bf16[96,1152]{1,0:T(8,128)(2,1)S(1)} %get-tuple-element.19), channel_id=1, source_target_pairs={{0,8},{8,12},{12,4},{4,0},{1,9},{9,13},{13,5},{5,1},{2,10},{10,14}... | collective-permute-start | bytes 663560 | tf_op jit(solution)/shard_map/ppermute | solution.py:382
  7.4 2.6 %second.1 = (bf16[2048,1024]{1,0:T(8,128)(2,1)S(1)}, bf16[96,1024]{1,0:T(8,128)(2,1)S(1)}) custom-call(bf16[96,2048]{1,0:T(8,128)(2,1)S(1)} %get-tuple-element.26.table_ref.refs_1_, bf16[2048,2048]{1,0:T(8,128)(2,1)} %weight_hbm.3, bf16[96,2048]{1,0:T(8,128)(2,1)} %tokens_hbm.3), custom_call_target="tpu_custom_call" | custom-call | bytes 1048576 | tf_op jit(solution)/shard_map/second/pallas_call | solution.py:202
  10.0 1.6 %collective-permute-start.3 = (bf16[96,1024]{1,0:T(8,128)(2,1)S(1)}, bf16[96,1024]{1,0:T(8,128)(2,1)S(1)}, u32[]{:S(2)}, u32[]{:S(2)}) collective-permute-start(bf16[96,1024]{1,0:T(8,128)(2,1)S(1)} %get-tuple-element.28), channel_id=1, source_target_pairs={{0,8},{8,12},{12,4},{4,0},{1,9},{9,13},{13,5},{5,1},{2,10},{10,14}... | collective-permute-start | bytes 589832 | tf_op jit(solution)/shard_map/ppermute | solution.py:382
  11.6 1.2 %collective-permute-done.arrived_ref = bf16[96,1152]{1,0:T(8,128)(2,1)S(1)} collective-permute-done((bf16[96,1152]{1,0:T(8,128)(2,1)S(1)}, bf16[96,1152]{1,0:T(8,128)(2,1)S(1)}, u32[]{:S(2)}, u32[]{:S(2)}) %collective-permute-start) | collective-permute-done | bytes 221216 | tf_op jit(solution)/shard_map/ppermute | solution.py:382
  12.8 0.0 copy-done
  12.8 1.3 %step_a.3 = (bf16[96,2048]{1,0:T(8,128)(2,1)S(1)}, bf16[96,1152]{1,0:T(8,128)(2,1)S(1)}) custom-call(s32[1]{0:T(128)} %bitcast.first_ref, bf16[96,1152]{1,0:T(8,128)(2,1)S(1)} %collective-permute-done.arrived_ref, bf16[2048,1024]{1,0:T(8,128)(2,1)S(1)} %get-tuple-element.20.weight_ref, f32[1,2048]{1,0:T(1,128)S(1)} %bitcast.4), custom_call_target="tpu_custom_call" | custom-call | bytes 1048576 | tf_op jit(solution)/shard_map/step_a/pallas_call | solution.py:238
  14.2 3.4 %collective-permute-start.1 = (bf16[96,1152]{1,0:T(8,128)(2,1)S(1)}, bf16[96,1152]{1,0:T(8,128)(2,1)S(1)}, u32[]{:S(2)}, u32[]{:S(2)}) collective-permute-start(bf16[96,1152]{1,0:T(8,128)(2,1)S(1)} %get-tuple-element.22), channel_id=1, source_target_pairs={{0,8},{8,12},{12,4},{4,0},{1,9},{9,13},{13,5},{5,1},{2,10},{10,14}... | collective-permute-start | bytes 663560 | tf_op jit(solution)/shard_map/ppermute | solution.py:382
  17.6 0.8 %multiply.5.part_ref = f32[96,1024]{1,0:T(8,128)S(1)} custom-call(bf16[96,2048]{1,0:T(8,128)(2,1)S(1)} %get-tuple-element.21.table_ref.refs_0_, bf16[2048,1024]{1,0:T(8,128)(2,1)S(1)} %get-tuple-element.27.weight_ref), custom_call_target="tpu_custom_call" | custom-call | bytes 1048576 | tf_op jit(solution)/shard_map/multiply/pallas_call | solution.py:269
  18.4 0.0 collective-permute-done.3.arrived_ref
  18.4 0.1 add.3
  18.5 1.6 %collective-permute-start.4 = (bf16[96,1024]{1,0:T(8,128)(2,1)S(1)}, bf16[96,1024]{1,0:T(8,128)(2,1)S(1)}, u32[]{:S(2)}, u32[]{:S(2)}) collective-permute-start(bf16[96,1024]{1,0:T(8,128)(2,1)S(1)} %add.3), channel_id=1, source_target_pairs={{0,8},{8,12},{12,4},{4,0},{1,9},{9,13},{13,5},{5,1},{2,10},{10,14}... | collective-permute-start | bytes 589832 | tf_op jit(solution)/shard_map/ppermute | solution.py:382
  20.1 3.1 %collective-permute-done.1.arrived_ref = bf16[96,1152]{1,0:T(8,128)(2,1)S(1)} collective-permute-done((bf16[96,1152]{1,0:T(8,128)(2,1)S(1)}, bf16[96,1152]{1,0:T(8,128)(2,1)S(1)}, u32[]{:S(2)}, u32[]{:S(2)}) %collective-permute-start.1) | collective-permute-done | bytes 221216 | tf_op jit(solution)/shard_map/ppermute | solution.py:382
  23.2 1.3 %step_a.4 = (bf16[96,2048]{1,0:T(8,128)(2,1)S(1)}, bf16[96,1152]{1,0:T(8,128)(2,1)S(1)}) custom-call(s32[1]{0:T(128)} %bitcast.first_ref, bf16[96,1152]{1,0:T(8,128)(2,1)S(1)} %collective-permute-done.1.arrived_ref, bf16[2048,1024]{1,0:T(8,128)(2,1)S(1)} %get-tuple-element.20.weight_ref, f32[1,2048]{1,0:T(1,128)S(1)} %bitcast.6), custom_call_target="tpu_custom_call" | custom-call | bytes 1048576 | tf_op jit(solution)/shard_map/step_a/pallas_call | solution.py:238
  24.5 3.2 %collective-permute-start.2 = (bf16[96,1152]{1,0:T(8,128)(2,1)S(1)}, bf16[96,1152]{1,0:T(8,128)(2,1)S(1)}, u32[]{:S(2)}, u32[]{:S(2)}) collective-permute-start(bf16[96,1152]{1,0:T(8,128)(2,1)S(1)} %get-tuple-element.24), channel_id=1, source_target_pairs={{0,8},{8,12},{12,4},{4,0},{1,9},{9,13},{13,5},{5,1},{2,10},{10,14}... | collective-permute-start | bytes 663560 | tf_op jit(solution)/shard_map/ppermute | solution.py:382
  27.7 0.8 %multiply.4.part_ref = f32[96,1024]{1,0:T(8,128)S(1)} custom-call(bf16[96,2048]{1,0:T(8,128)(2,1)S(1)} %get-tuple-element.23.table_ref.refs_1_, bf16[2048,1024]{1,0:T(8,128)(2,1)S(1)} %get-tuple-element.27.weight_ref), custom_call_target="tpu_custom_call" | custom-call | bytes 1048576 | tf_op jit(solution)/shard_map/multiply/pallas_call | solution.py:269
  28.5 0.0 collective-permute-done.4.arrived_ref
  28.5 0.1 add.4
  28.6 2.1 %collective-permute-start.5 = (bf16[96,1024]{1,0:T(8,128)(2,1)S(1)}, bf16[96,1024]{1,0:T(8,128)(2,1)S(1)}, u32[]{:S(2)}, u32[]{:S(2)}) collective-permute-start(bf16[96,1024]{1,0:T(8,128)(2,1)S(1)} %add.4), channel_id=1, source_target_pairs={{0,8},{8,12},{12,4},{4,0},{1,9},{9,13},{13,5},{5,1},{2,10},{10,14}... | collective-permute-start | bytes 589832 | tf_op jit(solution)/shard_map/ppermute | solution.py:382
  30.7 1.5 %collective-permute-done.2.arrived_ref = bf16[96,1152]{1,0:T(8,128)(2,1)S(1)} collective-permute-done((bf16[96,1152]{1,0:T(8,128)(2,1)S(1)}, bf16[96,1152]{1,0:T(8,128)(2,1)S(1)}, u32[]{:S(2)}, u32[]{:S(2)}) %collective-permute-start.2) | collective-permute-done | bytes 221216 | tf_op jit(solution)/shard_map/ppermute | solution.py:382
  32.2 1.3 %step_a.5 = (bf16[96,2048]{1,0:T(8,128)(2,1)S(1)}, bf16[96,1024]{1,0:T(8,128)(2,1)S(1)}) custom-call(s32[1]{0:T(128)} %bitcast.first_ref, bf16[96,1152]{1,0:T(8,128)(2,1)S(1)} %collective-permute-done.2.arrived_ref, bf16[2048,1024]{1,0:T(8,128)(2,1)S(1)} %get-tuple-element.20.weight_ref, f32[1,2048]{1,0:T(1,128)S(1)} %bitcast.8), custom_call_target="tpu_custom_call" | custom-call | bytes 1048576 | tf_op jit(solution)/shard_map/step_a/pallas_call | solution.py:238
  33.5 3.4 %collective-permute-start.9 = (bf16[96,1024]{1,0:T(8,128)(2,1)S(1)}, bf16[96,1024]{1,0:T(8,128)(2,1)S(1)}, u32[]{:S(2)}, u32[]{:S(2)}) collective-permute-start(bf16[96,1024]{1,0:T(8,128)(2,1)S(1)} %get-tuple-element.31.refs_2_), channel_id=1, source_target_pairs={{0,8},{8,12},{12,4},{4,0},{1,9},{9,13},{13,5},{5,1},{2,10},{10,14}... | collective-permute-start | bytes 589832 | tf_op jit(solution)/shard_map/ppermute | solution.py:382
  36.9 0.8 %multiply.3.part_ref = f32[96,1024]{1,0:T(8,128)S(1)} custom-call(bf16[96,2048]{1,0:T(8,128)(2,1)S(1)} %get-tuple-element.25.table_ref.refs_0_, bf16[2048,1024]{1,0:T(8,128)(2,1)S(1)} %get-tuple-element.27.weight_ref), custom_call_target="tpu_custom_call" | custom-call | bytes 1048576 | tf_op jit(solution)/shard_map/multiply/pallas_call | solution.py:269
  37.7 0.0 collective-permute-done.5.arrived_ref
  37.7 0.1 add.5.refs_2_
  37.8 1.7 %collective-permute-start.6 = (bf16[96,1024]{1,0:T(8,128)(2,1)S(1)}, bf16[96,1024]{1,0:T(8,128)(2,1)S(1)}, u32[]{:S(2)}, u32[]{:S(2)}) collective-permute-start(bf16[96,1024]{1,0:T(8,128)(2,1)S(1)} %add.5.refs_2_), channel_id=1, source_target_pairs={{0,8},{8,12},{12,4},{4,0},{1,9},{9,13},{13,5},{5,1},{2,10},{10,14}... | collective-permute-start | bytes 589832 | tf_op jit(solution)/shard_map/ppermute | solution.py:382
  39.5 2.2 %collective-permute-done.9.refs_3_.refs_4_ = bf16[96,1024]{1,0:T(8,128)(2,1)S(1)} collective-permute-done((bf16[96,1024]{1,0:T(8,128)(2,1)S(1)}, bf16[96,1024]{1,0:T(8,128)(2,1)S(1)}, u32[]{:S(2)}, u32[]{:S(2)}) %collective-permute-start.9) | collective-permute-done | bytes 196640 | tf_op jit(solution)/shard_map/ppermute | solution.py:382
  41.7 3.1 %collective-permute-start.10 = (bf16[96,1024]{1,0:T(8,128)(2,1)S(1)}, bf16[96,1024]{1,0:T(8,128)(2,1)S(1)}, u32[]{:S(2)}, u32[]{:S(2)}) collective-permute-start(bf16[96,1024]{1,0:T(8,128)(2,1)S(1)} %collective-permute-done.9.refs_3_.refs_4_), channel_id=1, source_target_pairs={{0,8},{8,12},{12,4},{4,0},{1,9},{9,13},{13,5},{5,1},{2,10},{10,14}... | collective-permute-start | bytes 589832 | tf_op jit(solution)/shard_map/ppermute | solution.py:382
  44.8 1.1 %collective-permute-done.6.refs_3_.refs_4_ = bf16[96,1024]{1,0:T(8,128)(2,1)S(1)} collective-permute-done((bf16[96,1024]{1,0:T(8,128)(2,1)S(1)}, bf16[96,1024]{1,0:T(8,128)(2,1)S(1)}, u32[]{:S(2)}, u32[]{:S(2)}) %collective-permute-start.6) | collective-permute-done | bytes 196640 | tf_op jit(solution)/shard_map/ppermute | solution.py:382
  45.9 3.1 %collective-permute-start.7 = (bf16[96,1024]{1,0:T(8,128)(2,1)S(1)}, bf16[96,1024]{1,0:T(8,128)(2,1)S(1)}, u32[]{:S(2)}, u32[]{:S(2)}) collective-permute-start(bf16[96,1024]{1,0:T(8,128)(2,1)S(1)} %collective-permute-done.6.refs_3_.refs_4_), channel_id=1, source_target_pairs={{0,8},{8,12},{12,4},{4,0},{1,9},{9,13},{13,5},{5,1},{2,10},{10,14}... | collective-permute-start | bytes 589832 | tf_op jit(solution)/shard_map/ppermute | solution.py:382
  49.0 1.3 %early_grad.3.refs_5_ = f32[2048,1024]{1,0:T(8,128)S(1)} custom-call(bf16[96,2048]{1,0:T(8,128)(2,1)S(1)} %get-tuple-element.25.table_ref.refs_0_, bf16[96,2048]{1,0:T(8,128)(2,1)S(1)} %get-tuple-element.26.table_ref.refs_1_, bf16[96,1024]{1,0:T(8,128)(2,1)S(1)} %get-tuple-element.31.refs_2_, bf16[96,1024]{1,0:T(8,128)(2,1)S(1)} %collective-permute-done.9.refs_3_.refs_4_), custom_call_target="tpu_custom_call" | custom-call | bytes 1048576 | tf_op jit(solution)/shard_map/early_grad/pallas_call | solution.py:312
  50.3 1.3 %early_grad.2.refs_5_ = f32[2048,1024]{1,0:T(8,128)S(1)} custom-call(bf16[96,2048]{1,0:T(8,128)(2,1)S(1)} %get-tuple-element.25.table_ref.refs_0_, bf16[96,2048]{1,0:T(8,128)(2,1)S(1)} %get-tuple-element.26.table_ref.refs_1_, bf16[96,1024]{1,0:T(8,128)(2,1)S(1)} %add.5.refs_2_, bf16[96,1024]{1,0:T(8,128)(2,1)S(1)} %collective-permute-done.6.refs_3_.refs_4_), custom_call_target="tpu_custom_call" | custom-call | bytes 1048576 | tf_op jit(solution)/shard_map/early_grad/pallas_call | solution.py:312
  51.6 0.0 collective-permute-done.10.refs_2_
  51.6 1.9 %collective-permute-start.11 = (bf16[96,1024]{1,0:T(8,128)(2,1)S(1)}, bf16[96,1024]{1,0:T(8,128)(2,1)S(1)}, u32[]{:S(2)}, u32[]{:S(2)}) collective-permute-start(bf16[96,1024]{1,0:T(8,128)(2,1)S(1)} %collective-permute-done.10.refs_2_), channel_id=1, source_target_pairs={{0,8},{8,12},{12,4},{4,0},{1,9},{9,13},{13,5},{5,1},{2,10},{10,14}... | collective-permute-start | bytes 589832 | tf_op jit(solution)/shard_map/ppermute | solution.py:382
  53.5 0.8 %collective-permute-done.7.refs_2_ = bf16[96,1024]{1,0:T(8,128)(2,1)S(1)} collective-permute-done((bf16[96,1024]{1,0:T(8,128)(2,1)S(1)}, bf16[96,1024]{1,0:T(8,128)(2,1)S(1)}, u32[]{:S(2)}, u32[]{:S(2)}) %collective-permute-start.7) | collective-permute-done | bytes 196640 | tf_op jit(solution)/shard_map/ppermute | solution.py:382
  54.3 3.4 %collective-permute-start.8 = (bf16[96,1024]{1,0:T(8,128)(2,1)S(1)}, bf16[96,1024]{1,0:T(8,128)(2,1)S(1)}, u32[]{:S(2)}, u32[]{:S(2)}) collective-permute-start(bf16[96,1024]{1,0:T(8,128)(2,1)S(1)} %collective-permute-done.7.refs_2_), channel_id=1, source_target_pairs={{0,8},{8,12},{12,4},{4,0},{1,9},{9,13},{13,5},{5,1},{2,10},{10,14}... | collective-permute-start | bytes 589832 | tf_op jit(solution)/shard_map/ppermute | solution.py:382
  57.7 0.0 collective-permute-done.11.refs_3_
  57.7 2.4 %grad.2 = (bf16[96,2048]{1,0:T(8,128)(2,1)}, bf16[2048,2048]{1,0:T(8,128)(2,1)}) custom-call(bf16[96,2048]{1,0:T(8,128)(2,1)S(1)} %get-tuple-element.21.table_ref.refs_0_, bf16[96,2048]{1,0:T(8,128)(2,1)S(1)} %get-tuple-element.23.table_ref.refs_1_, bf16[96,1024]{1,0:T(8,128)(2,1)S(1)} %collective-permute-done.10.refs_2_, ...), custom_call_target="tpu_custom_call" | custom-call | bytes 1048576 | tf_op jit(solution)/shard_map/grad/pallas_call | solution.py:355
  60.1 0.8 %collective-permute-done.8.refs_3_ = bf16[96,1024]{1,0:T(8,128)(2,1)S(1)} collective-permute-done((bf16[96,1024]{1,0:T(8,128)(2,1)S(1)}, bf16[96,1024]{1,0:T(8,128)(2,1)S(1)}, u32[]{:S(2)}, u32[]{:S(2)}) %collective-permute-start.8) | collective-permute-done | bytes 196640 | tf_op jit(solution)/shard_map/ppermute | solution.py:382
  60.9 2.4 %grad.3 = (bf16[96,2048]{1,0:T(8,128)(2,1)}, bf16[2048,2048]{1,0:T(8,128)(2,1)}) custom-call(bf16[96,2048]{1,0:T(8,128)(2,1)S(1)} %get-tuple-element.21.table_ref.refs_0_, bf16[96,2048]{1,0:T(8,128)(2,1)S(1)} %get-tuple-element.23.table_ref.refs_1_, ...), custom_call_target="tpu_custom_call", output_to_operand_aliasing={{0}: (6, {}), {1}: (7, {})} | custom-call | bytes 1048576 | tf_op jit(solution)/shard_map/grad/pallas_call | solution.py:355
Async XLA Ops:
  0.6 12.2 %copy-start = (f32[2048]{0:T(1024)S(1)}, f32[2048]{0:T(1024)}, u32[]{:S(2)}) copy-start(f32[2048]{0:T(1024)} %param.8) | copy-start | bytes 24580
  3.3 9.5 %collective-permute-start = (bf16[96,1152]{1,0:T(8,128)(2,1)S(1)}, bf16[96,1152]{1,0:T(8,128)(2,1)S(1)}, u32[]{:S(2)}, u32[]{:S(2)}) collective-permute-start(bf16[96,1152]{1,0:T(8,128)(2,1)S(1)} %get-tuple-element.19), channel_id=1, source_target_pairs={{0,8},{8,12},{12,4},{4,0},{1,9},{9,13},{13,5},{5,1},{2,10},{10,14}... | collective-permute-start | bytes 663560 | tf_op jit(solution)/shard_map/ppermute | solution.py:382
  10.0 8.5 %collective-permute-start.3 = (bf16[96,1024]{1,0:T(8,128)(2,1)S(1)}, bf16[96,1024]{1,0:T(8,128)(2,1)S(1)}, u32[]{:S(2)}, u32[]{:S(2)}) collective-permute-start(bf16[96,1024]{1,0:T(8,128)(2,1)S(1)} %get-tuple-element.28), channel_id=1, source_target_pairs={{0,8},{8,12},{12,4},{4,0},{1,9},{9,13},{13,5},{5,1},{2,10},{10,14}... | collective-permute-start | bytes 589832 | tf_op jit(solution)/shard_map/ppermute | solution.py:382
  14.2 9.0 %collective-permute-start.1 = (bf16[96,1152]{1,0:T(8,128)(2,1)S(1)}, bf16[96,1152]{1,0:T(8,128)(2,1)S(1)}, u32[]{:S(2)}, u32[]{:S(2)}) collective-permute-start(bf16[96,1152]{1,0:T(8,128)(2,1)S(1)} %get-tuple-element.22), channel_id=1, source_target_pairs={{0,8},{8,12},{12,4},{4,0},{1,9},{9,13},{13,5},{5,1},{2,10},{10,14}... | collective-permute-start | bytes 663560 | tf_op jit(solution)/shard_map/ppermute | solution.py:382
  18.5 10.0 %collective-permute-start.4 = (bf16[96,1024]{1,0:T(8,128)(2,1)S(1)}, bf16[96,1024]{1,0:T(8,128)(2,1)S(1)}, u32[]{:S(2)}, u32[]{:S(2)}) collective-permute-start(bf16[96,1024]{1,0:T(8,128)(2,1)S(1)} %add.3), channel_id=1, source_target_pairs={{0,8},{8,12},{12,4},{4,0},{1,9},{9,13},{13,5},{5,1},{2,10},{10,14}... | collective-permute-start | bytes 589832 | tf_op jit(solution)/shard_map/ppermute | solution.py:382
  24.5 7.7 %collective-permute-start.2 = (bf16[96,1152]{1,0:T(8,128)(2,1)S(1)}, bf16[96,1152]{1,0:T(8,128)(2,1)S(1)}, u32[]{:S(2)}, u32[]{:S(2)}) collective-permute-start(bf16[96,1152]{1,0:T(8,128)(2,1)S(1)} %get-tuple-element.24), channel_id=1, source_target_pairs={{0,8},{8,12},{12,4},{4,0},{1,9},{9,13},{13,5},{5,1},{2,10},{10,14}... | collective-permute-start | bytes 663560 | tf_op jit(solution)/shard_map/ppermute | solution.py:382
  28.6 9.1 %collective-permute-start.5 = (bf16[96,1024]{1,0:T(8,128)(2,1)S(1)}, bf16[96,1024]{1,0:T(8,128)(2,1)S(1)}, u32[]{:S(2)}, u32[]{:S(2)}) collective-permute-start(bf16[96,1024]{1,0:T(8,128)(2,1)S(1)} %add.4), channel_id=1, source_target_pairs={{0,8},{8,12},{12,4},{4,0},{1,9},{9,13},{13,5},{5,1},{2,10},{10,14}... | collective-permute-start | bytes 589832 | tf_op jit(solution)/shard_map/ppermute | solution.py:382
  33.5 8.2 %collective-permute-start.9 = (bf16[96,1024]{1,0:T(8,128)(2,1)S(1)}, bf16[96,1024]{1,0:T(8,128)(2,1)S(1)}, u32[]{:S(2)}, u32[]{:S(2)}) collective-permute-start(bf16[96,1024]{1,0:T(8,128)(2,1)S(1)} %get-tuple-element.31.refs_2_), channel_id=1, source_target_pairs={{0,8},{8,12},{12,4},{4,0},{1,9},{9,13},{13,5},{5,1},{2,10},{10,14}... | collective-permute-start | bytes 589832 | tf_op jit(solution)/shard_map/ppermute | solution.py:382
  37.8 8.1 %collective-permute-start.6 = (bf16[96,1024]{1,0:T(8,128)(2,1)S(1)}, bf16[96,1024]{1,0:T(8,128)(2,1)S(1)}, u32[]{:S(2)}, u32[]{:S(2)}) collective-permute-start(bf16[96,1024]{1,0:T(8,128)(2,1)S(1)} %add.5.refs_2_), channel_id=1, source_target_pairs={{0,8},{8,12},{12,4},{4,0},{1,9},{9,13},{13,5},{5,1},{2,10},{10,14}... | collective-permute-start | bytes 589832 | tf_op jit(solution)/shard_map/ppermute | solution.py:382
  41.7 9.9 %collective-permute-start.10 = (bf16[96,1024]{1,0:T(8,128)(2,1)S(1)}, bf16[96,1024]{1,0:T(8,128)(2,1)S(1)}, u32[]{:S(2)}, u32[]{:S(2)}) collective-permute-start(bf16[96,1024]{1,0:T(8,128)(2,1)S(1)} %collective-permute-done.9.refs_3_.refs_4_), channel_id=1, source_target_pairs={{0,8},{8,12},{12,4},{4,0},{1,9},{9,13},{13,5},{5,1},{2,10},{10,14}... | collective-permute-start | bytes 589832 | tf_op jit(solution)/shard_map/ppermute | solution.py:382
  45.9 8.4 %collective-permute-start.7 = (bf16[96,1024]{1,0:T(8,128)(2,1)S(1)}, bf16[96,1024]{1,0:T(8,128)(2,1)S(1)}, u32[]{:S(2)}, u32[]{:S(2)}) collective-permute-start(bf16[96,1024]{1,0:T(8,128)(2,1)S(1)} %collective-permute-done.6.refs_3_.refs_4_), channel_id=1, source_target_pairs={{0,8},{8,12},{12,4},{4,0},{1,9},{9,13},{13,5},{5,1},{2,10},{10,14}... | collective-permute-start | bytes 589832 | tf_op jit(solution)/shard_map/ppermute | solution.py:382
  51.6 6.1 %collective-permute-start.11 = (bf16[96,1024]{1,0:T(8,128)(2,1)S(1)}, bf16[96,1024]{1,0:T(8,128)(2,1)S(1)}, u32[]{:S(2)}, u32[]{:S(2)}) collective-permute-start(bf16[96,1024]{1,0:T(8,128)(2,1)S(1)} %collective-permute-done.10.refs_2_), channel_id=1, source_target_pairs={{0,8},{8,12},{12,4},{4,0},{1,9},{9,13},{13,5},{5,1},{2,10},{10,14}... | collective-permute-start | bytes 589832 | tf_op jit(solution)/shard_map/ppermute | solution.py:382
  54.3 6.6 %collective-permute-start.8 = (bf16[96,1024]{1,0:T(8,128)(2,1)S(1)}, bf16[96,1024]{1,0:T(8,128)(2,1)S(1)}, u32[]{:S(2)}, u32[]{:S(2)}) collective-permute-start(bf16[96,1024]{1,0:T(8,128)(2,1)S(1)} %collective-permute-done.7.refs_2_), channel_id=1, source_target_pairs={{0,8},{8,12},{12,4},{4,0},{1,9},{9,13},{13,5},{5,1},{2,10},{10,14}... | collective-permute-start | bytes 589832 | tf_op jit(solution)/shard_map/ppermute | solution.py:382

commit v8 on v7

--- a/solution.py
+++ b/solution.py
@@ -10,7 +10,7 @@
 LANES = 128
 EXPONENT_BITS = (1, 2, 4, 8, 16, 32, 64)
 GROUP = 8
-TILE = 512
+TILE = 1024
 LOAD_PARTS = 4
 VMEM_LIMIT = 24 * 1024 * 1024
 IN_VMEM = pl.BlockSpec(memory_space=pltpu.VMEM)
@@ -305,7 +305,7 @@
         out_ref[at, :] = contract_tokens(tables, all_ref, at)
 
 
-def early_grad(tables, errors, tile=256):
+def early_grad(tables, errors, tile=512):
     width = tables[0].shape[1]
     rows, columns = errors[0].shape
     blocks = len(errors)
@@ -341,7 +341,7 @@
         copy.wait()
 
 
-def grad_part(tables, errors, own, early, features, column0, previous, tile=256):
+def grad_part(tables, errors, own, early, features, column0, previous, tile=128):
     width = tables[0].shape[1]
     rows, columns = errors[0].shape
     blocks = len(errors)

time: 63.6 us -> 63.6 us (level)
  no operation moved by 1% of the time
where the time goes in v8:
time: 63.6 us; the launch traced here: 63.5 us
  starting transfers between devices  32.6 us (51%)
  Pallas kernels  19.2 us (30%)
  waiting for transfers between devices  10.8 us (17%)
  between operations  0.9 us (1%)
    ppermute x12, starting transfers between devices, send(): return lax.ppermute(x, 'latent', ring_next(count))  32.6 us
    ppermute x12, waiting for transfers between devices, send(): return lax.ppermute(x, 'latent', ring_next(count))  10.8 us
    pallas_call x2, Pallas kernels, grad_part(): pl.pallas_call(functools.partial(grad_kernel, blocks, column0, tile), in_...  4.81 us
    pallas_call x3, Pallas kernels, step_a(): pl.pallas_call(functools.partial(step_kernel, last), in_specs=[IN_SMEM] +...  4.03 us
    pallas_call x1, Pallas kernels, begin(): pl.pallas_call(begin_kernel, in_specs=[IN_SMEM] + [IN_HBM] * 4, out_specs...  2.65 us
    pallas_call x2, Pallas kernels, early_grad(): pl.pallas_call(functools.partial(early_kernel, blocks, tile), in_specs=[I...  2.58 us
    pallas_call x1, Pallas kernels, second(): pl.pallas_call(functools.partial(second_kernel, column0), in_specs=[IN_VM...  2.56 us
    pallas_call x3, Pallas kernels, step_b(): pl.pallas_call(multiply_kernel, in_specs=[IN_VMEM] * 2, out_specs=IN_VMEM...  2.42 us
  transfers between devices with their start and end apart: 12, of which 7 were waited for; matrix products, arithmetic and copies ran while one was open for 0% of the time, Pallas kernels for 22%

profile of v8, /device:TPU:0, one launch (start us, length us, event | category | flops | bytes accessed | tf_op | source)
XLA Modules:
  0.0 63.5 jit_solution(13149220447279764130)
XLA Ops:
  0.6 0.0 copy-start
  0.6 2.6 %begin.1 = (bf16[2048,1024]{1,0:T(8,128)(2,1)S(1)}, bf16[96,2048]{1,0:T(8,128)(2,1)S(1)}, bf16[96,1152]{1,0:T(8,128)(2,1)S(1)}) custom-call(s32[1]{0:T(128)} %bitcast.first_ref, s32[64,96]{1,0:T(8,128)} %bitcast.10, bf16[64,96]{1,0:T(8,128)(2,1)} %bitcast.11, bf16[2048,2048]{1,0:T(8,128)(2,1)} %weight_hbm.3, bf16[96,2048]{1,0:T(8,128)(2,1)} %tokens_hbm.3), custom_call_target="tpu_custom_call" | custom-call | bytes 1048576 | tf_op jit(solution)/shard_map/begin/pallas_call | solution.py:171
  3.3 4.1 %collective-permute-start = (bf16[96,1152]{1,0:T(8,128)(2,1)S(1)}, bf16[96,1152]{1,0:T(8,128)(2,1)S(1)}, u32[]{:S(2)}, u32[]{:S(2)}) collective-permute-start(bf16[96,1152]{1,0:T(8,128)(2,1)S(1)} %get-tuple-element.19), channel_id=1, source_target_pairs={{0,8},{8,12},{12,4},{4,0},{1,9},{9,13},{13,5},{5,1},{2,10},{10,14}... | collective-permute-start | bytes 663560 | tf_op jit(solution)/shard_map/ppermute | solution.py:382
  7.4 2.6 %second.1 = (bf16[2048,1024]{1,0:T(8,128)(2,1)S(1)}, bf16[96,1024]{1,0:T(8,128)(2,1)S(1)}) custom-call(bf16[96,2048]{1,0:T(8,128)(2,1)S(1)} %get-tuple-element.26.table_ref.refs_1_, bf16[2048,2048]{1,0:T(8,128)(2,1)} %weight_hbm.3, bf16[96,2048]{1,0:T(8,128)(2,1)} %tokens_hbm.3), custom_call_target="tpu_custom_call" | custom-call | bytes 1048576 | tf_op jit(solution)/shard_map/second/pallas_call | solution.py:202
  10.0 1.6 %collective-permute-start.3 = (bf16[96,1024]{1,0:T(8,128)(2,1)S(1)}, bf16[96,1024]{1,0:T(8,128)(2,1)S(1)}, u32[]{:S(2)}, u32[]{:S(2)}) collective-permute-start(bf16[96,1024]{1,0:T(8,128)(2,1)S(1)} %get-tuple-element.28), channel_id=1, source_target_pairs={{0,8},{8,12},{12,4},{4,0},{1,9},{9,13},{13,5},{5,1},{2,10},{10,14}... | collective-permute-start | bytes 589832 | tf_op jit(solution)/shard_map/ppermute | solution.py:382
  11.6 1.2 %collective-permute-done.arrived_ref = bf16[96,1152]{1,0:T(8,128)(2,1)S(1)} collective-permute-done((bf16[96,1152]{1,0:T(8,128)(2,1)S(1)}, bf16[96,1152]{1,0:T(8,128)(2,1)S(1)}, u32[]{:S(2)}, u32[]{:S(2)}) %collective-permute-start) | collective-permute-done | bytes 221216 | tf_op jit(solution)/shard_map/ppermute | solution.py:382
  12.8 0.0 copy-done
  12.8 1.3 %step_a.3 = (bf16[96,2048]{1,0:T(8,128)(2,1)S(1)}, bf16[96,1152]{1,0:T(8,128)(2,1)S(1)}) custom-call(s32[1]{0:T(128)} %bitcast.first_ref, bf16[96,1152]{1,0:T(8,128)(2,1)S(1)} %collective-permute-done.arrived_ref, bf16[2048,1024]{1,0:T(8,128)(2,1)S(1)} %get-tuple-element.20.weight_ref, f32[1,2048]{1,0:T(1,128)S(1)} %bitcast.4), custom_call_target="tpu_custom_call" | custom-call | bytes 1048576 | tf_op jit(solution)/shard_map/step_a/pallas_call | solution.py:238
  14.2 3.4 %collective-permute-start.1 = (bf16[96,1152]{1,0:T(8,128)(2,1)S(1)}, bf16[96,1152]{1,0:T(8,128)(2,1)S(1)}, u32[]{:S(2)}, u32[]{:S(2)}) collective-permute-start(bf16[96,1152]{1,0:T(8,128)(2,1)S(1)} %get-tuple-element.22), channel_id=1, source_target_pairs={{0,8},{8,12},{12,4},{4,0},{1,9},{9,13},{13,5},{5,1},{2,10},{10,14}... | collective-permute-start | bytes 663560 | tf_op jit(solution)/shard_map/ppermute | solution.py:382
  17.6 0.8 %multiply.5.part_ref = f32[96,1024]{1,0:T(8,128)S(1)} custom-call(bf16[96,2048]{1,0:T(8,128)(2,1)S(1)} %get-tuple-element.21.table_ref.refs_0_, bf16[2048,1024]{1,0:T(8,128)(2,1)S(1)} %get-tuple-element.27.weight_ref), custom_call_target="tpu_custom_call" | custom-call | bytes 1048576 | tf_op jit(solution)/shard_map/multiply/pallas_call | solution.py:269
  18.4 0.0 collective-permute-done.3.arrived_ref
  18.4 0.1 add.3
  18.5 1.6 %collective-permute-start.4 = (bf16[96,1024]{1,0:T(8,128)(2,1)S(1)}, bf16[96,1024]{1,0:T(8,128)(2,1)S(1)}, u32[]{:S(2)}, u32[]{:S(2)}) collective-permute-start(bf16[96,1024]{1,0:T(8,128)(2,1)S(1)} %add.3), channel_id=1, source_target_pairs={{0,8},{8,12},{12,4},{4,0},{1,9},{9,13},{13,5},{5,1},{2,10},{10,14}... | collective-permute-start | bytes 589832 | tf_op jit(solution)/shard_map/ppermute | solution.py:382
  20.1 3.1 %collective-permute-done.1.arrived_ref = bf16[96,1152]{1,0:T(8,128)(2,1)S(1)} collective-permute-done((bf16[96,1152]{1,0:T(8,128)(2,1)S(1)}, bf16[96,1152]{1,0:T(8,128)(2,1)S(1)}, u32[]{:S(2)}, u32[]{:S(2)}) %collective-permute-start.1) | collective-permute-done | bytes 221216 | tf_op jit(solution)/shard_map/ppermute | solution.py:382
  23.2 1.3 %step_a.4 = (bf16[96,2048]{1,0:T(8,128)(2,1)S(1)}, bf16[96,1152]{1,0:T(8,128)(2,1)S(1)}) custom-call(s32[1]{0:T(128)} %bitcast.first_ref, bf16[96,1152]{1,0:T(8,128)(2,1)S(1)} %collective-permute-done.1.arrived_ref, bf16[2048,1024]{1,0:T(8,128)(2,1)S(1)} %get-tuple-element.20.weight_ref, f32[1,2048]{1,0:T(1,128)S(1)} %bitcast.6), custom_call_target="tpu_custom_call" | custom-call | bytes 1048576 | tf_op jit(solution)/shard_map/step_a/pallas_call | solution.py:238
  24.5 3.2 %collective-permute-start.2 = (bf16[96,1152]{1,0:T(8,128)(2,1)S(1)}, bf16[96,1152]{1,0:T(8,128)(2,1)S(1)}, u32[]{:S(2)}, u32[]{:S(2)}) collective-permute-start(bf16[96,1152]{1,0:T(8,128)(2,1)S(1)} %get-tuple-element.24), channel_id=1, source_target_pairs={{0,8},{8,12},{12,4},{4,0},{1,9},{9,13},{13,5},{5,1},{2,10},{10,14}... | collective-permute-start | bytes 663560 | tf_op jit(solution)/shard_map/ppermute | solution.py:382
  27.7 0.8 %multiply.4.part_ref = f32[96,1024]{1,0:T(8,128)S(1)} custom-call(bf16[96,2048]{1,0:T(8,128)(2,1)S(1)} %get-tuple-element.23.table_ref.refs_1_, bf16[2048,1024]{1,0:T(8,128)(2,1)S(1)} %get-tuple-element.27.weight_ref), custom_call_target="tpu_custom_call" | custom-call | bytes 1048576 | tf_op jit(solution)/shard_map/multiply/pallas_call | solution.py:269
  28.5 0.0 collective-permute-done.4.arrived_ref
  28.5 0.1 add.4
  28.6 2.1 %collective-permute-start.5 = (bf16[96,1024]{1,0:T(8,128)(2,1)S(1)}, bf16[96,1024]{1,0:T(8,128)(2,1)S(1)}, u32[]{:S(2)}, u32[]{:S(2)}) collective-permute-start(bf16[96,1024]{1,0:T(8,128)(2,1)S(1)} %add.4), channel_id=1, source_target_pairs={{0,8},{8,12},{12,4},{4,0},{1,9},{9,13},{13,5},{5,1},{2,10},{10,14}... | collective-permute-start | bytes 589832 | tf_op jit(solution)/shard_map/ppermute | solution.py:382
  30.7 1.5 %collective-permute-done.2.arrived_ref = bf16[96,1152]{1,0:T(8,128)(2,1)S(1)} collective-permute-done((bf16[96,1152]{1,0:T(8,128)(2,1)S(1)}, bf16[96,1152]{1,0:T(8,128)(2,1)S(1)}, u32[]{:S(2)}, u32[]{:S(2)}) %collective-permute-start.2) | collective-permute-done | bytes 221216 | tf_op jit(solution)/shard_map/ppermute | solution.py:382
  32.2 1.3 %step_a.5 = (bf16[96,2048]{1,0:T(8,128)(2,1)S(1)}, bf16[96,1024]{1,0:T(8,128)(2,1)S(1)}) custom-call(s32[1]{0:T(128)} %bitcast.first_ref, bf16[96,1152]{1,0:T(8,128)(2,1)S(1)} %collective-permute-done.2.arrived_ref, bf16[2048,1024]{1,0:T(8,128)(2,1)S(1)} %get-tuple-element.20.weight_ref, f32[1,2048]{1,0:T(1,128)S(1)} %bitcast.8), custom_call_target="tpu_custom_call" | custom-call | bytes 1048576 | tf_op jit(solution)/shard_map/step_a/pallas_call | solution.py:238
  33.5 3.4 %collective-permute-start.9 = (bf16[96,1024]{1,0:T(8,128)(2,1)S(1)}, bf16[96,1024]{1,0:T(8,128)(2,1)S(1)}, u32[]{:S(2)}, u32[]{:S(2)}) collective-permute-start(bf16[96,1024]{1,0:T(8,128)(2,1)S(1)} %get-tuple-element.31.refs_2_), channel_id=1, source_target_pairs={{0,8},{8,12},{12,4},{4,0},{1,9},{9,13},{13,5},{5,1},{2,10},{10,14}... | collective-permute-start | bytes 589832 | tf_op jit(solution)/shard_map/ppermute | solution.py:382
  36.9 0.8 %multiply.3.part_ref = f32[96,1024]{1,0:T(8,128)S(1)} custom-call(bf16[96,2048]{1,0:T(8,128)(2,1)S(1)} %get-tuple-element.25.table_ref.refs_0_, bf16[2048,1024]{1,0:T(8,128)(2,1)S(1)} %get-tuple-element.27.weight_ref), custom_call_target="tpu_custom_call" | custom-call | bytes 1048576 | tf_op jit(solution)/shard_map/multiply/pallas_call | solution.py:269
  37.7 0.0 collective-permute-done.5.arrived_ref
  37.7 0.1 add.5.refs_2_
  37.8 1.7 %collective-permute-start.6 = (bf16[96,1024]{1,0:T(8,128)(2,1)S(1)}, bf16[96,1024]{1,0:T(8,128)(2,1)S(1)}, u32[]{:S(2)}, u32[]{:S(2)}) collective-permute-start(bf16[96,1024]{1,0:T(8,128)(2,1)S(1)} %add.5.refs_2_), channel_id=1, source_target_pairs={{0,8},{8,12},{12,4},{4,0},{1,9},{9,13},{13,5},{5,1},{2,10},{10,14}... | collective-permute-start | bytes 589832 | tf_op jit(solution)/shard_map/ppermute | solution.py:382
  39.5 2.2 %collective-permute-done.9.refs_3_.refs_4_ = bf16[96,1024]{1,0:T(8,128)(2,1)S(1)} collective-permute-done((bf16[96,1024]{1,0:T(8,128)(2,1)S(1)}, bf16[96,1024]{1,0:T(8,128)(2,1)S(1)}, u32[]{:S(2)}, u32[]{:S(2)}) %collective-permute-start.9) | collective-permute-done | bytes 196640 | tf_op jit(solution)/shard_map/ppermute | solution.py:382
  41.7 3.1 %collective-permute-start.10 = (bf16[96,1024]{1,0:T(8,128)(2,1)S(1)}, bf16[96,1024]{1,0:T(8,128)(2,1)S(1)}, u32[]{:S(2)}, u32[]{:S(2)}) collective-permute-start(bf16[96,1024]{1,0:T(8,128)(2,1)S(1)} %collective-permute-done.9.refs_3_.refs_4_), channel_id=1, source_target_pairs={{0,8},{8,12},{12,4},{4,0},{1,9},{9,13},{13,5},{5,1},{2,10},{10,14}... | collective-permute-start | bytes 589832 | tf_op jit(solution)/shard_map/ppermute | solution.py:382
  44.8 1.1 %collective-permute-done.6.refs_3_.refs_4_ = bf16[96,1024]{1,0:T(8,128)(2,1)S(1)} collective-permute-done((bf16[96,1024]{1,0:T(8,128)(2,1)S(1)}, bf16[96,1024]{1,0:T(8,128)(2,1)S(1)}, u32[]{:S(2)}, u32[]{:S(2)}) %collective-permute-start.6) | collective-permute-done | bytes 196640 | tf_op jit(solution)/shard_map/ppermute | solution.py:382
  45.9 3.1 %collective-permute-start.7 = (bf16[96,1024]{1,0:T(8,128)(2,1)S(1)}, bf16[96,1024]{1,0:T(8,128)(2,1)S(1)}, u32[]{:S(2)}, u32[]{:S(2)}) collective-permute-start(bf16[96,1024]{1,0:T(8,128)(2,1)S(1)} %collective-permute-done.6.refs_3_.refs_4_), channel_id=1, source_target_pairs={{0,8},{8,12},{12,4},{4,0},{1,9},{9,13},{13,5},{5,1},{2,10},{10,14}... | collective-permute-start | bytes 589832 | tf_op jit(solution)/shard_map/ppermute | solution.py:382
  49.0 1.3 %early_grad.3.refs_5_ = f32[2048,1024]{1,0:T(8,128)S(1)} custom-call(bf16[96,2048]{1,0:T(8,128)(2,1)S(1)} %get-tuple-element.25.table_ref.refs_0_, bf16[96,2048]{1,0:T(8,128)(2,1)S(1)} %get-tuple-element.26.table_ref.refs_1_, bf16[96,1024]{1,0:T(8,128)(2,1)S(1)} %get-tuple-element.31.refs_2_, bf16[96,1024]{1,0:T(8,128)(2,1)S(1)} %collective-permute-done.9.refs_3_.refs_4_), custom_call_target="tpu_custom_call" | custom-call | bytes 1048576 | tf_op jit(solution)/shard_map/early_grad/pallas_call | solution.py:312
  50.3 1.3 %early_grad.2.refs_5_ = f32[2048,1024]{1,0:T(8,128)S(1)} custom-call(bf16[96,2048]{1,0:T(8,128)(2,1)S(1)} %get-tuple-element.25.table_ref.refs_0_, bf16[96,2048]{1,0:T(8,128)(2,1)S(1)} %get-tuple-element.26.table_ref.refs_1_, bf16[96,1024]{1,0:T(8,128)(2,1)S(1)} %add.5.refs_2_, bf16[96,1024]{1,0:T(8,128)(2,1)S(1)} %collective-permute-done.6.refs_3_.refs_4_), custom_call_target="tpu_custom_call" | custom-call | bytes 1048576 | tf_op jit(solution)/shard_map/early_grad/pallas_call | solution.py:312
  51.6 0.0 collective-permute-done.10.refs_2_
  51.6 1.9 %collective-permute-start.11 = (bf16[96,1024]{1,0:T(8,128)(2,1)S(1)}, bf16[96,1024]{1,0:T(8,128)(2,1)S(1)}, u32[]{:S(2)}, u32[]{:S(2)}) collective-permute-start(bf16[96,1024]{1,0:T(8,128)(2,1)S(1)} %collective-permute-done.10.refs_2_), channel_id=1, source_target_pairs={{0,8},{8,12},{12,4},{4,0},{1,9},{9,13},{13,5},{5,1},{2,10},{10,14}... | collective-permute-start | bytes 589832 | tf_op jit(solution)/shard_map/ppermute | solution.py:382
  53.5 0.8 %collective-permute-done.7.refs_2_ = bf16[96,1024]{1,0:T(8,128)(2,1)S(1)} collective-permute-done((bf16[96,1024]{1,0:T(8,128)(2,1)S(1)}, bf16[96,1024]{1,0:T(8,128)(2,1)S(1)}, u32[]{:S(2)}, u32[]{:S(2)}) %collective-permute-start.7) | collective-permute-done | bytes 196640 | tf_op jit(solution)/shard_map/ppermute | solution.py:382
  54.3 3.4 %collective-permute-start.8 = (bf16[96,1024]{1,0:T(8,128)(2,1)S(1)}, bf16[96,1024]{1,0:T(8,128)(2,1)S(1)}, u32[]{:S(2)}, u32[]{:S(2)}) collective-permute-start(bf16[96,1024]{1,0:T(8,128)(2,1)S(1)} %collective-permute-done.7.refs_2_), channel_id=1, source_target_pairs={{0,8},{8,12},{12,4},{4,0},{1,9},{9,13},{13,5},{5,1},{2,10},{10,14}... | collective-permute-start | bytes 589832 | tf_op jit(solution)/shard_map/ppermute | solution.py:382
  57.7 0.0 collective-permute-done.11.refs_3_
  57.7 2.4 %grad.2 = (bf16[96,2048]{1,0:T(8,128)(2,1)}, bf16[2048,2048]{1,0:T(8,128)(2,1)}) custom-call(bf16[96,2048]{1,0:T(8,128)(2,1)S(1)} %get-tuple-element.21.table_ref.refs_0_, bf16[96,2048]{1,0:T(8,128)(2,1)S(1)} %get-tuple-element.23.table_ref.refs_1_, bf16[96,1024]{1,0:T(8,128)(2,1)S(1)} %collective-permute-done.10.refs_2_, ...), custom_call_target="tpu_custom_call" | custom-call | bytes 1048576 | tf_op jit(solution)/shard_map/grad/pallas_call | solution.py:355
  60.1 0.8 %collective-permute-done.8.refs_3_ = bf16[96,1024]{1,0:T(8,128)(2,1)S(1)} collective-permute-done((bf16[96,1024]{1,0:T(8,128)(2,1)S(1)}, bf16[96,1024]{1,0:T(8,128)(2,1)S(1)}, u32[]{:S(2)}, u32[]{:S(2)}) %collective-permute-start.8) | collective-permute-done | bytes 196640 | tf_op jit(solution)/shard_map/ppermute | solution.py:382
  60.9 2.4 %grad.3 = (bf16[96,2048]{1,0:T(8,128)(2,1)}, bf16[2048,2048]{1,0:T(8,128)(2,1)}) custom-call(bf16[96,2048]{1,0:T(8,128)(2,1)S(1)} %get-tuple-element.21.table_ref.refs_0_, bf16[96,2048]{1,0:T(8,128)(2,1)S(1)} %get-tuple-element.23.table_ref.refs_1_, ...), custom_call_target="tpu_custom_call", output_to_operand_aliasing={{0}: (6, {}), {1}: (7, {})} | custom-call | bytes 1048576 | tf_op jit(solution)/shard_map/grad/pallas_call | solution.py:355
Async XLA Ops:
  0.6 12.2 %copy-start = (f32[2048]{0:T(1024)S(1)}, f32[2048]{0:T(1024)}, u32[]{:S(2)}) copy-start(f32[2048]{0:T(1024)} %param.8) | copy-start | bytes 24580
  3.3 9.5 %collective-permute-start = (bf16[96,1152]{1,0:T(8,128)(2,1)S(1)}, bf16[96,1152]{1,0:T(8,128)(2,1)S(1)}, u32[]{:S(2)}, u32[]{:S(2)}) collective-permute-start(bf16[96,1152]{1,0:T(8,128)(2,1)S(1)} %get-tuple-element.19), channel_id=1, source_target_pairs={{0,8},{8,12},{12,4},{4,0},{1,9},{9,13},{13,5},{5,1},{2,10},{10,14}... | collective-permute-start | bytes 663560 | tf_op jit(solution)/shard_map/ppermute | solution.py:382
  10.0 8.5 %collective-permute-start.3 = (bf16[96,1024]{1,0:T(8,128)(2,1)S(1)}, bf16[96,1024]{1,0:T(8,128)(2,1)S(1)}, u32[]{:S(2)}, u32[]{:S(2)}) collective-permute-start(bf16[96,1024]{1,0:T(8,128)(2,1)S(1)} %get-tuple-element.28), channel_id=1, source_target_pairs={{0,8},{8,12},{12,4},{4,0},{1,9},{9,13},{13,5},{5,1},{2,10},{10,14}... | collective-permute-start | bytes 589832 | tf_op jit(solution)/shard_map/ppermute | solution.py:382
  14.2 9.0 %collective-permute-start.1 = (bf16[96,1152]{1,0:T(8,128)(2,1)S(1)}, bf16[96,1152]{1,0:T(8,128)(2,1)S(1)}, u32[]{:S(2)}, u32[]{:S(2)}) collective-permute-start(bf16[96,1152]{1,0:T(8,128)(2,1)S(1)} %get-tuple-element.22), channel_id=1, source_target_pairs={{0,8},{8,12},{12,4},{4,0},{1,9},{9,13},{13,5},{5,1},{2,10},{10,14}... | collective-permute-start | bytes 663560 | tf_op jit(solution)/shard_map/ppermute | solution.py:382
  18.5 10.1 %collective-permute-start.4 = (bf16[96,1024]{1,0:T(8,128)(2,1)S(1)}, bf16[96,1024]{1,0:T(8,128)(2,1)S(1)}, u32[]{:S(2)}, u32[]{:S(2)}) collective-permute-start(bf16[96,1024]{1,0:T(8,128)(2,1)S(1)} %add.3), channel_id=1, source_target_pairs={{0,8},{8,12},{12,4},{4,0},{1,9},{9,13},{13,5},{5,1},{2,10},{10,14}... | collective-permute-start | bytes 589832 | tf_op jit(solution)/shard_map/ppermute | solution.py:382
  24.5 7.7 %collective-permute-start.2 = (bf16[96,1152]{1,0:T(8,128)(2,1)S(1)}, bf16[96,1152]{1,0:T(8,128)(2,1)S(1)}, u32[]{:S(2)}, u32[]{:S(2)}) collective-permute-start(bf16[96,1152]{1,0:T(8,128)(2,1)S(1)} %get-tuple-element.24), channel_id=1, source_target_pairs={{0,8},{8,12},{12,4},{4,0},{1,9},{9,13},{13,5},{5,1},{2,10},{10,14}... | collective-permute-start | bytes 663560 | tf_op jit(solution)/shard_map/ppermute | solution.py:382
  28.6 9.1 %collective-permute-start.5 = (bf16[96,1024]{1,0:T(8,128)(2,1)S(1)}, bf16[96,1024]{1,0:T(8,128)(2,1)S(1)}, u32[]{:S(2)}, u32[]{:S(2)}) collective-permute-start(bf16[96,1024]{1,0:T(8,128)(2,1)S(1)} %add.4), channel_id=1, source_target_pairs={{0,8},{8,12},{12,4},{4,0},{1,9},{9,13},{13,5},{5,1},{2,10},{10,14}... | collective-permute-start | bytes 589832 | tf_op jit(solution)/shard_map/ppermute | solution.py:382
  33.5 8.2 %collective-permute-start.9 = (bf16[96,1024]{1,0:T(8,128)(2,1)S(1)}, bf16[96,1024]{1,0:T(8,128)(2,1)S(1)}, u32[]{:S(2)}, u32[]{:S(2)}) collective-permute-start(bf16[96,1024]{1,0:T(8,128)(2,1)S(1)} %get-tuple-element.31.refs_2_), channel_id=1, source_target_pairs={{0,8},{8,12},{12,4},{4,0},{1,9},{9,13},{13,5},{5,1},{2,10},{10,14}... | collective-permute-start | bytes 589832 | tf_op jit(solution)/shard_map/ppermute | solution.py:382
  37.8 8.1 %collective-permute-start.6 = (bf16[96,1024]{1,0:T(8,128)(2,1)S(1)}, bf16[96,1024]{1,0:T(8,128)(2,1)S(1)}, u32[]{:S(2)}, u32[]{:S(2)}) collective-permute-start(bf16[96,1024]{1,0:T(8,128)(2,1)S(1)} %add.5.refs_2_), channel_id=1, source_target_pairs={{0,8},{8,12},{12,4},{4,0},{1,9},{9,13},{13,5},{5,1},{2,10},{10,14}... | collective-permute-start | bytes 589832 | tf_op jit(solution)/shard_map/ppermute | solution.py:382
  41.7 9.9 %collective-permute-start.10 = (bf16[96,1024]{1,0:T(8,128)(2,1)S(1)}, bf16[96,1024]{1,0:T(8,128)(2,1)S(1)}, u32[]{:S(2)}, u32[]{:S(2)}) collective-permute-start(bf16[96,1024]{1,0:T(8,128)(2,1)S(1)} %collective-permute-done.9.refs_3_.refs_4_), channel_id=1, source_target_pairs={{0,8},{8,12},{12,4},{4,0},{1,9},{9,13},{13,5},{5,1},{2,10},{10,14}... | collective-permute-start | bytes 589832 | tf_op jit(solution)/shard_map/ppermute | solution.py:382
  45.9 8.4 %collective-permute-start.7 = (bf16[96,1024]{1,0:T(8,128)(2,1)S(1)}, bf16[96,1024]{1,0:T(8,128)(2,1)S(1)}, u32[]{:S(2)}, u32[]{:S(2)}) collective-permute-start(bf16[96,1024]{1,0:T(8,128)(2,1)S(1)} %collective-permute-done.6.refs_3_.refs_4_), channel_id=1, source_target_pairs={{0,8},{8,12},{12,4},{4,0},{1,9},{9,13},{13,5},{5,1},{2,10},{10,14}... | collective-permute-start | bytes 589832 | tf_op jit(solution)/shard_map/ppermute | solution.py:382
  51.6 6.1 %collective-permute-start.11 = (bf16[96,1024]{1,0:T(8,128)(2,1)S(1)}, bf16[96,1024]{1,0:T(8,128)(2,1)S(1)}, u32[]{:S(2)}, u32[]{:S(2)}) collective-permute-start(bf16[96,1024]{1,0:T(8,128)(2,1)S(1)} %collective-permute-done.10.refs_2_), channel_id=1, source_target_pairs={{0,8},{8,12},{12,4},{4,0},{1,9},{9,13},{13,5},{5,1},{2,10},{10,14}... | collective-permute-start | bytes 589832 | tf_op jit(solution)/shard_map/ppermute | solution.py:382
  54.3 6.6 %collective-permute-start.8 = (bf16[96,1024]{1,0:T(8,128)(2,1)S(1)}, bf16[96,1024]{1,0:T(8,128)(2,1)S(1)}, u32[]{:S(2)}, u32[]{:S(2)}) collective-permute-start(bf16[96,1024]{1,0:T(8,128)(2,1)S(1)} %collective-permute-done.7.refs_2_), channel_id=1, source_target_pairs={{0,8},{8,12},{12,4},{4,0},{1,9},{9,13},{13,5},{5,1},{2,10},{10,14}... | collective-permute-start | bytes 589832 | tf_op jit(solution)/shard_map/ppermute | solution.py:382

commit v9 on v8

--- a/solution.py
+++ b/solution.py
@@ -286,23 +286,17 @@
     )(part, arrived, bias)
 
 
-def contract_tokens(tables, all_ref, at):
+def contract_tokens(tables, errors, at):
     table = jnp.concatenate([table_ref[:, at] for table_ref in tables], axis=0)
-    return lax.dot_general(table, all_ref[...], (((0,), (0,)), ((), ())), preferred_element_type=jnp.float32)
-
-
-def gather_errors(errors, all_ref):
-    rows = errors[0].shape[0]
-    for b, error_ref in enumerate(errors):
-        all_ref[b * rows : (b + 1) * rows, :] = error_ref[...]
+    stacked = jnp.concatenate([error_ref[...] for error_ref in errors], axis=0)
+    return lax.dot_general(table, stacked, (((0,), (0,)), ((), ())), preferred_element_type=jnp.float32)
 
 
 def early_kernel(blocks, tile, *refs):
-    tables, errors, out_ref, all_ref = refs[:blocks], refs[blocks : 2 * blocks], refs[-2], refs[-1]
-    gather_errors(errors, all_ref)
+    tables, errors, out_ref = refs[:blocks], refs[blocks : 2 * blocks], refs[-1]
     for l in range(0, out_ref.shape[0], tile):
         at = slice(l, l + tile)
-        out_ref[at, :] = contract_tokens(tables, all_ref, at)
+        out_ref[at, :] = contract_tokens(tables, errors, at)
 
 
 def early_grad(tables, errors, tile=512):
@@ -314,7 +308,6 @@
         in_specs=[IN_VMEM] * (2 * blocks),
         out_specs=IN_VMEM,
         out_shape=jax.ShapeDtypeStruct((width, columns), jnp.float32),
-        scratch_shapes=[pltpu.VMEM((blocks * rows, columns), jnp.bfloat16)],
         compiler_params=params(),
         cost_estimate=cost(1 << 20),
         name="early_grad",
@@ -323,16 +316,15 @@
 
 def grad_kernel(blocks, column0, tile, *refs):
     tables, errors, (own_ref, early_ref) = refs[:blocks], refs[blocks : 2 * blocks], refs[2 * blocks : 2 * blocks + 2]
-    error_out, grad_out, all_ref, made_ref, sems = refs[-5:]
+    error_out, grad_out, made_ref, sems = refs[-4:]
     rows, columns = errors[0].shape
     width = tables[0].shape[1]
     part = pl.ds(column0, columns)
     copies = [pltpu.make_async_copy(own_ref, error_out.at[:, part], sems.at[width // tile])]
     copies[0].start()
-    gather_errors(errors, all_ref)
     for i, l in enumerate(range(0, width, tile)):
         at = slice(l, l + tile)
-        product = contract_tokens(tables, all_ref, at) + early_ref[at, :]
+        product = contract_tokens(tables, errors, at) + early_ref[at, :]
         made_ref[at, :] = product.astype(made_ref.dtype)
         copy = pltpu.make_async_copy(made_ref.at[pl.ds(l, tile), :], grad_out.at[pl.ds(l, tile), part], sems.at[i])
         copy.start()
@@ -361,7 +353,6 @@
             jax.ShapeDtypeStruct((width, features), jnp.bfloat16),
         ],
         scratch_shapes=[
-            pltpu.VMEM((blocks * rows, columns), jnp.bfloat16),
             pltpu.VMEM((width, columns), jnp.bfloat16),
             pltpu.SemaphoreType.DMA((width // tile + 1,)),
         ],

time: 63.6 us -> 63.6 us (level)
  no operation moved by 1% of the time
where the time goes in v9:
time: 63.6 us; the launch traced here: 63.5 us
  starting transfers between devices  32.5 us (51%)
  Pallas kernels  19.2 us (30%)
  waiting for transfers between devices  10.8 us (17%)
  between operations  0.9 us (1%)
    ppermute x12, starting transfers between devices, send(): return lax.ppermute(x, 'latent', ring_next(count))  32.5 us
    ppermute x12, waiting for transfers between devices, send(): return lax.ppermute(x, 'latent', ring_next(count))  10.8 us
    pallas_call x2, Pallas kernels, grad_part(): pl.pallas_call(functools.partial(grad_kernel, blocks, column0, tile), in_...  4.81 us
    pallas_call x3, Pallas kernels, step_a(): pl.pallas_call(functools.partial(step_kernel, last), in_specs=[IN_SMEM] +...  4.03 us
    pallas_call x1, Pallas kernels, begin(): pl.pallas_call(begin_kernel, in_specs=[IN_SMEM] + [IN_HBM] * 4, out_specs...  2.65 us
    pallas_call x2, Pallas kernels, early_grad(): pl.pallas_call(functools.partial(early_kernel, blocks, tile), in_specs=[I...  2.6 us
    pallas_call x1, Pallas kernels, second(): pl.pallas_call(functools.partial(second_kernel, column0), in_specs=[IN_VM...  2.56 us
    pallas_call x3, Pallas kernels, step_b(): pl.pallas_call(multiply_kernel, in_specs=[IN_VMEM] * 2, out_specs=IN_VMEM...  2.42 us
  transfers between devices with their start and end apart: 12, of which 7 were waited for; matrix products, arithmetic and copies ran while one was open for 0% of the time, Pallas kernels for 22%

profile of v9, /device:TPU:0, one launch (start us, length us, event | category | flops | bytes accessed | tf_op | source)
XLA Modules:
  0.0 63.5 jit_solution(8130251349920749983)
XLA Ops:
  0.6 0.0 copy-start
  0.6 2.6 %begin.1 = (bf16[2048,1024]{1,0:T(8,128)(2,1)S(1)}, bf16[96,2048]{1,0:T(8,128)(2,1)S(1)}, bf16[96,1152]{1,0:T(8,128)(2,1)S(1)}) custom-call(s32[1]{0:T(128)} %bitcast.first_ref, s32[64,96]{1,0:T(8,128)} %bitcast.10, bf16[64,96]{1,0:T(8,128)(2,1)} %bitcast.11, bf16[2048,2048]{1,0:T(8,128)(2,1)} %weight_hbm.3, bf16[96,2048]{1,0:T(8,128)(2,1)} %tokens_hbm.3), custom_call_target="tpu_custom_call" | custom-call | bytes 1048576 | tf_op jit(solution)/shard_map/begin/pallas_call | solution.py:171
  3.3 4.1 %collective-permute-start = (bf16[96,1152]{1,0:T(8,128)(2,1)S(1)}, bf16[96,1152]{1,0:T(8,128)(2,1)S(1)}, u32[]{:S(2)}, u32[]{:S(2)}) collective-permute-start(bf16[96,1152]{1,0:T(8,128)(2,1)S(1)} %get-tuple-element.19), channel_id=1, source_target_pairs={{0,8},{8,12},{12,4},{4,0},{1,9},{9,13},{13,5},{5,1},{2,10},{10,14}... | collective-permute-start | bytes 663560 | tf_op jit(solution)/shard_map/ppermute | solution.py:373
  7.4 2.6 %second.1 = (bf16[2048,1024]{1,0:T(8,128)(2,1)S(1)}, bf16[96,1024]{1,0:T(8,128)(2,1)S(1)}) custom-call(bf16[96,2048]{1,0:T(8,128)(2,1)S(1)} %get-tuple-element.26.table_ref.refs_1_, bf16[2048,2048]{1,0:T(8,128)(2,1)} %weight_hbm.3, bf16[96,2048]{1,0:T(8,128)(2,1)} %tokens_hbm.3), custom_call_target="tpu_custom_call" | custom-call | bytes 1048576 | tf_op jit(solution)/shard_map/second/pallas_call | solution.py:202
  10.0 1.6 %collective-permute-start.3 = (bf16[96,1024]{1,0:T(8,128)(2,1)S(1)}, bf16[96,1024]{1,0:T(8,128)(2,1)S(1)}, u32[]{:S(2)}, u32[]{:S(2)}) collective-permute-start(bf16[96,1024]{1,0:T(8,128)(2,1)S(1)} %get-tuple-element.28), channel_id=1, source_target_pairs={{0,8},{8,12},{12,4},{4,0},{1,9},{9,13},{13,5},{5,1},{2,10},{10,14}... | collective-permute-start | bytes 589832 | tf_op jit(solution)/shard_map/ppermute | solution.py:373
  11.6 1.2 %collective-permute-done.arrived_ref = bf16[96,1152]{1,0:T(8,128)(2,1)S(1)} collective-permute-done((bf16[96,1152]{1,0:T(8,128)(2,1)S(1)}, bf16[96,1152]{1,0:T(8,128)(2,1)S(1)}, u32[]{:S(2)}, u32[]{:S(2)}) %collective-permute-start) | collective-permute-done | bytes 221216 | tf_op jit(solution)/shard_map/ppermute | solution.py:373
  12.8 0.0 copy-done
  12.8 1.3 %step_a.3 = (bf16[96,2048]{1,0:T(8,128)(2,1)S(1)}, bf16[96,1152]{1,0:T(8,128)(2,1)S(1)}) custom-call(s32[1]{0:T(128)} %bitcast.first_ref, bf16[96,1152]{1,0:T(8,128)(2,1)S(1)} %collective-permute-done.arrived_ref, bf16[2048,1024]{1,0:T(8,128)(2,1)S(1)} %get-tuple-element.20.weight_ref, f32[1,2048]{1,0:T(1,128)S(1)} %bitcast.4), custom_call_target="tpu_custom_call" | custom-call | bytes 1048576 | tf_op jit(solution)/shard_map/step_a/pallas_call | solution.py:238
  14.2 3.4 %collective-permute-start.1 = (bf16[96,1152]{1,0:T(8,128)(2,1)S(1)}, bf16[96,1152]{1,0:T(8,128)(2,1)S(1)}, u32[]{:S(2)}, u32[]{:S(2)}) collective-permute-start(bf16[96,1152]{1,0:T(8,128)(2,1)S(1)} %get-tuple-element.22), channel_id=1, source_target_pairs={{0,8},{8,12},{12,4},{4,0},{1,9},{9,13},{13,5},{5,1},{2,10},{10,14}... | collective-permute-start | bytes 663560 | tf_op jit(solution)/shard_map/ppermute | solution.py:373
  17.6 0.8 %multiply.5.part_ref = f32[96,1024]{1,0:T(8,128)S(1)} custom-call(bf16[96,2048]{1,0:T(8,128)(2,1)S(1)} %get-tuple-element.21.table_ref.refs_0_, bf16[2048,1024]{1,0:T(8,128)(2,1)S(1)} %get-tuple-element.27.weight_ref), custom_call_target="tpu_custom_call" | custom-call | bytes 1048576 | tf_op jit(solution)/shard_map/multiply/pallas_call | solution.py:269
  18.4 0.0 collective-permute-done.3.arrived_ref
  18.4 0.1 add.3
  18.5 1.6 %collective-permute-start.4 = (bf16[96,1024]{1,0:T(8,128)(2,1)S(1)}, bf16[96,1024]{1,0:T(8,128)(2,1)S(1)}, u32[]{:S(2)}, u32[]{:S(2)}) collective-permute-start(bf16[96,1024]{1,0:T(8,128)(2,1)S(1)} %add.3), channel_id=1, source_target_pairs={{0,8},{8,12},{12,4},{4,0},{1,9},{9,13},{13,5},{5,1},{2,10},{10,14}... | collective-permute-start | bytes 589832 | tf_op jit(solution)/shard_map/ppermute | solution.py:373
  20.1 3.1 %collective-permute-done.1.arrived_ref = bf16[96,1152]{1,0:T(8,128)(2,1)S(1)} collective-permute-done((bf16[96,1152]{1,0:T(8,128)(2,1)S(1)}, bf16[96,1152]{1,0:T(8,128)(2,1)S(1)}, u32[]{:S(2)}, u32[]{:S(2)}) %collective-permute-start.1) | collective-permute-done | bytes 221216 | tf_op jit(solution)/shard_map/ppermute | solution.py:373
  23.2 1.3 %step_a.4 = (bf16[96,2048]{1,0:T(8,128)(2,1)S(1)}, bf16[96,1152]{1,0:T(8,128)(2,1)S(1)}) custom-call(s32[1]{0:T(128)} %bitcast.first_ref, bf16[96,1152]{1,0:T(8,128)(2,1)S(1)} %collective-permute-done.1.arrived_ref, bf16[2048,1024]{1,0:T(8,128)(2,1)S(1)} %get-tuple-element.20.weight_ref, f32[1,2048]{1,0:T(1,128)S(1)} %bitcast.6), custom_call_target="tpu_custom_call" | custom-call | bytes 1048576 | tf_op jit(solution)/shard_map/step_a/pallas_call | solution.py:238
  24.5 3.2 %collective-permute-start.2 = (bf16[96,1152]{1,0:T(8,128)(2,1)S(1)}, bf16[96,1152]{1,0:T(8,128)(2,1)S(1)}, u32[]{:S(2)}, u32[]{:S(2)}) collective-permute-start(bf16[96,1152]{1,0:T(8,128)(2,1)S(1)} %get-tuple-element.24), channel_id=1, source_target_pairs={{0,8},{8,12},{12,4},{4,0},{1,9},{9,13},{13,5},{5,1},{2,10},{10,14}... | collective-permute-start | bytes 663560 | tf_op jit(solution)/shard_map/ppermute | solution.py:373
  27.7 0.8 %multiply.4.part_ref = f32[96,1024]{1,0:T(8,128)S(1)} custom-call(bf16[96,2048]{1,0:T(8,128)(2,1)S(1)} %get-tuple-element.23.table_ref.refs_1_, bf16[2048,1024]{1,0:T(8,128)(2,1)S(1)} %get-tuple-element.27.weight_ref), custom_call_target="tpu_custom_call" | custom-call | bytes 1048576 | tf_op jit(solution)/shard_map/multiply/pallas_call | solution.py:269
  28.5 0.0 collective-permute-done.4.arrived_ref
  28.5 0.1 add.4
  28.6 2.1 %collective-permute-start.5 = (bf16[96,1024]{1,0:T(8,128)(2,1)S(1)}, bf16[96,1024]{1,0:T(8,128)(2,1)S(1)}, u32[]{:S(2)}, u32[]{:S(2)}) collective-permute-start(bf16[96,1024]{1,0:T(8,128)(2,1)S(1)} %add.4), channel_id=1, source_target_pairs={{0,8},{8,12},{12,4},{4,0},{1,9},{9,13},{13,5},{5,1},{2,10},{10,14}... | collective-permute-start | bytes 589832 | tf_op jit(solution)/shard_map/ppermute | solution.py:373
  30.7 1.5 %collective-permute-done.2.arrived_ref = bf16[96,1152]{1,0:T(8,128)(2,1)S(1)} collective-permute-done((bf16[96,1152]{1,0:T(8,128)(2,1)S(1)}, bf16[96,1152]{1,0:T(8,128)(2,1)S(1)}, u32[]{:S(2)}, u32[]{:S(2)}) %collective-permute-start.2) | collective-permute-done | bytes 221216 | tf_op jit(solution)/shard_map/ppermute | solution.py:373
  32.2 1.3 %step_a.5 = (bf16[96,2048]{1,0:T(8,128)(2,1)S(1)}, bf16[96,1024]{1,0:T(8,128)(2,1)S(1)}) custom-call(s32[1]{0:T(128)} %bitcast.first_ref, bf16[96,1152]{1,0:T(8,128)(2,1)S(1)} %collective-permute-done.2.arrived_ref, bf16[2048,1024]{1,0:T(8,128)(2,1)S(1)} %get-tuple-element.20.weight_ref, f32[1,2048]{1,0:T(1,128)S(1)} %bitcast.8), custom_call_target="tpu_custom_call" | custom-call | bytes 1048576 | tf_op jit(solution)/shard_map/step_a/pallas_call | solution.py:238
  33.5 3.4 %collective-permute-start.9 = (bf16[96,1024]{1,0:T(8,128)(2,1)S(1)}, bf16[96,1024]{1,0:T(8,128)(2,1)S(1)}, u32[]{:S(2)}, u32[]{:S(2)}) collective-permute-start(bf16[96,1024]{1,0:T(8,128)(2,1)S(1)} %get-tuple-element.31.refs_2_), channel_id=1, source_target_pairs={{0,8},{8,12},{12,4},{4,0},{1,9},{9,13},{13,5},{5,1},{2,10},{10,14}... | collective-permute-start | bytes 589832 | tf_op jit(solution)/shard_map/ppermute | solution.py:373
  36.9 0.8 %multiply.3.part_ref = f32[96,1024]{1,0:T(8,128)S(1)} custom-call(bf16[96,2048]{1,0:T(8,128)(2,1)S(1)} %get-tuple-element.25.table_ref.refs_0_, bf16[2048,1024]{1,0:T(8,128)(2,1)S(1)} %get-tuple-element.27.weight_ref), custom_call_target="tpu_custom_call" | custom-call | bytes 1048576 | tf_op jit(solution)/shard_map/multiply/pallas_call | solution.py:269
  37.7 0.0 collective-permute-done.5.arrived_ref
  37.7 0.1 add.5.refs_2_
  37.8 1.7 %collective-permute-start.6 = (bf16[96,1024]{1,0:T(8,128)(2,1)S(1)}, bf16[96,1024]{1,0:T(8,128)(2,1)S(1)}, u32[]{:S(2)}, u32[]{:S(2)}) collective-permute-start(bf16[96,1024]{1,0:T(8,128)(2,1)S(1)} %add.5.refs_2_), channel_id=1, source_target_pairs={{0,8},{8,12},{12,4},{4,0},{1,9},{9,13},{13,5},{5,1},{2,10},{10,14}... | collective-permute-start | bytes 589832 | tf_op jit(solution)/shard_map/ppermute | solution.py:373
  39.5 2.2 %collective-permute-done.9.refs_3_.refs_4_ = bf16[96,1024]{1,0:T(8,128)(2,1)S(1)} collective-permute-done((bf16[96,1024]{1,0:T(8,128)(2,1)S(1)}, bf16[96,1024]{1,0:T(8,128)(2,1)S(1)}, u32[]{:S(2)}, u32[]{:S(2)}) %collective-permute-start.9) | collective-permute-done | bytes 196640 | tf_op jit(solution)/shard_map/ppermute | solution.py:373
  41.7 3.1 %collective-permute-start.10 = (bf16[96,1024]{1,0:T(8,128)(2,1)S(1)}, bf16[96,1024]{1,0:T(8,128)(2,1)S(1)}, u32[]{:S(2)}, u32[]{:S(2)}) collective-permute-start(bf16[96,1024]{1,0:T(8,128)(2,1)S(1)} %collective-permute-done.9.refs_3_.refs_4_), channel_id=1, source_target_pairs={{0,8},{8,12},{12,4},{4,0},{1,9},{9,13},{13,5},{5,1},{2,10},{10,14}... | collective-permute-start | bytes 589832 | tf_op jit(solution)/shard_map/ppermute | solution.py:373
  44.8 1.1 %collective-permute-done.6.refs_3_.refs_4_ = bf16[96,1024]{1,0:T(8,128)(2,1)S(1)} collective-permute-done((bf16[96,1024]{1,0:T(8,128)(2,1)S(1)}, bf16[96,1024]{1,0:T(8,128)(2,1)S(1)}, u32[]{:S(2)}, u32[]{:S(2)}) %collective-permute-start.6) | collective-permute-done | bytes 196640 | tf_op jit(solution)/shard_map/ppermute | solution.py:373
  45.9 3.1 %collective-permute-start.7 = (bf16[96,1024]{1,0:T(8,128)(2,1)S(1)}, bf16[96,1024]{1,0:T(8,128)(2,1)S(1)}, u32[]{:S(2)}, u32[]{:S(2)}) collective-permute-start(bf16[96,1024]{1,0:T(8,128)(2,1)S(1)} %collective-permute-done.6.refs_3_.refs_4_), channel_id=1, source_target_pairs={{0,8},{8,12},{12,4},{4,0},{1,9},{9,13},{13,5},{5,1},{2,10},{10,14}... | collective-permute-start | bytes 589832 | tf_op jit(solution)/shard_map/ppermute | solution.py:373
  49.0 1.3 %early_grad.3.refs_5_ = f32[2048,1024]{1,0:T(8,128)S(1)} custom-call(bf16[96,2048]{1,0:T(8,128)(2,1)S(1)} %get-tuple-element.25.table_ref.refs_0_, bf16[96,2048]{1,0:T(8,128)(2,1)S(1)} %get-tuple-element.26.table_ref.refs_1_, bf16[96,1024]{1,0:T(8,128)(2,1)S(1)} %get-tuple-element.31.refs_2_, bf16[96,1024]{1,0:T(8,128)(2,1)S(1)} %collective-permute-done.9.refs_3_.refs_4_), custom_call_target="tpu_custom_call" | custom-call | bytes 1048576 | tf_op jit(solution)/shard_map/early_grad/pallas_call | solution.py:306
  50.3 1.3 %early_grad.2.refs_5_ = f32[2048,1024]{1,0:T(8,128)S(1)} custom-call(bf16[96,2048]{1,0:T(8,128)(2,1)S(1)} %get-tuple-element.25.table_ref.refs_0_, bf16[96,2048]{1,0:T(8,128)(2,1)S(1)} %get-tuple-element.26.table_ref.refs_1_, bf16[96,1024]{1,0:T(8,128)(2,1)S(1)} %add.5.refs_2_, bf16[96,1024]{1,0:T(8,128)(2,1)S(1)} %collective-permute-done.6.refs_3_.refs_4_), custom_call_target="tpu_custom_call" | custom-call | bytes 1048576 | tf_op jit(solution)/shard_map/early_grad/pallas_call | solution.py:306
  51.6 0.0 collective-permute-done.10.refs_2_
  51.6 1.9 %collective-permute-start.11 = (bf16[96,1024]{1,0:T(8,128)(2,1)S(1)}, bf16[96,1024]{1,0:T(8,128)(2,1)S(1)}, u32[]{:S(2)}, u32[]{:S(2)}) collective-permute-start(bf16[96,1024]{1,0:T(8,128)(2,1)S(1)} %collective-permute-done.10.refs_2_), channel_id=1, source_target_pairs={{0,8},{8,12},{12,4},{4,0},{1,9},{9,13},{13,5},{5,1},{2,10},{10,14}... | collective-permute-start | bytes 589832 | tf_op jit(solution)/shard_map/ppermute | solution.py:373
  53.5 0.8 %collective-permute-done.7.refs_2_ = bf16[96,1024]{1,0:T(8,128)(2,1)S(1)} collective-permute-done((bf16[96,1024]{1,0:T(8,128)(2,1)S(1)}, bf16[96,1024]{1,0:T(8,128)(2,1)S(1)}, u32[]{:S(2)}, u32[]{:S(2)}) %collective-permute-start.7) | collective-permute-done | bytes 196640 | tf_op jit(solution)/shard_map/ppermute | solution.py:373
  54.3 3.4 %collective-permute-start.8 = (bf16[96,1024]{1,0:T(8,128)(2,1)S(1)}, bf16[96,1024]{1,0:T(8,128)(2,1)S(1)}, u32[]{:S(2)}, u32[]{:S(2)}) collective-permute-start(bf16[96,1024]{1,0:T(8,128)(2,1)S(1)} %collective-permute-done.7.refs_2_), channel_id=1, source_target_pairs={{0,8},{8,12},{12,4},{4,0},{1,9},{9,13},{13,5},{5,1},{2,10},{10,14}... | collective-permute-start | bytes 589832 | tf_op jit(solution)/shard_map/ppermute | solution.py:373
  57.7 0.0 collective-permute-done.11.refs_3_
  57.7 2.4 %grad.2 = (bf16[96,2048]{1,0:T(8,128)(2,1)}, bf16[2048,2048]{1,0:T(8,128)(2,1)}) custom-call(bf16[96,2048]{1,0:T(8,128)(2,1)S(1)} %get-tuple-element.21.table_ref.refs_0_, bf16[96,2048]{1,0:T(8,128)(2,1)S(1)} %get-tuple-element.23.table_ref.refs_1_, bf16[96,1024]{1,0:T(8,128)(2,1)S(1)} %collective-permute-done.10.refs_2_, ...), custom_call_target="tpu_custom_call" | custom-call | bytes 1048576 | tf_op jit(solution)/shard_map/grad/pallas_call | solution.py:347
  60.1 0.8 %collective-permute-done.8.refs_3_ = bf16[96,1024]{1,0:T(8,128)(2,1)S(1)} collective-permute-done((bf16[96,1024]{1,0:T(8,128)(2,1)S(1)}, bf16[96,1024]{1,0:T(8,128)(2,1)S(1)}, u32[]{:S(2)}, u32[]{:S(2)}) %collective-permute-start.8) | collective-permute-done | bytes 196640 | tf_op jit(solution)/shard_map/ppermute | solution.py:373
  60.9 2.4 %grad.3 = (bf16[96,2048]{1,0:T(8,128)(2,1)}, bf16[2048,2048]{1,0:T(8,128)(2,1)}) custom-call(bf16[96,2048]{1,0:T(8,128)(2,1)S(1)} %get-tuple-element.21.table_ref.refs_0_, bf16[96,2048]{1,0:T(8,128)(2,1)S(1)} %get-tuple-element.23.table_ref.refs_1_, ...), custom_call_target="tpu_custom_call", output_to_operand_aliasing={{0}: (6, {}), {1}: (7, {})} | custom-call | bytes 1048576 | tf_op jit(solution)/shard_map/grad/pallas_call | solution.py:347
Async XLA Ops:
  0.6 12.2 %copy-start = (f32[2048]{0:T(1024)S(1)}, f32[2048]{0:T(1024)}, u32[]{:S(2)}) copy-start(f32[2048]{0:T(1024)} %param.8) | copy-start | bytes 24580
  3.3 9.5 %collective-permute-start = (bf16[96,1152]{1,0:T(8,128)(2,1)S(1)}, bf16[96,1152]{1,0:T(8,128)(2,1)S(1)}, u32[]{:S(2)}, u32[]{:S(2)}) collective-permute-start(bf16[96,1152]{1,0:T(8,128)(2,1)S(1)} %get-tuple-element.19), channel_id=1, source_target_pairs={{0,8},{8,12},{12,4},{4,0},{1,9},{9,13},{13,5},{5,1},{2,10},{10,14}... | collective-permute-start | bytes 663560 | tf_op jit(solution)/shard_map/ppermute | solution.py:373
  10.0 8.5 %collective-permute-start.3 = (bf16[96,1024]{1,0:T(8,128)(2,1)S(1)}, bf16[96,1024]{1,0:T(8,128)(2,1)S(1)}, u32[]{:S(2)}, u32[]{:S(2)}) collective-permute-start(bf16[96,1024]{1,0:T(8,128)(2,1)S(1)} %get-tuple-element.28), channel_id=1, source_target_pairs={{0,8},{8,12},{12,4},{4,0},{1,9},{9,13},{13,5},{5,1},{2,10},{10,14}... | collective-permute-start | bytes 589832 | tf_op jit(solution)/shard_map/ppermute | solution.py:373
  14.2 9.0 %collective-permute-start.1 = (bf16[96,1152]{1,0:T(8,128)(2,1)S(1)}, bf16[96,1152]{1,0:T(8,128)(2,1)S(1)}, u32[]{:S(2)}, u32[]{:S(2)}) collective-permute-start(bf16[96,1152]{1,0:T(8,128)(2,1)S(1)} %get-tuple-element.22), channel_id=1, source_target_pairs={{0,8},{8,12},{12,4},{4,0},{1,9},{9,13},{13,5},{5,1},{2,10},{10,14}... | collective-permute-start | bytes 663560 | tf_op jit(solution)/shard_map/ppermute | solution.py:373
  18.5 10.1 %collective-permute-start.4 = (bf16[96,1024]{1,0:T(8,128)(2,1)S(1)}, bf16[96,1024]{1,0:T(8,128)(2,1)S(1)}, u32[]{:S(2)}, u32[]{:S(2)}) collective-permute-start(bf16[96,1024]{1,0:T(8,128)(2,1)S(1)} %add.3), channel_id=1, source_target_pairs={{0,8},{8,12},{12,4},{4,0},{1,9},{9,13},{13,5},{5,1},{2,10},{10,14}... | collective-permute-start | bytes 589832 | tf_op jit(solution)/shard_map/ppermute | solution.py:373
  24.5 7.7 %collective-permute-start.2 = (bf16[96,1152]{1,0:T(8,128)(2,1)S(1)}, bf16[96,1152]{1,0:T(8,128)(2,1)S(1)}, u32[]{:S(2)}, u32[]{:S(2)}) collective-permute-start(bf16[96,1152]{1,0:T(8,128)(2,1)S(1)} %get-tuple-element.24), channel_id=1, source_target_pairs={{0,8},{8,12},{12,4},{4,0},{1,9},{9,13},{13,5},{5,1},{2,10},{10,14}... | collective-permute-start | bytes 663560 | tf_op jit(solution)/shard_map/ppermute | solution.py:373
  28.6 9.1 %collective-permute-start.5 = (bf16[96,1024]{1,0:T(8,128)(2,1)S(1)}, bf16[96,1024]{1,0:T(8,128)(2,1)S(1)}, u32[]{:S(2)}, u32[]{:S(2)}) collective-permute-start(bf16[96,1024]{1,0:T(8,128)(2,1)S(1)} %add.4), channel_id=1, source_target_pairs={{0,8},{8,12},{12,4},{4,0},{1,9},{9,13},{13,5},{5,1},{2,10},{10,14}... | collective-permute-start | bytes 589832 | tf_op jit(solution)/shard_map/ppermute | solution.py:373
  33.5 8.2 %collective-permute-start.9 = (bf16[96,1024]{1,0:T(8,128)(2,1)S(1)}, bf16[96,1024]{1,0:T(8,128)(2,1)S(1)}, u32[]{:S(2)}, u32[]{:S(2)}) collective-permute-start(bf16[96,1024]{1,0:T(8,128)(2,1)S(1)} %get-tuple-element.31.refs_2_), channel_id=1, source_target_pairs={{0,8},{8,12},{12,4},{4,0},{1,9},{9,13},{13,5},{5,1},{2,10},{10,14}... | collective-permute-start | bytes 589832 | tf_op jit(solution)/shard_map/ppermute | solution.py:373
  37.8 8.1 %collective-permute-start.6 = (bf16[96,1024]{1,0:T(8,128)(2,1)S(1)}, bf16[96,1024]{1,0:T(8,128)(2,1)S(1)}, u32[]{:S(2)}, u32[]{:S(2)}) collective-permute-start(bf16[96,1024]{1,0:T(8,128)(2,1)S(1)} %add.5.refs_2_), channel_id=1, source_target_pairs={{0,8},{8,12},{12,4},{4,0},{1,9},{9,13},{13,5},{5,1},{2,10},{10,14}... | collective-permute-start | bytes 589832 | tf_op jit(solution)/shard_map/ppermute | solution.py:373
  41.7 9.9 %collective-permute-start.10 = (bf16[96,1024]{1,0:T(8,128)(2,1)S(1)}, bf16[96,1024]{1,0:T(8,128)(2,1)S(1)}, u32[]{:S(2)}, u32[]{:S(2)}) collective-permute-start(bf16[96,1024]{1,0:T(8,128)(2,1)S(1)} %collective-permute-done.9.refs_3_.refs_4_), channel_id=1, source_target_pairs={{0,8},{8,12},{12,4},{4,0},{1,9},{9,13},{13,5},{5,1},{2,10},{10,14}... | collective-permute-start | bytes 589832 | tf_op jit(solution)/shard_map/ppermute | solution.py:373
  45.9 8.4 %collective-permute-start.7 = (bf16[96,1024]{1,0:T(8,128)(2,1)S(1)}, bf16[96,1024]{1,0:T(8,128)(2,1)S(1)}, u32[]{:S(2)}, u32[]{:S(2)}) collective-permute-start(bf16[96,1024]{1,0:T(8,128)(2,1)S(1)} %collective-permute-done.6.refs_3_.refs_4_), channel_id=1, source_target_pairs={{0,8},{8,12},{12,4},{4,0},{1,9},{9,13},{13,5},{5,1},{2,10},{10,14}... | collective-permute-start | bytes 589832 | tf_op jit(solution)/shard_map/ppermute | solution.py:373
  51.6 6.1 %collective-permute-start.11 = (bf16[96,1024]{1,0:T(8,128)(2,1)S(1)}, bf16[96,1024]{1,0:T(8,128)(2,1)S(1)}, u32[]{:S(2)}, u32[]{:S(2)}) collective-permute-start(bf16[96,1024]{1,0:T(8,128)(2,1)S(1)} %collective-permute-done.10.refs_2_), channel_id=1, source_target_pairs={{0,8},{8,12},{12,4},{4,0},{1,9},{9,13},{13,5},{5,1},{2,10},{10,14}... | collective-permute-start | bytes 589832 | tf_op jit(solution)/shard_map/ppermute | solution.py:373
  54.3 6.6 %collective-permute-start.8 = (bf16[96,1024]{1,0:T(8,128)(2,1)S(1)}, bf16[96,1024]{1,0:T(8,128)(2,1)S(1)}, u32[]{:S(2)}, u32[]{:S(2)}) collective-permute-start(bf16[96,1024]{1,0:T(8,128)(2,1)S(1)} %collective-permute-done.7.refs_2_), channel_id=1, source_target_pairs={{0,8},{8,12},{12,4},{4,0},{1,9},{9,13},{13,5},{5,1},{2,10},{10,14}... | collective-permute-start | bytes 589832 | tf_op jit(solution)/shard_map/ppermute | solution.py:373
